TPU v7x, 32 devices: a whole 2x2x4 slice. The times are simulated.
32 devices in a mesh: seq: 8 (over z, x), head: 4 (over y, core).
Axes of the slice: x: 2, y: 2, z: 4, core: 2. Of those that a mesh axis runs over, the one named last changes fastest.
Arguments:
- tokens_in: bfloat16 [4, 2048, 768], P(None, 'seq', 'head'), may hold values from -6 to 6
- out_grad: bfloat16 [4, 2048, 768], P(None, 'seq', 'head'), may hold values from -6 to 6
- lengths: int32 [4, 4], replicated, may hold values from 1 to 1920, as said below
- norm_gain: bfloat16 [768], P('head'), may hold values from 0.5 to 1.5
- proj_z: bfloat16 [768, 1536], P(None, 'head'), may hold values from -0.21875 to 0.21875
- proj_x: bfloat16 [768, 1536], P(None, 'head'), may hold values from -0.21875 to 0.21875
- proj_bc: bfloat16 [768, 256], P(None, 'head'), may hold values from -0.21875 to 0.21875
- proj_dt: bfloat16 [768, 24], P(None, 'head'), may hold values from -0.21875 to 0.21875
- conv_x: bfloat16 [4, 1536], P(None, 'head'), may hold values from -3 to 3
- conv_bc: bfloat16 [4, 256], P(None, 'head'), may hold values from -3 to 3
- bias_x: bfloat16 [1536], P('head'), may hold values from -3 to 3
- bias_bc: bfloat16 [256], P('head'), may hold values from -3 to 3
- dt_bias: bfloat16 [24], P('head'), may hold values from -5 to -3
- a_log: bfloat16 [24], P('head'), may hold values from -12 to 1
- d_skip: bfloat16 [24], P('head'), may hold values from 0.5 to 1.5
- gate_gain: bfloat16 [1536], P('head'), may hold values from 0.5 to 1.5
- proj_out: bfloat16 [1536, 768], P('head'), may hold values from -0.15625 to 0.15625
Outputs:
- block_out: bfloat16 [4, 2048, 768], P(None, 'seq', 'head')
- in_grad: float32 [4, 2048, 768], P(None, 'seq', 'head')
- grad_norm_gain: float32 [768], P('head')
- grad_proj_z: float32 [768, 1536], P(None, 'head')
- grad_proj_x: float32 [768, 1536], P(None, 'head')
- grad_proj_bc: float32 [768, 256], P(None, 'head')
- grad_proj_dt: float32 [768, 24], P(None, 'head')
- grad_conv_x: float32 [4, 1536], P(None, 'head')
- grad_conv_bc: float32 [4, 256], P(None, 'head')
- grad_bias_x: float32 [1536], P('head')
- grad_bias_bc: float32 [256], P('head')
- grad_dt_bias: float32 [24], P('head')
- grad_a_log: float32 [24], P('head')
- grad_d_skip: float32 [24], P('head')
- grad_gate_gain: float32 [1536], P('head')
- grad_proj_out: float32 [1536, 768], P('head')
Inputs may be any that keep to these rules, and one draw needn't show every extreme that they name: Each row holds 4 lengths that sum to 2048; exactly one of them is 2048 minus half of 256, the others share the rest.
All inputs are finite; a program needn't handle non-finite values.
Results may differ from a plain program's by a relative error of at most 0.012.
The roundings to bfloat16 on the way count: a program that leaves them out, or rounds other values in their place, can miss the bound.
Values may be sent and summed in bfloat16 or wider, within the bound.
No kernel may reach another device: no remote copies, remote signals or barrier semaphores. Data moves between devices by JAX's collectives and lax.ppermute only.
A program may use at most 192 MiB of HBM per device.

v0:
```python
import jax
import jax.numpy as jnp
from jax import lax
from jax.sharding import PartitionSpec as P

EPSILON = 1e-05
PRECISE = lax.Precision.HIGHEST


def from_behind(block, axis, distance):
    devices = range(lax.axis_size(axis))
    route = [(i - distance, i) for i in devices if i - distance in devices]
    return lax.ppermute(block, axis, route)


def entering(x, axis, combine, identity, reverse):
    devices, position = (lax.axis_size(axis), lax.axis_index(axis))
    everything = jax.tree.map(lambda part: lax.all_gather(part, axis), x)
    start = jax.tree.map(
        lambda part, zero: jnp.broadcast_to(jnp.asarray(zero, part.dtype), part.shape), x, identity
    )

    def lap(k, before):
        at = devices - 1 - k if reverse else k
        reached = at > position if reverse else at < position
        new = combine(before, jax.tree.map(lambda part: part[at], everything))
        return jax.tree.map(lambda a, b: jnp.where(reached, a, b), new, before)

    return lax.fori_loop(0, devices, lap, start)


def combine_states(earlier, later):
    return (earlier[0] * later[0], later[0][:, :, None, None] * earlier[1] + later[1])


def below_diag(count):
    row_ids = lax.broadcasted_iota(jnp.int32, (count, count), 0)
    col_ids = lax.broadcasted_iota(jnp.int32, (count, count), 1)
    return row_ids >= col_ids


def decay_sums(dt_raw, dt_bias, a_log):
    dt_vals = jax.nn.softplus(dt_raw + dt_bias)
    rate_vals = dt_vals * -jnp.exp(a_log)
    count = dt_raw.shape[1]
    cum_decay = jnp.einsum(
        "ts,ksh->kth", below_diag(count).astype(jnp.float32), rate_vals, precision=PRECISE
    )
    return (dt_vals, cum_decay)


def ssd_block_output(
    x_heads, bc_full, dt_raw, dt_bias, a_log, d_skip, state_in, segment, carry_flag
):
    state_size = bc_full.shape[2] // 2
    b_vals = bc_full[..., :state_size]
    c_vals = bc_full[..., state_size:]
    dt_vals, cum_decay = decay_sums(dt_raw, dt_bias, a_log)
    count = x_heads.shape[1]
    same_seq = ((segment[:, :, None] == segment[:, None, :]) & below_diag(count)[None])[..., None]
    decay_mat = jnp.where(
        same_seq,
        jnp.exp(jnp.where(same_seq, cum_decay[:, :, None, :] - cum_decay[:, None, :, :], 0.0)),
        0.0,
    )
    scores = jnp.einsum("ktn,ksn->kts", c_vals, b_vals, precision=PRECISE)
    scaled = x_heads * dt_vals[..., None]
    inner = jnp.einsum("ktsh,kshp->kthp", scores[..., None] * decay_mat, scaled, precision=PRECISE)
    carried = jnp.einsum("khpn,ktn->kthp", state_in, c_vals, precision=PRECISE)
    return (
        inner
        + (carry_flag[:, :, None] * jnp.exp(cum_decay))[..., None] * carried
        + x_heads * d_skip[None, None, :, None]
    )


def ssd_block_state(x_heads, bc_full, dt_raw, dt_bias, a_log, segment, carry_flag):
    state_size = bc_full.shape[2] // 2
    b_vals = bc_full[..., :state_size]
    dt_vals, cum_decay = decay_sums(dt_raw, dt_bias, a_log)
    keep_end = (segment == segment[:, -1:])[..., None]
    end_weight = jnp.where(
        keep_end, jnp.exp(jnp.where(keep_end, cum_decay[:, -1:, :] - cum_decay, 0.0)), 0.0
    )
    local_state = jnp.einsum(
        "ksh,kshp,ksn->khpn", end_weight, x_heads * dt_vals[..., None], b_vals, precision=PRECISE
    )
    carry_decay = carry_flag[:, -1:] * jnp.exp(cum_decay[:, -1, :])
    return (carry_decay, local_state)


def local_conv(extended, kernel, offset, masks):
    width = kernel.shape[0]
    count = extended.shape[1] - width + 1
    summed = jnp.broadcast_to(offset[None, None, :], (extended.shape[0], count, offset.shape[0]))
    for lag_index in range(width):
        summed = (
            summed
            + kernel[lag_index][None, None, :]
            * extended[:, lag_index : lag_index + count, :]
            * masks[lag_index][:, :, None]
        )
    return jax.nn.silu(summed)


def shards(
    tokens_in,
    out_grad,
    lengths,
    norm_gain,
    proj_z,
    proj_x,
    proj_bc,
    proj_dt,
    conv_x,
    conv_bc,
    bias_x,
    bias_bc,
    dt_bias,
    a_log,
    d_skip,
    gate_gain,
    proj_out,
):
    packs, count, width_local = tokens_in.shape
    inner_local = proj_x.shape[1]
    bc_local = proj_bc.shape[1]
    heads_local = proj_dt.shape[1]
    head_size = inner_local // heads_local
    width = conv_x.shape[0]
    total_inner = inner_local * lax.axis_size("head")
    seq_place = lax.axis_index("seq")
    head_place = lax.axis_index("head")
    tokens_full, gain_full, cot_full = (
        lax.all_gather(tokens_in, "head", axis=2, tiled=True),
        lax.all_gather(norm_gain, "head", axis=0, tiled=True),
        lax.all_gather(out_grad, "head", axis=2, tiled=True),
    )
    tokens_f = tokens_full.astype(jnp.float32)
    inv_rms = lax.rsqrt(jnp.mean(tokens_f * tokens_f, axis=-1, keepdims=True) + EPSILON)
    unit_tokens = tokens_f * inv_rms
    gain_f = gain_full.astype(jnp.float32)
    normed = (unit_tokens * gain_f).astype(jnp.bfloat16)
    proj_all = jnp.concatenate([proj_z, proj_x, proj_bc, proj_dt], axis=1)
    projected = jnp.einsum(
        "ktd,de->kte", normed, proj_all, preferred_element_type=jnp.float32
    ).astype(jnp.bfloat16)
    gate_raw = projected[..., :inner_local]
    conv_raw = projected[..., inner_local : 2 * inner_local + bc_local]
    dt_raw = projected[..., 2 * inner_local + bc_local :].astype(jnp.float32)
    seq_ends = jnp.cumsum(lengths, axis=-1)
    positions = (
        seq_place * count - (width - 1) + lax.broadcasted_iota(jnp.int32, (count + width - 1,), 0)
    )
    seg_ext = jnp.sum((positions[None, :, None] >= seq_ends[:, None, :]).astype(jnp.int32), axis=2)
    segment = seg_ext[:, width - 1 :]
    carry_flag = ((segment == seg_ext[:, width - 2 : width - 1]) & (seq_place > 0)).astype(
        jnp.float32
    )
    masks = jnp.stack(
        [
            (seg_ext[:, lag_index : lag_index + count] == segment).astype(jnp.float32)
            for lag_index in range(width)
        ]
    )
    prev_edge = from_behind(conv_raw[:, count - (width - 1) :, :], "seq", 1)
    extended = jnp.concatenate([prev_edge, conv_raw], axis=1).astype(jnp.float32)
    kernel = jnp.concatenate([conv_x, conv_bc], axis=1).astype(jnp.float32)
    offset = jnp.concatenate([bias_x, bias_bc]).astype(jnp.float32)
    conv_out, conv_pull = jax.vjp(
        lambda ext_in, kern_in, off_in: local_conv(ext_in, kern_in, off_in, masks),
        extended,
        kernel,
        offset,
    )
    conv_low = conv_out.astype(jnp.bfloat16)
    bc_full = lax.all_gather(conv_low[..., inner_local:], "head", axis=2, tiled=True).astype(
        jnp.float32
    )
    x_heads = (
        conv_low[..., :inner_local]
        .astype(jnp.float32)
        .reshape(packs, count, heads_local, head_size)
    )
    dt_bias_f = dt_bias.astype(jnp.float32)
    a_log_f = a_log.astype(jnp.float32)
    d_skip_f = d_skip.astype(jnp.float32)
    (carry_decay, local_state), state_pull = jax.vjp(
        lambda x_in, bc_in, raw_in, bias_in, alog_in: ssd_block_state(
            x_in, bc_in, raw_in, bias_in, alog_in, segment, carry_flag
        ),
        x_heads,
        bc_full,
        dt_raw,
        dt_bias_f,
        a_log_f,
    )
    identity = (jnp.ones_like(carry_decay), jnp.zeros_like(local_state))
    state_in = entering((carry_decay, local_state), "seq", combine_states, identity, False)[1]
    ssd_out, output_pull = jax.vjp(
        lambda x_in, bc_in, raw_in, bias_in, alog_in, skip_in, state_arg: ssd_block_output(
            x_in, bc_in, raw_in, bias_in, alog_in, skip_in, state_arg, segment, carry_flag
        ),
        x_heads,
        bc_full,
        dt_raw,
        dt_bias_f,
        a_log_f,
        d_skip_f,
        state_in,
    )
    ssd_flat = ssd_out.reshape(packs, count, inner_local)
    gate_f = gate_raw.astype(jnp.float32)
    gate_sig = jax.nn.sigmoid(gate_f)
    gate_act = gate_f * gate_sig
    mixed = ssd_flat * gate_act
    square_total = lax.psum(jnp.sum(mixed * mixed, axis=-1), "head")
    inv_gate = lax.rsqrt(square_total / total_inner + EPSILON)[..., None]
    gain_gate = gate_gain.astype(jnp.float32)
    gated = (mixed * inv_gate * gain_gate).astype(jnp.bfloat16)
    partial_out = jnp.einsum("kte,ed->ktd", gated, proj_out, preferred_element_type=jnp.float32)
    block_out = (
        lax.psum_scatter(partial_out, "head", scatter_dimension=2, tiled=True)
        + tokens_in.astype(jnp.float32)
    ).astype(jnp.bfloat16)
    grad_gated = jnp.einsum("ktd,ed->kte", cot_full, proj_out, preferred_element_type=jnp.float32)
    grad_gate_gain = jnp.sum(grad_gated * mixed * inv_gate, axis=(0, 1))
    grad_proj_out = jnp.einsum("kte,ktd->ed", gated, cot_full, preferred_element_type=jnp.float32)
    gain_dot = lax.psum(jnp.sum(gain_gate * grad_gated * mixed, axis=-1), "head")
    grad_mixed = inv_gate * gain_gate * grad_gated - mixed * inv_gate**3 * (
        gain_dot[..., None] / total_inner
    )
    grad_ssd = (grad_mixed * gate_act).reshape(packs, count, heads_local, head_size)
    grad_gate = grad_mixed * ssd_flat * gate_sig * (1.0 + gate_f * (1.0 - gate_sig))
    (
        grad_x_out,
        grad_bc_out,
        grad_dt_out,
        grad_bias_out,
        grad_alog_out,
        grad_d_skip,
        grad_state_in,
    ) = output_pull(grad_ssd)
    state_grad = entering((carry_decay, grad_state_in), "seq", combine_states, identity, True)[1]
    grad_carry = jnp.sum(state_grad * state_in, axis=(2, 3))
    grad_x_st, grad_bc_st, grad_dt_st, grad_bias_st, grad_alog_st = state_pull(
        (grad_carry, state_grad)
    )
    bc_grad_local = lax.psum_scatter(
        grad_bc_out + grad_bc_st, "head", scatter_dimension=2, tiled=True
    )
    grad_conv_out = jnp.concatenate(
        [(grad_x_out + grad_x_st).reshape(packs, count, inner_local), bc_grad_local], axis=2
    )
    grad_ext, grad_kernel, grad_offset = conv_pull(grad_conv_out)
    edge_back = from_behind(grad_ext[:, : width - 1, :], "seq", -1)
    grad_conv_raw = grad_ext[:, width - 1 :, :]
    grad_conv_raw = jnp.concatenate(
        [
            grad_conv_raw[:, : count - (width - 1), :],
            grad_conv_raw[:, count - (width - 1) :, :] + edge_back,
        ],
        axis=1,
    )
    grad_proj = jnp.concatenate(
        [grad_gate, grad_conv_raw, grad_dt_out + grad_dt_st], axis=2
    ).astype(jnp.bfloat16)
    grad_proj_all = jnp.einsum("ktd,kte->de", normed, grad_proj, preferred_element_type=jnp.float32)
    normed_terms = jnp.einsum(
        "kte,de->ktd", grad_proj, proj_all, preferred_element_type=jnp.float32
    )
    start_col = head_place * width_local
    grad_normed = lax.psum(normed_terms, "head")
    gain_grad_x = gain_f * grad_normed
    grad_tokens = inv_rms * (
        gain_grad_x - unit_tokens * jnp.mean(gain_grad_x * unit_tokens, axis=-1, keepdims=True)
    )
    in_grad = lax.dynamic_slice_in_dim(grad_tokens, start_col, width_local, 2) + out_grad.astype(
        jnp.float32
    )
    grad_norm_gain = jnp.sum(
        lax.dynamic_slice_in_dim(grad_normed * unit_tokens, start_col, width_local, 2), axis=(0, 1)
    )
    grad_proj_z = grad_proj_all[:, :inner_local]
    grad_proj_x = grad_proj_all[:, inner_local : 2 * inner_local]
    grad_proj_bc = grad_proj_all[:, 2 * inner_local : 2 * inner_local + bc_local]
    grad_proj_dt = grad_proj_all[:, 2 * inner_local + bc_local :]
    grad_conv_x = grad_kernel[:, :inner_local]
    grad_conv_bc = grad_kernel[:, inner_local:]
    grad_bias_x = grad_offset[:inner_local]
    grad_bias_bc = grad_offset[inner_local:]
    grad_dt_bias = grad_bias_out + grad_bias_st
    grad_a_log = grad_alog_out + grad_alog_st
    (
        grad_norm_gain,
        grad_proj_z,
        grad_proj_x,
        grad_proj_bc,
        grad_proj_dt,
        grad_conv_x,
        grad_conv_bc,
        grad_bias_x,
        grad_bias_bc,
        grad_dt_bias,
        grad_a_log,
        grad_d_skip,
        grad_gate_gain,
        grad_proj_out,
    ) = lax.psum(
        (
            grad_norm_gain,
            grad_proj_z,
            grad_proj_x,
            grad_proj_bc,
            grad_proj_dt,
            grad_conv_x,
            grad_conv_bc,
            grad_bias_x,
            grad_bias_bc,
            grad_dt_bias,
            grad_a_log,
            grad_d_skip,
            grad_gate_gain,
            grad_proj_out,
        ),
        "seq",
    )
    return (
        block_out,
        in_grad,
        grad_norm_gain,
        grad_proj_z,
        grad_proj_x,
        grad_proj_bc,
        grad_proj_dt,
        grad_conv_x,
        grad_conv_bc,
        grad_bias_x,
        grad_bias_bc,
        grad_dt_bias,
        grad_a_log,
        grad_d_skip,
        grad_gate_gain,
        grad_proj_out,
    )


def solution(mesh):
    return jax.shard_map(
        shards,
        mesh=mesh,
        in_specs=(
            P(None, "seq", "head"),
            P(None, "seq", "head"),
            P(),
            P("head"),
            P(None, "head"),
            P(None, "head"),
            P(None, "head"),
            P(None, "head"),
            P(None, "head"),
            P(None, "head"),
            P("head"),
            P("head"),
            P("head"),
            P("head"),
            P("head"),
            P("head"),
            P("head", None),
        ),
        out_specs=(
            P(None, "seq", "head"),
            P(None, "seq", "head"),
            P("head"),
            P(None, "head"),
            P(None, "head"),
            P(None, "head"),
            P(None, "head"),
            P(None, "head"),
            P(None, "head"),
            P("head"),
            P("head"),
            P("head"),
            P("head"),
            P("head"),
            P("head"),
            P("head", None),
        ),
        check_vma=False,
    )
```

profile of v0, /device:TPU:0, one launch (start us, length us, event | category | flops | bytes accessed | tf_op | source)
XLA Modules:
  0.0 682.2 jit_solution(105817919872023821)
XLA Ops:
  15.6 8.3 %all-reduce.13 = bf16[768]{0:T(1024)(128)(2,1)S(1)} all-reduce(bf16[768]{0:T(1024)(128)(2,1)S(1)} %dynamic-update-slice), channel_id=1, replica_groups=mesh['seq'=8,'head'=4] {'head'}, use_global_device_ids=true, to_apply=%add.13 | all-reduce | flops 768 | bytes 3072
  27.5 5.1 all-gather.7.cloned.1.call-done
  39.9 4.5 copy.343
  60.8 6.9 %all_gather.32 = bf16[4,256,256]{1,0,2:T(4,128)(2,1)S(1)} all-gather(bf16[4,256,64]{1,0,2:T(4,128)(2,1)S(1)} %copy.349), channel_id=1, replica_groups=mesh['seq'=8,'head'=4] {'head'}, dimensions={2}, use_global_device_ids=true | all-gather | bytes 655360 | tf_op jit(solution)/shard_map/all_gather | solution.py:177
  79.8 27.1 %all_gather.33 = f32[8,4,6]{2,1,0:T(4,128)S(1)} all-gather(f32[1,4,6]{2,1,0:T(4,128)S(1)} %bitcast_multiply_fusion.10), channel_id=1, replica_groups=mesh['seq'=8,'head'=4] {'seq'}, dimensions={0}, use_global_device_ids=true | all-gather | bytes 864 | tf_op jit(solution)/shard_map/all_gather | solution.py:18
  114.7 61.4 %all-gather.11.cloned.1.call-done = f32[32,6,64,128]{3,2,1,0:T(8,128)} async-done(((f32[4,6,64,128]{3,2,1,0:T(8,128)}), f32[32,6,64,128]{3,2,1,0:T(8,128)}) %all-gather.11.cloned.1.call-update) | async-done | bytes 6291472 | tf_op jit(solution)/shard_map/all_gather | solution.py:18
  176.1 10.7 %while.30 = (s32[]{:T(128)}, f32[4,6,64,128]{3,2,1,0:T(8,128)S(1)}, s32[]{:T(128)}, f32[8,4,6]{2,1,0:T(4,128)S(1)}, f32[8,4,6,64,128]{4,3,2,1,0:T(8,128)}, /*index=5*/s32[]{:T(128)}, s32[]{:T(128)}) while((s32[]{:T(128)}, f32[4,6,64,128]{3,2,1,0:T(8,128)S(1)}, s32[]{:T(128)}, f32[8,4,6]{2,1,0:T(4,128)S(1)}, ...), condition=%wide.region_4.6_spmd.clone, body=%wide.region_3.5_spmd.clone.sunk | while | flops 786436 | bytes 2359697 | solution.py:29
  188.8 9.5 %fusion.36 = f32[4,256,6,64]{1,3,2,0:T(8,128)} fusion(f32[4,256,6,64]{1,3,2,0:T(8,128)S(1)} %bitcast.176, f32[4,256,6,64]{1,3,2,0:T(8,128)S(1)} %fusion.84, f32[4,256,6]{1,2,0:T(8,128)S(1)} %bitcast.182, f32[4,256,256]{2,1,0:T(8,128)S(1)} %copy-done.31, pred[4,256,256]{2,1,0:T(8,128)(4,1)} %compare_and_fusion, f32[6]{0:T(128)S(1)} %copy-done.77, ...), kind=kOutput, calls=%fused_computation.67 | convolution fusion | flops 1216217088 | bytes 6103064 | tf_op jit(solution)/shard_map/jvp(ktsh,kshp->kthp)/dot_general | solution.py:68
  200.9 4.5 multiply_reduce_fusion.11
  207.1 6.7 psum.119
  223.9 6.9 %psum.120 = f32[4,256]{1,0:T(4,128)} all-reduce(f32[4,256]{1,0:T(4,128)} %copy.361), channel_id=1, replica_groups=mesh['seq'=8,'head'=4] {'head'}, use_global_device_ids=true, to_apply=%region_9.11 | all-reduce | flops 1024 | bytes 8192 | tf_op jit(solution)/shard_map/psum | solution.py:229
  233.6 7.6 %multiply_reduce_fusion.7 = (f32[384]{0:T(512)}, f32[4,256,384]{2,0,1:T(4,128)}, bf16[4,256,384]{2,0,1:T(4,128)(2,1)}, bf16[4,256,384]{2,0,1:T(4,128)(2,1)}) fusion(bf16[4,256,448]{2,0,1:T(4,128)(2,1)} %copy-done.8, bf16[4,256,838]{2,0,1:T(4,128)(2,1)} %copy.343, f32[4,256]{0,1:T(8,128)} %copy.362, f32[4,256,384]{2,0,1:T(4,128)} %get-tuple-element.489, ...), kind=kLoop, calls=%fused_computation.70 | loop fusion | flops 9436800 | bytes 9452544 | tf_op jit(solution)/shard_map/transpose(jvp())/reduce_sum | solution.py:73
  251.4 11.2 %fusion.13 = (f32[4,256,6]{1,2,0:T(8,128)}, f32[4,256,6]{1,2,0:T(8,128)}, f32[4,256,256]{2,1,0:T(8,128)S(1)}) fusion(f32[4,256,6]{1,2,0:T(8,128)S(1)} %bitcast.183, f32[4,256,256]{2,1,0:T(8,128)S(1)} %copy-done.32, pred[4,256,256]{2,1,0:T(8,128)(4,1)S(1)} %copy-done.43, f32[4,6,64,256]{3,2,1,0:T(8,128)S(1)} %bitcast.171, f32[4,256,6,64]{1,3,2,0:T(8,128)} %bitcast.173, ...), kind=kOutput, calls=%fused_computation.20 | convolution fusion | flops 1225379840 | bytes 5603328 | tf_op jit(solution)/shard_map/transpose(jvp(ktsh,kshp->kthp))/dot_general | solution.py:68
  265.9 78.0 %all-gather.13.cloned.1.call-done = f32[32,6,64,128]{3,2,1,0:T(8,128)} async-done(((f32[4,6,64,128]{3,2,1,0:T(8,128)}), f32[32,6,64,128]{3,2,1,0:T(8,128)}) %all-gather.13.cloned.1.call-update) | async-done | bytes 6291472 | tf_op jit(solution)/shard_map/all_gather | solution.py:18
  343.9 19.1 %while.31 = (s32[]{:T(128)}, f32[4,6,64,128]{3,2,1,0:T(8,128)}, s32[]{:T(128)}, f32[8,4,6]{2,1,0:T(4,128)S(1)}, f32[8,4,6,64,128]{4,3,2,1,0:T(8,128)}, /*index=5*/s32[]{:T(128)}, s32[]{:T(128)}, s32[]{:T(128)}, s32[]{:T(128)}) while((s32[]{:T(128)}, f32[4,6,64,128]{3,2,1,0:T(8,128)}, s32[]{:T(128)}, f32[8,4,6]{2,1,0:T(4,128)S(1)}, ...), condition=%wide.region_11.13_spmd.clone, body=%wide.region_10.12_spmd.clone.sunk | while | flops 786440 | bytes 2359759 | solution.py:29
  363.0 4.5 fusion.56
  381.5 8.1 %fusion.8 = f32[4,6,64,256]{3,2,1,0:T(8,128)} fusion(f32[4,6,64,256]{3,2,1,0:T(8,128)} %bitcast.169, f32[4,256,6]{1,2,0:T(8,128)S(1)} %bitcast.184, f32[4,256,256]{2,1,0:T(8,128)} %fusion.125, pred[4,256,256]{2,1,0:T(8,128)(4,1)S(1)} %copy-done.44), kind=kOutput, calls=%fused_computation.15 | convolution fusion | flops 1214251008 | bytes 4481024 | tf_op jit(solution)/shard_map/transpose(jvp(ktsh,kshp->kthp))/dot_general | solution.py:68
  390.0 5.3 multiply_reduce_fusion.5
  409.9 6.6 multiply_reduce_fusion.4
  424.0 4.9 pad_maximum_fusion.1
  431.7 5.1 fusion.76
  448.9 68.4 %all-reduce.21.cloned.1.call-done = f32[4,256,768]{2,1,0:T(8,128)} async-done(((f32[4,256,768]{2,1,0:T(8,128)}), f32[4,256,768]{2,1,0:T(8,128)}) %all-reduce.21.cloned.1.call-update) | async-done | bytes 3145744 | tf_op jit(solution)/shard_map/psum | solution.py:273
  523.9 40.6 %all-reduce.15 = (f32[192]{0:T(256)}, f32[768,6]{0,1:T(8,128)}, f32[4,384]{1,0:T(4,128)}, f32[4,64]{1,0:T(4,128)}, f32[384]{0:T(512)}, /*index=5*/f32[64]{0:T(12...) all-reduce(f32[192]{0:T(256)S(1)} %get-tuple-element.494, ...), channel_id=1, replica_groups=mesh['seq'=8,'head'=4] {'seq'}, use_global_device_ids=true, to_apply=%region_24.26 | all-reduce | flops 7442 | bytes 59536 | tf_op jit(solution)/shard_map/psum | solution.py:309
  564.6 104.5 %all-reduce.25.cloned.1.call-done = (f32[768,384]{0,1:T(8,128)}, f32[768,384]{0,1:T(8,128)}, f32[768,64]{0,1:T(8,128)}, f32[384,768]{1,0:T(8,128)}) async-done(((f32[768,384]{0,1:T(8,128)}, f32[768,384]{0,1:T(8,128)}, f32[768,64]{0,1:T(8,128)}, f32[384,768]{1,0:T(8,128)}), (f32[768,384]{0,1:T(8,128)}, f32[768,384]{0,1:T(8,128)}, f32[768,64]{0,1:T(8,128)}, ...) | async-done | bytes 3735568 | tf_op jit(solution)/shard_map/psum | solution.py:309
  (347 shorter events, 178.9 us)
Async XLA Ops:
  7.2 99.8 %copy-start = (bf16[384,768]{1,0:T(8,128)(2,1)S(1)}, bf16[384,768]{1,0:T(8,128)(2,1)}, u32[]{:S(2)}) copy-start(bf16[384,768]{1,0:T(8,128)(2,1)} %param.38) | copy-start | bytes 1769476
  7.2 25.4 %all-gather.7.cloned.1.call-start = ((), (), s32[]{:S(2)}) async-start(), calls=%async_computation.1 | async-start | bytes 1966080 | tf_op jit(solution)/shard_map/all_gather | solution.py:135
  9.5 97.5 %all-gather.9.cloned.1.call-start = ((), (), s32[]{:S(2)}) async-start(), calls=%async_computation.3 | async-start | bytes 1966080 | tf_op jit(solution)/shard_map/all_gather | solution.py:137
  10.2 165.9 %all-gather.11.cloned.1.call-start = ((), (), s32[]{:S(2)}) async-start(), calls=%async_computation.5 | async-start | bytes 7077888 | tf_op jit(solution)/shard_map/all_gather | solution.py:18
  10.9 37.7 %copy-start.68 = (f32[6]{0:T(128)}, f32[6]{0:T(128)S(1)}, u32[]{:S(2)}) copy-start(f32[6]{0:T(128)S(1)} %convert_element_type.97) | copy-start | bytes 76
  11.6 37.0 %copy-start.70 = (f32[6]{0:T(128)}, f32[6]{0:T(128)S(1)}, u32[]{:S(2)}) copy-start(f32[6]{0:T(128)S(1)} %fusion.111) | copy-start | bytes 76
  24.7 31.0 %copy-start.51 = (f32[1,448]{1,0:T(1,128)}, f32[1,448]{1,0:T(1,128)S(1)}, u32[]{:S(2)}) copy-start(f32[1,448]{1,0:T(1,128)S(1)} %get-tuple-element.511) | copy-start | bytes 5380
  24.7 31.0 %copy-start.53 = (f32[1,448]{1,0:T(1,128)}, f32[1,448]{1,0:T(1,128)S(1)}, u32[]{:S(2)}) copy-start(f32[1,448]{1,0:T(1,128)S(1)} %get-tuple-element.512) | copy-start | bytes 5380
  24.7 31.0 %copy-start.55 = (f32[1,448]{1,0:T(1,128)}, f32[1,448]{1,0:T(1,128)S(1)}, u32[]{:S(2)}) copy-start(f32[1,448]{1,0:T(1,128)S(1)} %get-tuple-element.513) | copy-start | bytes 5380
  24.7 31.0 %copy-start.57 = (f32[1,448]{1,0:T(1,128)}, f32[1,448]{1,0:T(1,128)S(1)}, u32[]{:S(2)}) copy-start(f32[1,448]{1,0:T(1,128)S(1)} %get-tuple-element.514) | copy-start | bytes 5380
  24.8 26.8 %copy-start.61 = (pred[4,256]{1,0:T(4,128)(4,1)}, pred[4,256]{1,0:T(4,128)(4,1)S(1)}, u32[]{:S(2)}) copy-start(pred[4,256]{1,0:T(4,128)(4,1)S(1)} %get-tuple-element.515) | copy-start | bytes 3076
  25.0 30.8 %copy-start.18 = (f32[4,256]{0,1:T(8,128)}, f32[4,256]{0,1:T(8,128)S(1)}, u32[]{:S(2)}) copy-start(f32[4,256]{0,1:T(8,128)S(1)} %copy.346) | copy-start | bytes 12292
  25.1 30.7 %copy-start.20 = (f32[4,256]{0,1:T(8,128)}, f32[4,256]{0,1:T(8,128)S(1)}, u32[]{:S(2)}) copy-start(f32[4,256]{0,1:T(8,128)S(1)} %copy.345) | copy-start | bytes 12292
  25.3 30.5 %copy-start.22 = (f32[4,256]{0,1:T(8,128)}, f32[4,256]{0,1:T(8,128)S(1)}, u32[]{:S(2)}) copy-start(f32[4,256]{0,1:T(8,128)S(1)} %copy.344) | copy-start | bytes 12292
  45.3 8.5 %collective-permute-start = (bf16[4,3,448]{2,0,1:T(4,128)(2,1)S(1)}, bf16[4,3,448]{2,0,1:T(4,128)(2,1)S(1)}, u32[]{:S(2)}, u32[]{:S(2)}) collective-permute-start(bf16[4,3,448]{2,0,1:T(4,128)(2,1)S(1)} %slice.155), channel_id=1, source_target_pairs={{0,4},{4,8},{8,12},{12,16},{16,20},{20,24},{24,28},{1,5},{5,9},{9,... | collective-permute-start | bytes 32264 | tf_op jit(solution)/shard_map/ppermute | solution.py:13
  52.3 21.8 %copy-start.38 = (f32[4,256,6]{1,2,0:T(8,128)}, f32[4,256,6]{1,2,0:T(8,128)S(1)}, u32[]{:S(2)}) copy-start(f32[4,256,6]{1,2,0:T(8,128)S(1)} %get-tuple-element.510) | copy-start | bytes 73732
  53.8 20.2 %copy-start.40 = (f32[4,256,6]{1,2,0:T(8,128)}, f32[4,256,6]{1,2,0:T(8,128)S(1)}, u32[]{:S(2)}) copy-start(f32[4,256,6]{1,2,0:T(8,128)S(1)} %copy.348) | copy-start | bytes 73732
  77.3 266.5 %all-gather.13.cloned.1.call-start = ((), (), s32[]{:S(2)}) async-start(), calls=%async_computation.6 | async-start | bytes 7077888 | tf_op jit(solution)/shard_map/all_gather | solution.py:18
  247.0 161.7 %all-reduce.23.cloned.1.call-start = ((), (), s32[]{:S(2)}) async-start(), calls=%async_computation.7 | async-start | bytes 2097152
  371.2 75.7 %reduce-scatter.2.cloned.1.call-start = ((), (), s32[]{:S(2)}) async-start(), calls=%async_computation.2 | async-start | bytes 3932160 | tf_op jit(solution)/shard_map/reduce_scatter | solution.py:223
  377.2 140.1 %all-reduce.21.cloned.1.call-start = ((), (), s32[]{:S(2)}) async-start(), calls=%async_computation.4 | async-start | bytes 6291456 | tf_op jit(solution)/shard_map/psum | solution.py:273
  418.2 5.7 collective-permute-start.1
  436.9 232.2 %all-reduce.25.cloned.1.call-start = ((), (), s32[]{:S(2)}) async-start(), calls=%async_computation.8 | async-start | bytes 7471104 | tf_op jit(solution)/shard_map/psum | solution.py:309
  448.9 71.1 %copy-start.48 = (f32[4,448]{1,0:T(4,128)}, f32[4,448]{1,0:T(4,128)S(1)}, u32[]{:S(2)}) copy-start(f32[4,448]{1,0:T(4,128)S(1)} %pad_add_fusion.3) | copy-start | bytes 21508
  (72 other events, 378.3 us)
Sparse Core Ops, SparseCore 0:
  10.2 22.3 all-gather.6
  34.2 19.6 all-gather.8
  77.5 98.6 all-gather.10
  247.1 96.7 all-gather.12
  371.3 34.5 all-reduce.22
  408.4 38.0 reduce-scatter.1
  448.9 68.4 all-reduce.20
  522.5 146.5 all-reduce.24
where the time goes:
time: 692 us; the launch traced here: 682 us
  waiting for transfers between devices  321 us (46%)
  blocking collectives  96.7 us (14%)
  other arithmetic  95.4 us (14%)
  matrix products  79.6 us (12%)
  local copies, waits for them, and re-layouts  67.1 us (10%)
  between operations  17.1 us (2%)
    all_gather x2, waiting for transfers between devices, entering(): everything = jax.tree.map(lambda part: lax.all_gather(part, axis), x)  139 us
    psum x1, waiting for transfers between devices, shards(): lax.psum((grad_norm_gain, grad_proj_z, grad_proj_x, grad_proj_bc, grad_pr...  105 us
    psum x1, waiting for transfers between devices, shards(): grad_normed = lax.psum(normed_terms, 'head')  68.4 us
    psum x1, blocking collectives, shards(): lax.psum((grad_norm_gain, grad_proj_z, grad_proj_x, grad_proj_bc, grad_pr...  40.6 us
    select_n x16, other arithmetic, lap(): return jax.tree.map(lambda a, b: jnp.where(reached, a, b), new, before)  29.6 us
    dot_general x3, matrix products, ssd_block_output(): jnp.einsum('ktsh,kshp->kthp', scores[..., None] * decay_mat, scaled, prec...  28.9 us
    all_gather x1, blocking collectives, entering(): everything = jax.tree.map(lambda part: lax.all_gather(part, axis), x)  27.1 us
    unnamed x183, local copies, waits for them, and re-layouts  20.1 us
  transfers between devices with their start and end apart: 10, of which 6 were waited for; matrix products, arithmetic and copies ran while one was open for 21% of the time, Pallas kernels for 0%

commit v1 on v0

v1 whole, which is shorter than its diff:
```python
import functools

import jax
import jax.numpy as jnp
from jax import lax
from jax.experimental import pallas as pl
from jax.experimental.pallas import tpu as pltpu
from jax.sharding import PartitionSpec as P

EPSILON = 1e-05
bf16 = jnp.bfloat16
f32 = jnp.float32
LANES = 128
EDGE = 16
VMEM_LIMIT = 60 * 1024 * 1024
STEPS = 32000.0
UNIT = 16384.0
LN2 = 0.6931471805599453


def swap(x, axis, bit):
    return lax.ppermute(x, axis, [(i, i ^ bit) for i in range(lax.axis_size(axis))])


def shift(x, axis, distance):
    n = lax.axis_size(axis)
    return lax.ppermute(x, axis, [(i, i + distance) for i in range(n) if 0 <= i + distance < n])


def head_pieces(x):
    far = swap(x, "head", 2)
    near = swap(x, "head", 1)
    return x, near, far, swap(far, "head", 1)


def nn(a, b):
    return lax.dot_general(a, b, (((1,), (0,)), ((), ())), preferred_element_type=f32)


def nt(a, b):
    return lax.dot_general(a, b, (((1,), (1,)), ((), ())), preferred_element_type=f32)


def tn(a, b):
    return lax.dot_general(a, b, (((0,), (0,)), ((), ())), preferred_element_type=f32)


def split2(v):
    hi = v.astype(bf16)
    return hi, (v - hi.astype(f32)).astype(bf16)


def split3(v):
    hi = v.astype(bf16)
    rest = v - hi.astype(f32)
    mid = rest.astype(bf16)
    return hi, mid, (rest - mid.astype(f32)).astype(bf16)


def spread_matrix(heads, size):
    row = lax.broadcasted_iota(jnp.int32, (LANES, heads * size), 0)
    col = lax.broadcasted_iota(jnp.int32, (LANES, heads * size), 1)
    inside = (col >= row * size) & (col < (row + 1) * size)
    return jnp.where(inside, 1.0, 0.0).astype(bf16)


def spread(v, matrix):
    hi, lo = split2(v)
    return nn(hi, matrix) + nn(lo, matrix)


def collapse(v, matrix):
    hi, lo = split2(v)
    return nt(hi, matrix) + nt(lo, matrix)


def triangle(count, lower):
    row = lax.broadcasted_iota(jnp.int32, (count, count), 0)
    col = lax.broadcasted_iota(jnp.int32, (count, count), 1)
    keep = (row >= col) if lower else (row <= col)
    return jnp.where(keep, 1.0, 0.0).astype(bf16)


def exact_sums(matrix, v):
    hi, mid, lo = split3(v)
    return nn(matrix, hi) + nn(matrix, mid) + nn(matrix, lo)


def segments(positions, lens_ref, pack, count):
    total = jnp.zeros(positions.shape, jnp.int32)
    end = jnp.int32(0)
    for k in range(count):
        end = end + lens_ref[pack, k]
        total = total + jnp.where(positions >= end, 1, 0)
    return total


def column_segments(meta_ref, lens_ref, pack, count, nseq, before):
    rows = lax.broadcasted_iota(jnp.int32, (count + before, 1), 0)
    return segments(rows + (meta_ref[0] * count - before), lens_ref, pack, nseq)


def row_segments(meta_ref, lens_ref, pack, count, nseq):
    cols = lax.broadcasted_iota(jnp.int32, (1, count), 1)
    return segments(cols + meta_ref[0] * count, lens_ref, pack, nseq)


def carry_column(meta_ref, seg_ext, before):
    same = seg_ext[before:] == seg_ext[before - 1 : before]
    return jnp.where(same & (meta_ref[0] > 0), 1.0, 0.0)


def to_int16(v):
    return jnp.floor(v + 0.5).astype(jnp.int32).astype(jnp.int16)


def encode_state(out, p, state, decay, heads, size):
    lane = lax.broadcasted_iota(jnp.int32, (1, LANES), 1)
    powers = jnp.zeros((1, LANES), f32)
    for h in range(heads):
        part = state[h * size : (h + 1) * size]
        top = jnp.max(jnp.max(jnp.abs(part), axis=0, keepdims=True), axis=1, keepdims=True)
        power = jnp.ceil(jnp.log(jnp.maximum(top, 1e-30)) / LN2)
        powers = powers + jnp.where(lane == h, power, 0.0)
        codes = jnp.clip(part * (jnp.exp(-power * LN2) * STEPS), -32767.0, 32767.0)
        out[p, h * size : (h + 1) * size, :] = to_int16(codes)
    row = lax.broadcasted_iota(jnp.int32, (EDGE, LANES), 0)
    coarse = jnp.floor(decay * UNIT)
    fine = (decay * UNIT - coarse) * UNIT
    tail = jnp.where(row == 0, powers, jnp.where(row == 1, coarse, jnp.where(row == 2, fine, 0.0)))
    out[p, heads * size :, :] = to_int16(tail)


def decode_state(block, heads, size):
    values = block.astype(jnp.int32).astype(f32)
    tail = values[heads * size :]
    scale = jnp.exp(tail[0:1] * LN2) / STEPS
    decay = (tail[1:2] + tail[2:3] / UNIT) / UNIT
    return scaled_state(values[: heads * size], scale, heads, size), decay


def sigmoid(v):
    return 1.0 / (1.0 + jnp.exp(-v))


def scaled_state(state, decay, heads, size):
    return jnp.concatenate(
        [state[h * size : (h + 1) * size] * decay[:, h : h + 1] for h in range(heads)], axis=0
    )


def front_kernel(dims, meta, lens, *refs):
    packs, count, features, inner, bc, heads, size, width, nseq = dims
    tokens, edges, shared = refs[0:4], refs[4:8], refs[8:12]
    wz, wx, wdt, conv_x, small = refs[12:17]
    (
        normed_o, inv_o, edge_o, edge_inv_o, gate_o, rawx_o, rawbc_o, xbc_o, dsx_o, dsbc_o, dt_o,
        sig_o, cum_o, keep_o, send_o,
    ) = refs[17:32]
    stage, edge_stage, weights, raws, edge_raws, conv, gain = refs[32:]
    pack = pl.program_id(0)
    head = meta[1]
    part = features // 4
    wide = edge_stage.shape[2]

    def normalise(values):
        mean = jnp.sum(values * values, axis=0, keepdims=True) / features
        inv = lax.rsqrt(mean + EPSILON)
        return inv, ((values * inv) * gain[...]).astype(bf16)

    def raw_of(normed):
        wbc = weights[...].reshape(bc, weights.shape[2])[:, :features]
        return jnp.concatenate([nn(normed, wx[...]), nt(normed, wbc)], axis=1).astype(bf16)

    @pl.when(pack == 0)
    def _():
        for k in range(4):
            weights[head ^ k] = shared[k][...]
            edge_stage[head ^ k] = edges[k][...]
        extra = weights[...].reshape(bc, weights.shape[2])[:, features:].astype(f32)
        conv[:, :inner] = conv_x[...]
        conv[:, inner:] = jnp.transpose(extra)[0:8]
        bc_part = bc // 4
        pieces = part // bc_part
        for h in range(4):
            for c in range(pieces):
                gain[h * part + c * bc_part : h * part + (c + 1) * bc_part, :] = extra[
                    h * bc_part : (h + 1) * bc_part, width + 1 + c : width + 2 + c
                ]
        inv, normed = normalise(edge_stage[...].reshape(features, wide).astype(f32))
        edge_inv_o[...] = inv
        edge_o[...] = normed
        edge_raws[...] = raw_of(jnp.transpose(normed)).astype(f32)

    for k in range(4):
        stage[head ^ k] = tokens[k][0]
    inv, normed_t = normalise(stage[...].reshape(features, count).astype(f32))
    inv_o[0] = inv
    normed_o[0] = normed_t
    normed = jnp.transpose(normed_t)
    gate_o[0] = nn(normed, wz[...]).astype(bf16)
    raws[EDGE:, :] = raw_of(normed).astype(f32)
    raws[0:EDGE, :] = edge_raws[pl.ds(pl.multiple_of(pack * EDGE, EDGE), EDGE), :]

    def own_bc(values):
        bc_part = bc // 4
        parts = [values[:, inner + h * bc_part : inner + (h + 1) * bc_part] for h in range(4)]
        low = jnp.where((head & 1) == 0, parts[0], parts[1])
        high = jnp.where((head & 1) == 0, parts[2], parts[3])
        return jnp.where((head >> 1) == 0, low, high)

    rawx_o[0] = raws[:, :inner].astype(bf16)
    rawbc_o[0] = own_bc(raws[...]).astype(bf16)
    seg = column_segments(meta, lens, pack, count, nseq, EDGE)
    seg_main = seg[EDGE:]
    pre = jnp.broadcast_to(conv[width : width + 1, :], (count, inner + bc))
    for k in range(width):
        low = EDGE - (width - 1) + k
        mask = jnp.where(seg[low : low + count] == seg_main, 1.0, 0.0)
        pre = pre + conv[k : k + 1, :] * raws[low : low + count, :] * mask
    sig_pre = sigmoid(pre)
    xbc = (pre * sig_pre).astype(bf16)
    xbc_o[0] = xbc
    slope = sig_pre * (1.0 + pre * (1.0 - sig_pre))
    dsx_o[0] = slope[:, :inner]
    dsbc_o[0] = own_bc(slope)
    lane = lax.broadcasted_iota(jnp.int32, (1, LANES), 1)
    live = lane < heads
    v = nt(normed, wdt[...]).astype(bf16).astype(f32) + small[0:1, :]
    soft = jnp.maximum(v, 0.0) + jnp.log1p(jnp.exp(-jnp.abs(v)))
    dt = jnp.where(live, soft, 0.0)
    dt_o[0] = dt
    sig_o[0] = jnp.where(live, sigmoid(v), 0.0)
    rate = -dt * jnp.exp(small[1:2, :])
    cum = exact_sums(triangle(count, True), rate)
    cum_o[0] = cum
    cum_end = cum[count - 1 : count]
    weight = jnp.where(seg_main == seg[count + EDGE - 1 :], jnp.exp(cum_end - cum), 0.0) * dt
    matrix = spread_matrix(heads, size)
    scaled = (xbc[:, :inner].astype(f32) * spread(weight, matrix)).astype(bf16)
    state = tn(scaled, xbc[:, inner : inner + bc // 2])
    carry = carry_column(meta, seg, EDGE)
    store_state(
        meta, packs, pack, keep_o, send_o, state, carry[count - 1 :] * jnp.exp(cum_end), heads, size
    )


def store_state(meta, packs, pack, keep_o, send_o, state, decay, heads, size):
    mine = (pack // (packs // 2)) == (meta[0] & 1)

    @pl.when(mine)
    def _():
        encode_state(keep_o, 0, state, decay, heads, size)

    @pl.when(jnp.logical_not(mine))
    def _():
        encode_state(send_o, 0, state, decay, heads, size)


def load_state(meta, packs, pack, keep, recv, heads, size):
    mine = (pack // (packs // 2)) == (meta[0] & 1)
    block = jnp.where(mine, keep[0].astype(jnp.int32), recv[0].astype(jnp.int32))
    return decode_state(block, heads, size)[0]


def decay_parts(cum_col, cum_row, masked):
    return masked * jnp.exp(jnp.minimum(cum_col - cum_row, 0.0))


def block_mask(meta, lens, pack, count, nseq):
    col = column_segments(meta, lens, pack, count, nseq, 0)
    row = row_segments(meta, lens, pack, count, nseq)
    tri = lax.broadcasted_iota(jnp.int32, (count, count), 0) >= lax.broadcasted_iota(
        jnp.int32, (count, count), 1
    )
    return tri & (col == row)


def inner_kernel(dims, meta, lens, *refs):
    packs, count, features, inner, bc, heads, size, width, nseq = dims
    xbc, dt, cum, cot0, cot1, cot2, cot3, wout, inner_o, cot_o, gg_o, stage = refs
    pack = pl.program_id(0)
    head = meta[1]
    half = bc // 2
    b_vals, c_vals = xbc[0, :, inner : inner + half], xbc[0, :, inner + half :]
    scores = jnp.where(block_mask(meta, lens, pack, count, nseq), nt(c_vals, b_vals), 0.0)
    cum_col = cum[0]
    cum_row = jnp.transpose(cum_col)
    dt_row = jnp.transpose(dt[0])
    lane = lax.broadcasted_iota(jnp.int32, (count, 2 * size), 1)
    for pair in range(heads // 2):
        cols = slice(2 * pair * size, (2 * pair + 2) * size)
        x_pair = xbc[0, :, cols]
        parts = []
        for h in (2 * pair, 2 * pair + 1):
            weights = decay_parts(cum_col[:, h : h + 1], cum_row[h : h + 1], scores)
            parts.append(nn((weights * dt_row[h : h + 1]).astype(bf16), x_pair))
        inner_o[0, :, cols] = jnp.where(lane < size, parts[0], parts[1])
    for k, cot in enumerate((cot0, cot1, cot2, cot3)):
        stage[head ^ k] = cot[0]
    cotangent = stage[...].reshape(features, count)
    cot_o[0] = cotangent
    gg_o[0] = jnp.transpose(nn(wout[...], cotangent))


def compose(lower, upper, heads, size):
    return scaled_state(lower[0], upper[1], heads, size) + upper[0], lower[1] * upper[1]


def choose(flag, a, b):
    return jnp.where(flag, a[0], b[0]), jnp.where(flag, a[1], b[1])


def pair_kernel(dims, rev, meta, own, other, out):
    packs, heads, size = dims
    upper_is_own = ((meta[0] & 1) ^ rev) == 1
    for p in range(packs // 2):
        a, b = decode_state(own[p], heads, size), decode_state(other[p], heads, size)
        both = compose(choose(upper_is_own, b, a), choose(upper_is_own, a, b), heads, size)
        encode_state(out, p, *both, heads, size)


def entering_from(before, b, p, heads, size):
    if before is None:
        return (jnp.zeros_like(b[0]), jnp.ones_like(b[1])), b
    entering = decode_state(before[p], heads, size)
    return entering, compose(b, entering, heads, size)


def cube_kernel(dims, rev, bit, first, meta, *refs):
    packs, heads, size = dims
    total, other = refs[0], refs[1]
    before, next_o, before_o = (None, refs[2], refs[3]) if first else refs[2:5]
    upper_is_own = (((meta[0] >> bit) & 1) ^ rev) == 1
    for p in range(packs // 2):
        a, b = decode_state(total[p], heads, size), decode_state(other[p], heads, size)
        both = compose(choose(upper_is_own, b, a), choose(upper_is_own, a, b), heads, size)
        encode_state(next_o, p, *both, heads, size)
        entering, longer = entering_from(before, b, p, heads, size)
        encode_state(before_o, p, *choose(upper_is_own, longer, entering), heads, size)


def last_kernel(dims, rev, bit, first, meta, *refs):
    packs, heads, size = dims
    own, pair, other = refs[0:3]
    before, keep_o, send_o = (None, refs[3], refs[4]) if first else refs[3:6]
    add = (((meta[0] >> bit) & 1) ^ rev) == 1
    upper_is_own = ((meta[0] & 1) ^ rev) == 1
    for p in range(packs // 2):
        entering, longer = entering_from(
            before, decode_state(other[p], heads, size), p, heads, size
        )
        low = choose(add, longer, entering)
        lower = decode_state(jnp.where(upper_is_own, pair[p].astype(jnp.int32), own[p].astype(jnp.int32)), heads, size)
        high = compose(low, lower, heads, size)
        encode_state(keep_o, p, *choose(upper_is_own, high, low), heads, size)
        encode_state(send_o, p, *choose(upper_is_own, low, high), heads, size)


def gate_kernel(dims, meta, lens, *refs):
    packs, count, features, inner, bc, heads, size, width, nseq = dims
    xbc, cum, inner_in, keep, recv, gate, gg, gain, skip, y_o, mixed_o, stats_o = refs
    pack = pl.program_id(0)
    state_hi, state_lo = split2(load_state(meta, packs, pack, keep, recv, heads, size))
    carry = carry_column(meta, column_segments(meta, lens, pack, count, nseq, EDGE), EDGE)
    matrix = spread_matrix(heads, size)
    entering = spread(carry * jnp.exp(cum[0]), matrix)
    c_vals = xbc[0, :, inner + bc // 2 :]
    y = inner_in[0] + entering * (nt(c_vals, state_hi) + nt(c_vals, state_lo))
    y_o[0] = y
    gate_f = gate[0].astype(f32)
    ssd = y + xbc[0, :, :inner].astype(f32) * skip[...]
    mixed = ssd * (gate_f * sigmoid(gate_f))
    mixed_o[0] = mixed
    squares = jnp.sum(mixed * mixed, axis=1, keepdims=True)
    dots = jnp.sum(gain[...] * gg[0] * mixed, axis=1, keepdims=True)
    lane = lax.broadcasted_iota(jnp.int32, (count, LANES), 1)
    both = jnp.where(lane == 0, squares, 0.0) + jnp.where(lane == 1, dots, 0.0)
    stats_o[0] = jnp.transpose(both)[0:2]


def grad_kernel(dims, total_inner, meta, lens, *refs):
    packs, count, features, inner, bc, heads, size, width, nseq = dims
    (
        stats, xbc, cum, y, mixed, gate, gg, gain, skip,
        gy_o, ey_o, el_o, gated_o, ggate_o, keep_o, send_o, small_o,
    ) = refs
    pack = pl.program_id(0)
    sums = stats[0, 0] + stats[1, 0] + stats[2, 0] + stats[3, 0]
    row = lax.broadcasted_iota(jnp.int32, (LANES, count), 0)
    wide = jnp.where(row == 0, sums[0:1], 0.0) + jnp.where(row == 1, sums[1:2], 0.0)
    cols = jnp.transpose(wide)
    inv = lax.rsqrt(cols[:, 0:1] / total_inner + EPSILON)
    dot = cols[:, 1:2] / total_inner
    mixed_f, gg_f = mixed[0], gg[0]
    gated_o[0] = (mixed_f * inv * gain[...]).astype(bf16)
    grad_mixed = inv * gain[...] * gg_f - mixed_f * (inv * inv * inv * dot)
    gate_f = gate[0].astype(f32)
    sig = sigmoid(gate_f)
    gy_f = grad_mixed * (gate_f * sig)
    gy_o[0] = gy_f
    x_f = xbc[0, :, :inner].astype(f32)
    ssd = y[0] + x_f * skip[...]
    ggate_o[0] = (grad_mixed * ssd * sig * (1.0 + gate_f * (1.0 - sig))).astype(bf16)
    carry = carry_column(meta, column_segments(meta, lens, pack, count, nseq, EDGE), EDGE)
    matrix = spread_matrix(heads, size)
    ey_hi, ey_lo = split2(gy_f * spread(carry * jnp.exp(cum[0]), matrix))
    ey_o[0] = ey_hi
    el_o[0] = ey_lo
    c_vals = xbc[0, :, inner + bc // 2 :]
    state_grad = tn(ey_hi, c_vals) + tn(ey_lo, c_vals)
    decay = carry[count - 1 :] * jnp.exp(cum[0, count - 1 :])
    store_state(meta, packs, pack, keep_o, send_o, state_grad, decay, heads, size)

    @pl.when(pack == 0)
    def _():
        small_o[...] = jnp.zeros_like(small_o)

    small_o[0:1, :] += jnp.sum(gg_f * mixed_f * inv, axis=0, keepdims=True)
    small_o[1:2, :] += jnp.sum(gy_f * x_f, axis=0, keepdims=True)


def diag_kernel(dims, meta, lens, *refs):
    packs, count, features, inner, bc, heads, size, width, nseq = dims
    xbc, dt, cum, gy, ey, el, keep, recv, dx_o, dbc_o = refs
    pack = pl.program_id(0)
    half = bc // 2
    b_vals, c_vals = xbc[0, :, inner : inner + half], xbc[0, :, inner + half :]
    mask = block_mask(meta, lens, pack, count, nseq)
    scores = jnp.where(mask, nt(c_vals, b_vals), 0.0)
    cum_col = cum[0]
    cum_row = jnp.transpose(cum_col)
    dt_row = jnp.transpose(dt[0])
    lane = lax.broadcasted_iota(jnp.int32, (count, 2 * size), 1)
    grad_scores = jnp.zeros((count, count), f32)
    zero = jnp.zeros((), bf16)
    for pair in range(heads // 2):
        cols = slice(2 * pair * size, (2 * pair + 2) * size)
        x_pair = xbc[0, :, cols]
        gy_pair, gy_rest = split2(gy[0, :, cols])
        parts = []
        for h in (2 * pair, 2 * pair + 1):
            own = (lane < size) if h % 2 == 0 else (lane >= size)
            part = jnp.exp(jnp.minimum(cum_col[:, h : h + 1] - cum_row[h : h + 1], 0.0)) * dt_row[h : h + 1]
            weights = (scores * part).astype(bf16)
            parts.append(tn(weights, gy_pair))
            outer = nt(jnp.where(own, gy_pair, zero), x_pair) + nt(
                jnp.where(own, gy_rest, zero), x_pair
            )
            grad_scores = grad_scores + outer * part
        dx_o[0, :, cols] = jnp.where(lane < size, parts[0], parts[1])
    hi, lo = split2(jnp.where(mask, grad_scores, 0.0))
    state_hi, state_lo = split2(load_state(meta, packs, pack, keep, recv, heads, size))
    dbc_o[0, :, :half] = tn(hi, c_vals) + tn(lo, c_vals)
    dbc_o[0, :, half:] = (
        nn(hi, b_vals) + nn(lo, b_vals) + nn(ey[0], state_hi) + nn(ey[0], state_lo) + nn(el[0], state_hi)
    )


def scatter_pieces(head, stage, own_o, far_o, send_o):
    own_o[0] = stage[head]
    send_o[0, 0] = stage[head ^ 1].astype(bf16)
    far_o[0] = stage[head ^ 2]
    send_o[1, 0] = stage[head ^ 3].astype(bf16)


def side_kernel(dims, meta, lens, *refs):
    packs, count, features, inner, bc, heads, size, width, nseq = dims
    gated, cot, wout, normed, ggate, wz, own_o, far_o, send_o, terms_o, grads_o, stage, sums = refs
    pack = pl.program_id(0)
    out = tn(wout[...], jnp.transpose(gated[0]))
    stage[...] = out.reshape(stage.shape)
    scatter_pieces(meta[1], stage, own_o, far_o, send_o)
    terms_o[0] = nt(wz[...], ggate[0])

    @pl.when(pack == 0)
    def _():
        sums[...] = jnp.zeros_like(sums)

    sums[0:features, :] += nn(normed[0], ggate[0])
    sums[features:, :] += nn(cot[0], gated[0])

    @pl.when(pack == packs - 1)
    def _():
        grads_o[...] = sums[...].astype(bf16)


def end_weights(seg, seg_main, cum_col, dt_col, count):
    cum_end = cum_col[count - 1 :]
    end = seg[count + EDGE - 1 :]
    return jnp.where(seg_main == end, jnp.exp(cum_end - cum_col), 0.0) * dt_col


def share_kernel(dims, meta, lens, *refs):
    packs, count, features, inner, bc, heads, size, width, nseq = dims
    xbc, dt, cum, dbc, gkeep, grecv, own_o, near_o = refs
    pack = pl.program_id(0)
    half, quarter = bc // 2, bc // 4
    g_hi, g_lo = split2(load_state(meta, packs, pack, gkeep, grecv, heads, size))
    seg = column_segments(meta, lens, pack, count, nseq, EDGE)
    weight = end_weights(seg, seg[EDGE:], cum[0], dt[0], count)
    wide = spread(weight, spread_matrix(heads, size))
    hi, lo = split2(wide * xbc[0, :, :inner].astype(f32))
    grad_b = dbc[0, :, :half] + nn(hi, g_hi) + nn(lo, g_hi) + nn(hi, g_lo)
    grad_c = dbc[0, :, half:]
    even = jnp.concatenate([grad_b[:, :quarter], grad_c[:, :quarter]], axis=1)
    odd = jnp.concatenate([grad_b[:, quarter:], grad_c[:, quarter:]], axis=1)
    first = (meta[1] & 1) == 0
    own_o[0] = jnp.where(first, even, odd)
    near_o[0] = jnp.where(first, odd, even)


def middle_kernel(dims, meta, *refs):
    packs, quarter = dims
    own, near, keep_o, send_o = refs
    first = (meta[1] >> 1) == 0
    for p in range(packs // 2):
        a, b = own[p] + near[p], own[p + packs // 2] + near[p + packs // 2]
        low = jnp.concatenate([a[:, :quarter], b[:, :quarter]], axis=1)
        high = jnp.concatenate([a[:, quarter:], b[:, quarter:]], axis=1)
        keep_o[p] = jnp.where(first, low, high)
        send_o[p] = jnp.where(first, high, low)


def conv_back(grads, gpad, raws, conv, gconv_o, seg, dims):
    count, width = dims
    ext = count + EDGE
    seg_main = seg[EDGE:]
    seg_pad = jnp.concatenate([seg, jnp.full((8, 1), -1, jnp.int32)], axis=0)
    gpad[EDGE : EDGE + count, :] = grads
    total = jnp.zeros((ext, grads.shape[1]), f32)
    for k in range(width):
        low = EDGE - (width - 1) + k
        mask = jnp.where(seg[low : low + count] == seg_main, 1.0, 0.0)
        gconv_o[k : k + 1, :] += jnp.sum(
            grads * (raws[low : low + count, :] * mask), axis=0, keepdims=True
        )
        lag = width - 1 - k
        mask_back = jnp.where(seg_pad[lag : lag + ext] == seg, 1.0, 0.0)
        total = total + conv[k : k + 1, :] * (gpad[lag : lag + ext, :] * mask_back)
    gconv_o[width : width + 1, :] += jnp.sum(grads, axis=0, keepdims=True)
    return total.astype(bf16)


def xback_kernel(dims, meta, lens, *refs):
    packs, count, features, inner, bc, heads, size, width, nseq = dims
    (
        xbc, dt, sig, cum, gy, y, dx, keep, recv, gkeep, grecv, slope, raw, normed, edge, terms,
        wx, wdt, conv, small, skip,
        terms_o, edge_o, grads_o, gconv_o, gsmall_o, gdt_o,
        gpad, raws, sums, gdt_sums,
    ) = refs
    pack = pl.program_id(0)
    state = load_state(meta, packs, pack, keep, recv, heads, size)
    gstate = load_state(meta, packs, pack, gkeep, grecv, heads, size)
    g_hi, g_lo = split2(gstate)
    seg = column_segments(meta, lens, pack, count, nseq, EDGE)
    matrix = spread_matrix(heads, size)
    b_vals = xbc[0, :, inner : inner + bc // 2]
    x_f = xbc[0, :, :inner].astype(f32)
    gy_f = gy[0].astype(bf16).astype(f32)
    cum_col, dt_col = cum[0], dt[0]
    cum_end = cum_col[count - 1 :]
    wide = spread(end_weights(seg, seg[EDGE:], cum_col, dt_col, count), matrix)
    u_wide = wide * (nt(b_vals, g_hi) + nt(b_vals, g_lo))
    diag = dx[0]
    grad_x = (diag + u_wide + gy_f * skip[...]) * slope[0]
    row_sum = collapse(gy_f * y[0], matrix)
    col_sum = collapse(x_f * diag, matrix)
    state_sum = collapse(x_f * u_wide, matrix)
    carry = carry_column(meta, seg, EDGE)
    hi, lo = split2(gstate * state)
    ones = jnp.ones((8, LANES), bf16)
    by_head = collapse(nt(ones, hi) + nt(ones, lo), matrix)[0:1]
    last = by_head * carry[count - 1 :] * jnp.exp(cum_end) + jnp.sum(state_sum, axis=0, keepdims=True)
    rows = lax.broadcasted_iota(jnp.int32, (count, LANES), 0)
    grad_cum = row_sum - col_sum - state_sum + jnp.where(rows == count - 1, last, 0.0)
    grad_rate = exact_sums(triangle(count, False), grad_cum)
    decay_rate = -jnp.exp(small[1:2, :])
    ratio = jnp.where(dt_col > 1e-30, sig[0] / jnp.maximum(dt_col, 1e-30), 1.0)
    lane = lax.broadcasted_iota(jnp.int32, (1, LANES), 1)
    grad_dt = ratio * (col_sum + state_sum) + grad_rate * decay_rate * sig[0]
    grad_dt = jnp.where(lane < heads, grad_dt, 0.0)
    grad_dt_low = grad_dt.astype(bf16)

    @pl.when(pack == 0)
    def _():
        for ref in (sums, gdt_sums, gconv_o, gsmall_o, gpad, edge_o):
            ref[...] = jnp.zeros_like(ref)

    gsmall_o[0:1, :] += jnp.sum(grad_dt, axis=0, keepdims=True)
    gsmall_o[1:2, :] += jnp.sum(grad_rate * dt_col * decay_rate, axis=0, keepdims=True)
    raws[...] = raw[0].astype(f32)
    grad_raw = conv_back(grad_x, gpad, raws, conv, gconv_o, seg, (count, width))
    main = grad_raw[EDGE:]
    edge_o[pl.ds(pl.multiple_of(pack * EDGE, EDGE), EDGE), :] = grad_raw[:EDGE]
    terms_o[0] = terms[0] + nt(wx[...], main) + nt(wdt[...], grad_dt_low)
    sums[...] += nn(normed[0], main)
    gdt_sums[...] += nn(normed[0], grad_dt_low)

    @pl.when(pack == packs - 1)
    def _():
        grads_o[...] = (sums[...] + nn(edge[...], edge_o[...])).astype(bf16)
        gdt_o[...] = jnp.transpose(gdt_sums[...])[0:8]


def bcback_kernel(dims, meta, lens, *refs):
    packs, count, features, inner, bc, heads, size, width, nseq = dims
    (
        keep, recv, slope, raw, normed, edge, terms, wbc, wx, edge_x, conv,
        own_o, far_o, send_o, dots_o, grads_o, gconv_o,
        stage, gpad, raws, sums, edge_bc,
    ) = refs
    pack = pl.program_id(0)
    quarter = bc // 4
    wide = edge.shape[1]

    @pl.when(pack == 0)
    def _():
        for ref in (sums, gconv_o, gpad, edge_bc):
            ref[...] = jnp.zeros_like(ref)

    @pl.when(pack < packs)
    def _():
        both = keep[0] + recv[0]
        grad = jnp.where(pack < packs // 2, both[:, :quarter], both[:, quarter:]) * slope[0]
        seg = column_segments(meta, lens, pack, count, nseq, EDGE)
        raws[...] = raw[0].astype(f32)
        grad_raw = conv_back(grad, gpad, raws, conv, gconv_o, seg, (count, width))
        main = grad_raw[EDGE:]
        edge_bc[pl.ds(pl.multiple_of(pack * EDGE, EDGE), EDGE), :] = grad_raw[:EDGE]
        whole = terms[0] + nt(wbc[...], main)
        sums[...] += nn(normed[0], main)
        dots_o[0] = jnp.sum(whole * normed[0].astype(f32), axis=0, keepdims=True)
        stage[...] = whole.reshape(stage.shape)

    @pl.when(pack == packs)
    def _():
        whole = nt(wx[...], edge_x[...]) + nt(wbc[...], edge_bc[...])
        dots = jnp.sum(whole * edge[...].astype(f32), axis=0, keepdims=True)
        dots_o[0] = jnp.concatenate([dots, jnp.zeros((1, count - wide), f32)], axis=1)
        total = jnp.transpose(sums[...] + nn(edge[...], edge_bc[...]))
        grads_o[...] = jnp.concatenate(
            [total[:, :inner], total[:, inner:]], axis=0
        ).astype(bf16)
        padded = jnp.concatenate([whole, jnp.zeros((features, count - wide), f32)], axis=1)
        stage[...] = padded.reshape(stage.shape)

    scatter_pieces(meta[1], stage, own_o, far_o, send_o)


def final_kernel(dims, meta, *refs):
    packs, count, features = dims
    (
        own, near, far, dots, tokens, edge, inv, edge_inv, gain, out_grad,
        in_grad_o, edge_o, gain_o,
    ) = refs
    pack = pl.program_id(0)
    wide = edge.shape[1]
    grad = own[0] + near[0, 0].astype(f32) + far[0].astype(f32)
    mean = (dots[0, 0] + dots[1, 0] + dots[2, 0] + dots[3, 0]) / features

    @pl.when(pack == 0)
    def _():
        gain_o[...] = jnp.zeros_like(gain_o)

    @pl.when(pack < packs)
    def _():
        unit = tokens[0].astype(f32) * inv[0]
        grads = inv[0] * (gain[...] * grad - unit * mean)
        in_grad_o[0] = out_grad[0].astype(f32) + grads
        gain_o[...] += jnp.sum(grad * unit, axis=1, keepdims=True)

    @pl.when(pack == packs)
    def _():
        unit = edge[...].astype(f32) * edge_inv[...]
        edge_o[...] = edge_inv[...] * (gain[...] * grad[:, :wide] - unit * mean[:, :wide])
        gain_o[...] += jnp.sum(grad[:, :wide] * unit, axis=1, keepdims=True)


def total_kernel(parts, out):
    total = parts[0].astype(f32)
    for k in range(1, parts.shape[0]):
        total = total + parts[k].astype(f32)
    total = total.astype(bf16)
    for k in range(out.shape[0]):
        out[k] = total


def whole_spec(shape):
    return pl.BlockSpec(shape, lambda p, *_: (0,) * len(shape))


def pack_spec(shape):
    return pl.BlockSpec((1,) + shape, lambda p, *_: (p,) + (0,) * len(shape))


def half_spec(shape, half):
    return pl.BlockSpec((1,) + shape, lambda p, *_: (p % half,) + (0,) * len(shape))


def side_spec(shape, half, keep):
    def index(p, meta, *_):
        side = meta[0] & 1 if keep else 1 - (meta[0] & 1)
        group = p // half
        spot = jnp.where(group == side, p % half, jnp.where(group < side, 0, half - 1))
        return (spot,) + (0,) * len(shape)

    return pl.BlockSpec((1,) + shape, index)


def call(kernel, grid, in_specs, out_specs, out_shape, scratch, cost, prefetch, *args):
    return pl.pallas_call(
        kernel,
        grid_spec=pltpu.PrefetchScalarGridSpec(
            num_scalar_prefetch=len(prefetch),
            grid=grid,
            in_specs=in_specs,
            out_specs=out_specs,
            scratch_shapes=scratch,
        ),
        out_shape=out_shape,
        compiler_params=pltpu.CompilerParams(vmem_limit_bytes=VMEM_LIMIT),
        cost_estimate=pl.CostEstimate(flops=cost[0], bytes_accessed=cost[1], transcendentals=0),
    )(*prefetch, *args)


def shape(*dims_and_type):
    return jax.ShapeDtypeStruct(dims_and_type[:-1], dims_and_type[-1])


def scan_states(keep, send, meta, packs, heads, size, rev):
    dims = (packs, heads, size)
    rows = heads * size
    half = packs // 2
    pay = shape(half, rows + EDGE, LANES, jnp.int16)
    spec = whole_spec(pay.shape)
    cost = (1 << 20, 1 << 20)
    bits = (lax.axis_size("seq") - 1).bit_length()
    other = swap(send, "seq", 1)
    total = call(
        functools.partial(pair_kernel, dims, rev), (1,), [spec, spec], spec, pay, [], cost, (meta,),
        keep, other,
    )
    before = None
    for bit in range(1, bits):
        got = swap(total, "seq", 1 << bit)
        extra = () if before is None else (before,)
        if bit < bits - 1:
            total, before = call(
                functools.partial(cube_kernel, dims, rev, bit, before is None), (1,),
                [spec] * (2 + len(extra)), [spec, spec], [pay, pay], [], cost, (meta,),
                total, got, *extra,
            )
        else:
            own, back = call(
                functools.partial(last_kernel, dims, rev, bit, before is None), (1,),
                [spec] * (3 + len(extra)), [spec, spec], [pay, pay], [], cost,
                (meta,), keep, other, got, *extra,
            )
    return own, swap(back, "seq", 1)


def reduce_over_seq(parts, cost):
    n = lax.axis_size("seq")
    rows, cols = parts.shape
    pieces = lax.all_to_all(parts.reshape(n, rows // n, cols), "seq", 0, 0)
    spec = whole_spec(pieces.shape)
    shares = call(total_kernel, (1,), [spec], spec, shape(*pieces.shape, bf16), [], cost, (), pieces)
    return lax.all_to_all(shares, "seq", 0, 0).reshape(rows, cols)


def shards(
    tokens_in, out_grad, lengths, norm_gain, proj_z, proj_x, proj_bc, proj_dt, conv_x, conv_bc,
    bias_x, bias_bc, dt_bias, a_log, d_skip, gate_gain, proj_out,
):
    packs, count, part = tokens_in.shape
    features, inner = proj_x.shape
    heads = proj_dt.shape[1]
    size = inner // heads
    width = conv_x.shape[0]
    nseq = lengths.shape[1]
    bc_part = proj_bc.shape[1]
    bc = bc_part * lax.axis_size("head")
    half = packs // 2
    chans = inner + bc
    ext = count + EDGE
    rows = heads * size
    total_inner = inner * lax.axis_size("head")
    dims = (packs, count, features, inner, bc, heads, size, width, nseq)
    seq_place, head_place = lax.axis_index("seq"), lax.axis_index("head")
    meta = jnp.stack([seq_place, head_place]).astype(jnp.int32)
    pre = (meta, lengths)
    grid = (packs,)

    tokens = jnp.swapaxes(tokens_in, 1, 2)
    cotangent = jnp.swapaxes(out_grad, 1, 2)
    token_pieces = head_pieces(tokens)
    tail = jnp.concatenate([tokens[p, :, count - EDGE :] for p in range(packs)], axis=1)
    tail = jnp.pad(tail, ((0, 0), (0, LANES - packs * EDGE)))
    edge_pieces = head_pieces(shift(tail, "seq", 1))
    extra = jnp.concatenate(
        [conv_bc.T, bias_bc[:, None], norm_gain.reshape(-1, bc_part).T], axis=1
    )
    extra = jnp.pad(extra, ((0, 0), (0, LANES - extra.shape[1])))
    weight_pieces = head_pieces(jnp.concatenate([proj_bc.T, extra], axis=1))
    conv_own = jnp.pad(
        jnp.concatenate([conv_x, bias_x[None]], axis=0).astype(f32), ((0, 7 - width), (0, 0))
    )
    conv_bc_own = jnp.pad(
        jnp.concatenate([conv_bc, bias_bc[None]], axis=0).astype(f32), ((0, 7 - width), (0, 0))
    )
    w_dt = jnp.pad(proj_dt, ((0, 0), (0, LANES - heads)))
    small = jnp.pad(jnp.stack([dt_bias, a_log]).astype(f32), ((0, 6), (0, LANES - heads)))
    skip = jnp.repeat(d_skip.astype(f32), size)[None]
    gain_gate = gate_gain.astype(f32)[None]

    lane_spec = pack_spec((count, LANES))
    chan_spec = pack_spec((count, inner))
    xbc_spec = pack_spec((count, chans))
    model_spec = pack_spec((features, count))
    piece_spec = pack_spec((part, count))
    edge_spec = whole_spec((part, LANES))
    pay_shape = (rows + EDGE, LANES)
    pay_specs = [side_spec(pay_shape, half, k) for k in (True, False)]
    pay = shape(half, *pay_shape, jnp.int16)
    state_spec = half_spec(pay_shape, half)
    vec = whole_spec((1, inner))
    square = whole_spec((features, inner))

    (
        normed, inv, edge, edge_inv, gate, raw_x, raw_bc, xbc, slope_x, slope_bc, dt, sig, cum,
        keep, send,
    ) = call(
        functools.partial(front_kernel, dims),
        grid,
        [piece_spec] * 4
        + [edge_spec] * 4
        + [whole_spec((bc_part, features + LANES))] * 4
        + [square, square, whole_spec((LANES, features)), whole_spec((8, inner)),
           whole_spec((8, LANES))],
        [
            model_spec, pack_spec((1, count)), whole_spec((features, LANES)),
            whole_spec((1, LANES)), chan_spec, pack_spec((ext, inner)), pack_spec((ext, bc_part)),
            xbc_spec, chan_spec, pack_spec((count, bc_part)), lane_spec, lane_spec, lane_spec,
            *pay_specs,
        ],
        [
            shape(packs, features, count, bf16), shape(packs, 1, count, f32),
            shape(features, LANES, bf16), shape(1, LANES, f32), shape(packs, count, inner, bf16),
            shape(packs, ext, inner, bf16), shape(packs, ext, bc_part, bf16),
            shape(packs, count, chans, bf16), shape(packs, count, inner, f32),
            shape(packs, count, bc_part, f32), shape(packs, count, LANES, f32),
            shape(packs, count, LANES, f32), shape(packs, count, LANES, f32), pay, pay,
        ],
        [
            pltpu.VMEM((4, part, count), bf16), pltpu.VMEM((4, part, LANES), bf16),
            pltpu.VMEM((4, bc_part, features + LANES), bf16), pltpu.VMEM((ext, chans), f32),
            pltpu.VMEM((LANES, chans), f32), pltpu.VMEM((8, chans), f32),
            pltpu.VMEM((features, 1), f32),
        ],
        (2 * packs * ext * features * (inner * 2 + bc + LANES), 12 << 20),
        pre,
        *token_pieces, *edge_pieces, *weight_pieces, proj_z, proj_x, w_dt.T, conv_own, small,
    )

    inner_out, cot, gg = call(
        functools.partial(inner_kernel, dims),
        grid,
        [xbc_spec, lane_spec, lane_spec] + [piece_spec] * 4 + [whole_spec((inner, features))],
        [chan_spec, model_spec, chan_spec],
        [
            shape(packs, count, inner, f32), shape(packs, features, count, bf16),
            shape(packs, count, inner, f32),
        ],
        [pltpu.VMEM((4, part, count), bf16)],
        (2 * packs * count * (features * inner + heads * count * 256), 16 << 20),
        pre,
        xbc, dt, cum, *head_pieces(cotangent), proj_out,
    )

    state_keep, state_recv = scan_states(keep, send, meta, packs, heads, size, 0)

    y, mixed, stats = call(
        functools.partial(gate_kernel, dims),
        grid,
        [
            xbc_spec, lane_spec, chan_spec, state_spec, state_spec, chan_spec, chan_spec, vec, vec,
        ],
        [chan_spec, chan_spec, pack_spec((2, count))],
        [
            shape(packs, count, inner, f32), shape(packs, count, inner, f32),
            shape(packs, 2, count, f32),
        ],
        [],
        (2 * packs * count * inner * LANES, 12 << 20),
        pre,
        xbc, cum, inner_out, state_keep, state_recv, gate, gg, gain_gate, skip,
    )
    stats_all = lax.all_gather(stats, "head")

    gy, ey, el, gated, ggate, gkeep, gsend, gate_small = call(
        functools.partial(grad_kernel, dims, total_inner),
        grid,
        [
            pl.BlockSpec((4, 1, 2, count), lambda p, *_: (0, p, 0, 0)),
            xbc_spec, lane_spec, chan_spec, chan_spec, chan_spec, chan_spec, vec, vec,
        ],
        [chan_spec] * 5 + pay_specs + [whole_spec((8, inner))],
        [shape(packs, count, inner, f32)] + [shape(packs, count, inner, bf16)] * 4
        + [pay, pay, shape(8, inner, f32)],
        [],
        (2 * packs * count * inner * LANES, 16 << 20),
        pre,
        stats_all, xbc, cum, y, mixed, gate, gg, gain_gate, skip,
    )

    dx, dbc = call(
        functools.partial(diag_kernel, dims),
        grid,
        [xbc_spec, lane_spec, lane_spec, chan_spec, chan_spec, chan_spec, state_spec, state_spec],
        [chan_spec, pack_spec((count, bc))],
        [shape(packs, count, inner, f32), shape(packs, count, bc, f32)],
        [],
        (4 * packs * count * heads * count * 256, 12 << 20),
        pre,
        xbc, dt, cum, gy, ey, el, state_keep, state_recv,
    )

    def scatter_shapes(n):
        return (
            [piece_spec, piece_spec,
             pl.BlockSpec((2, 1, part, count), lambda p, *_: (0, p, 0, 0))],
            [shape(n, part, count, f32), shape(n, part, count, f32),
             shape(2, n, part, count, bf16)],
        )

    specs, shapes = scatter_shapes(packs)
    out_own, out_far, out_send, terms, grads_zo = call(
        functools.partial(side_kernel, dims),
        grid,
        [chan_spec, model_spec, whole_spec((inner, features)), model_spec, chan_spec, square],
        specs + [model_spec, whole_spec((2 * features, inner))],
        shapes + [shape(packs, features, count, f32), shape(2 * features, inner, bf16)],
        [pltpu.VMEM((4, part, count), f32), pltpu.VMEM((2 * features, inner), f32)],
        (8 * packs * count * features * inner, 20 << 20),
        pre,
        gated, cot, proj_out, normed, ggate, proj_z,
    )

    def to_far(far, near):
        return swap((far + near[1].astype(f32)).astype(bf16), "head", 2)

    near = swap(out_send, "head", 1)
    block_out = tokens.astype(f32) + out_own + near[0].astype(f32) + to_far(out_far, near).astype(f32)
    block_out = jnp.swapaxes(block_out.astype(bf16), 1, 2)

    gstate_keep, gstate_recv = scan_states(gkeep, gsend, meta, packs, heads, size, 1)

    share_own, share_near = call(
        functools.partial(share_kernel, dims),
        grid,
        [xbc_spec, lane_spec, lane_spec, pack_spec((count, bc)), state_spec, state_spec],
        [lane_spec, lane_spec],
        [shape(packs, count, LANES, f32)] * 2,
        [],
        (6 * packs * count * inner * LANES, 6 << 20),
        pre,
        xbc, dt, cum, dbc, gstate_keep, gstate_recv,
    )
    two = shape(half, count, LANES, f32)
    bc_keep, bc_send = call(
        functools.partial(middle_kernel, (packs, bc_part)),
        (1,),
        [whole_spec((packs, count, LANES))] * 2,
        [whole_spec(two.shape)] * 2,
        [two, two],
        [],
        (1 << 20, 2 << 20),
        (meta,),
        share_own, swap(share_near, "head", 1),
    )
    bc_recv = swap(bc_send, "head", 2)

    terms, edge_x, grads_x, grad_conv, grad_small, grad_dt = call(
        functools.partial(xback_kernel, dims),
        grid,
        [
            xbc_spec, lane_spec, lane_spec, lane_spec, chan_spec, chan_spec, chan_spec,
            state_spec, state_spec, state_spec, state_spec, chan_spec, pack_spec((ext, inner)),
            model_spec, whole_spec((features, LANES)), model_spec, square,
            whole_spec((features, LANES)), whole_spec((8, inner)), whole_spec((8, LANES)), vec,
        ],
        [
            model_spec, whole_spec((LANES, inner)), square, whole_spec((8, inner)),
            whole_spec((8, LANES)), whole_spec((8, features)),
        ],
        [
            shape(packs, features, count, f32), shape(LANES, inner, bf16),
            shape(features, inner, bf16), shape(8, inner, f32), shape(8, LANES, f32),
            shape(8, features, f32),
        ],
        [
            pltpu.VMEM((ext + EDGE, inner), f32), pltpu.VMEM((ext, inner), f32),
            pltpu.VMEM((features, inner), f32), pltpu.VMEM((features, LANES), f32),
        ],
        (4 * packs * ext * features * inner, 24 << 20),
        pre,
        xbc, dt, sig, cum, gy, y, dx, state_keep, state_recv, gstate_keep, gstate_recv, slope_x,
        raw_x, normed, edge, terms, proj_x, w_dt, conv_own, small, skip,
    )

    def late(spec_shape):
        return pl.BlockSpec(
            (1,) + spec_shape,
            lambda p, *_: (jnp.minimum(p, packs - 1),) + (0,) * len(spec_shape),
        )

    def late_half(spec_shape):
        return pl.BlockSpec(
            (1,) + spec_shape,
            lambda p, *_: (jnp.minimum(p, packs - 1) % half,) + (0,) * len(spec_shape),
        )

    specs, shapes = scatter_shapes(packs + 1)
    gn_own, gn_far, gn_send, dots, grads_bc, grad_conv_bc = call(
        functools.partial(bcback_kernel, dims),
        (packs + 1,),
        [
            late_half((count, LANES)), late_half((count, LANES)), late((count, bc_part)),
            late((ext, bc_part)), late((features, count)), whole_spec((features, LANES)),
            late((features, count)), whole_spec((features, bc_part)), square,
            whole_spec((LANES, inner)), whole_spec((8, bc_part)),
        ],
        specs + [
            pack_spec((1, count)), whole_spec((2 * bc_part, inner)), whole_spec((8, bc_part)),
        ],
        shapes + [
            shape(packs + 1, 1, count, f32), shape(2 * bc_part, inner, bf16),
            shape(8, bc_part, f32),
        ],
        [
            pltpu.VMEM((4, part, count), f32), pltpu.VMEM((ext + EDGE, bc_part), f32),
            pltpu.VMEM((ext, bc_part), f32), pltpu.VMEM((features, bc_part), f32),
            pltpu.VMEM((LANES, bc_part), bf16),
        ],
        (4 * packs * ext * features * bc_part, 20 << 20),
        pre,
        bc_keep, bc_recv, slope_bc, raw_bc, normed, edge, terms, proj_bc, proj_x, edge_x,
        conv_bc_own,
    )

    near = swap(gn_send, "head", 1)
    far = to_far(gn_far, near)
    dots_all = lax.all_gather(dots, "head")
    in_grad, edge_grad, grad_gain = call(
        functools.partial(final_kernel, (packs, count, features)),
        (packs + 1,),
        [
            piece_spec, pl.BlockSpec((1, 1, part, count), lambda p, *_: (0, p, 0, 0)), piece_spec,
            pl.BlockSpec((4, 1, 1, count), lambda p, *_: (0, p, 0, 0)), late((part, count)),
            edge_spec, late((1, count)), whole_spec((1, LANES)), whole_spec((part, 1)),
            late((part, count)),
        ],
        [late((part, count)), edge_spec, edge_spec],
        [shape(packs, part, count, f32), shape(part, LANES, f32), shape(part, LANES, f32)],
        [],
        (1 << 20, 6 << 20),
        (meta,),
        gn_own, near, far, dots_all, tokens, edge_pieces[0], inv, edge_inv,
        norm_gain.astype(f32)[:, None], cotangent,
    )
    from_next = shift(edge_grad, "seq", -1)[:, : packs * EDGE]
    from_next = from_next.reshape(part, packs, EDGE).transpose(1, 0, 2)
    in_grad = in_grad + jnp.pad(from_next, ((0, 0), (0, 0), (count - EDGE, 0)))
    in_grad = jnp.swapaxes(in_grad, 1, 2)

    cost = (1 << 20, 4 << 20)
    grads_zo = reduce_over_seq(grads_zo, cost)
    grads_x = reduce_over_seq(grads_x, cost)
    grads_bc = reduce_over_seq(grads_bc, cost)
    grad_bc = jnp.concatenate([grads_bc[:bc_part], grads_bc[bc_part:]], axis=1)
    smalls = [
        grad_gain[:, 0], grad_dt[:heads], grad_conv[: width + 1], grad_conv_bc[: width + 1],
        gate_small[0:2], grad_small[0:2],
    ]
    flat = jnp.concatenate([v.reshape(-1) for v in smalls])
    flat = jnp.pad(flat, (0, -flat.shape[0] % (8 * LANES))).reshape(-1, LANES)
    bit = 1
    while bit < lax.axis_size("seq"):
        flat = flat + swap(flat, "seq", bit)
        bit *= 2
    flat = flat.reshape(-1)
    sums, start = [], 0
    for v in smalls:
        sums.append(flat[start : start + v.size].reshape(v.shape))
        start += v.size
    grad_gain, grad_dt, grad_conv, grad_conv_bc, gate_small, grad_small = sums
    return (
        block_out,
        in_grad,
        grad_gain,
        grads_zo[:features].astype(f32),
        grads_x.astype(f32),
        grad_bc.T.astype(f32),
        grad_dt.T,
        grad_conv[:width],
        grad_conv_bc[:width],
        grad_conv[width],
        grad_conv_bc[width],
        grad_small[0, :heads],
        grad_small[1, :heads],
        jnp.sum(gate_small[1].reshape(heads, size), axis=1),
        gate_small[0],
        grads_zo[features:].astype(f32).T,
    )


def solution(mesh):
    token, column, vector = P(None, "seq", "head"), P(None, "head"), P("head")
    row = P("head", None)
    return jax.shard_map(
        shards,
        mesh=mesh,
        in_specs=(
            token, token, P(), vector, column, column, column, column, column, column, vector,
            vector, vector, vector, vector, vector, row,
        ),
        out_specs=(
            token, token, vector, column, column, column, column, column, column, vector, vector,
            vector, vector, vector, vector, row,
        ),
        check_vma=False,
    )
```

time: 692 us -> 348 us (0.50); the launches traced: 682 us -> 345 us
  waiting for transfers between devices: 321 us -> 97.8 us
  Pallas kernels: 0 us -> 121 us
  other arithmetic: 95.4 us -> 15.5 us
  matrix products: 79.6 us -> 0 us
  blocking collectives: 96.7 us -> 35.5 us
  starting transfers between devices: 4.99 us -> 46.4 us
  local copies, waits for them, and re-layouts: 67.1 us -> 28 us
  between operations: 17.1 us -> 1.19 us
    psum x2 -> x0, waiting for transfers between devices: 173 us -> none  [the longest x1 105 us: shards(): lax.psum((grad_norm_gain, grad_proj_z, grad_proj_x, grad_proj_bc, grad_pr...]
    all_gather x4 -> x0, waiting for transfers between devices: 145 us -> none  [the longest x2 139 us: entering(): everything = jax.tree.map(lambda part: lax.all_gather(part, axis), x)]
    pallas_call x0 -> x20, Pallas kernels: none -> 121 us  [call(): pl.pallas_call(kernel, grid_spec=pltpu.PrefetchScalarGridSpec(num_scalar_...]
    dot_general x21 -> x0, matrix products: 79.6 us -> none  [the longest x3 28.9 us: ssd_block_output(): jnp.einsum('ktsh,kshp->kthp', scores[..., None] * decay_mat, scaled, prec...]
    psum x3 -> x0, blocking collectives: 54.3 us -> none  [the longest x1 40.6 us: shards(): lax.psum((grad_norm_gain, grad_proj_z, grad_proj_x, grad_proj_bc, grad_pr...]
    ppermute x2 -> x31, waiting for transfers between devices: 2.9 us -> 56.3 us  [the longest x29 56.3 us: swap(): lax.ppermute(x, axis, [(i, i ^ bit) for i in range(lax.axis_size(axis))])]
    all_to_all x0 -> x4, waiting for transfers between devices: none -> 41.6 us  [the longest x2 37.4 us: reduce_over_seq(): pieces = lax.all_to_all(parts.reshape(n, rows // n, cols), 'seq', 0, 0)]
    reduce_sum x13 -> x1, other arithmetic: 35.6 us -> 0.63 us  [shards(): jnp.sum(gate_small[1].reshape(heads, size), axis=1)]
  transfers between devices with their start and end apart: 10 -> 35, of which waited for: 6 -> 16; matrix products, arithmetic and copies ran while one was open for 21% -> 9% of each run, Pallas kernels for 0% -> 23%
where the time goes in v1:
time: 348 us; the launch traced here: 345 us
  Pallas kernels  121 us (35%)
  waiting for transfers between devices  97.8 us (28%)
  starting transfers between devices  46.4 us (13%)
  blocking collectives  35.5 us (10%)
  local copies, waits for them, and re-layouts  28 us (8%)
  other arithmetic  15.5 us (4%)
    pallas_call x20, Pallas kernels, call(): pl.pallas_call(kernel, grid_spec=pltpu.PrefetchScalarGridSpec(num_scalar_...  121 us
    ppermute x29, waiting for transfers between devices, swap(): lax.ppermute(x, axis, [(i, i ^ bit) for i in range(lax.axis_size(axis))])  56.3 us
    all_to_all x2, waiting for transfers between devices, reduce_over_seq(): pieces = lax.all_to_all(parts.reshape(n, rows // n, cols), 'seq', 0, 0)  37.4 us
    ppermute x29, starting transfers between devices, swap(): lax.ppermute(x, axis, [(i, i ^ bit) for i in range(lax.axis_size(axis))])  27 us
    all_to_all x1, blocking collectives, reduce_over_seq(): pieces = lax.all_to_all(parts.reshape(n, rows // n, cols), 'seq', 0, 0)  12.9 us
    unnamed x92, local copies, waits for them, and re-layouts  11.8 us
    all_to_all x1, blocking collectives, reduce_over_seq(): return lax.all_to_all(shares, 'seq', 0, 0).reshape(rows, cols)  10.7 us
    all_to_all x2, starting transfers between devices, reduce_over_seq(): pieces = lax.all_to_all(parts.reshape(n, rows // n, cols), 'seq', 0, 0)  7.32 us
  transfers between devices with their start and end apart: 35, of which 16 were waited for; matrix products, arithmetic and copies ran while one was open for 9% of the time, Pallas kernels for 23%

profile of v1, /device:TPU:0, one launch (start us, length us, event | category | flops | bytes accessed | tf_op | source)
XLA Modules:
  0.0 345.3 jit_solution(5064272738256554461)
XLA Ops:
  25.3 15.0 %shard_map.288 = (bf16[4,768,256]{2,1,0:T(8,128)(2,1)}, f32[4,1,256]{2,1,0:T(1,128)}, bf16[768,128]{1,0:T(8,128)(2,1)}, f32[1,128]{1,0:T(1,128)}, bf16[4,256,384...) custom-call(s32[2]{0:T(128)} %pad_add_fusion.meta, ...), custom_call_target="tpu_custom_call" | custom-call | flops 1925185536 | bytes 12582912 | tf_op jit(solution)/shard_map/pallas_call | solution.py:713
  41.9 5.9 %collective-permute-done.13.other.refs_1_ = s16[2,400,128]{2,1,0:T(8,128)(2,1)S(1)} collective-permute-done((s16[2,400,128]{2,1,0:T(8,128)(2,1)}, s16[2,400,128]{2,1,0:T(8,128)(2,1)S(1)}, u32[]{:S(2)}, u32[]{:S(2)}) %collective-permute-start.13) | collective-permute-done | bytes 204832 | tf_op jit(solution)/shard_map/ppermute | solution.py:22
  53.4 4.5 %collective-permute-done.14.refs_1_ = s16[2,400,128]{2,1,0:T(8,128)(2,1)S(1)} collective-permute-done((s16[2,400,128]{2,1,0:T(8,128)(2,1)}, s16[2,400,128]{2,1,0:T(8,128)(2,1)S(1)}, u32[]{:S(2)}, u32[]{:S(2)}) %collective-permute-start.14) | collective-permute-done | bytes 204832 | tf_op jit(solution)/shard_map/ppermute | solution.py:22
  64.1 8.4 %collective-permute-done.15.refs_2_ = s16[2,400,128]{2,1,0:T(8,128)(2,1)S(1)} collective-permute-done((s16[2,400,128]{2,1,0:T(8,128)(2,1)}, s16[2,400,128]{2,1,0:T(8,128)(2,1)S(1)}, u32[]{:S(2)}, u32[]{:S(2)}) %collective-permute-start.15) | collective-permute-done | bytes 204832 | tf_op jit(solution)/shard_map/ppermute | solution.py:22
  80.0 7.1 %shard_map.289 = (f32[4,256,384]{2,1,0:T(8,128)}, bf16[4,768,256]{2,1,0:T(8,128)(2,1)}, f32[4,256,384]{2,1,0:T(8,128)}) custom-call(s32[2]{0:T(128)} %pad_add_fusion.meta, s32[4,4]{1,0:T(4,128)} %lens.17, bf16[4,256,640]{2,1,0:T(8,128)(2,1)} %get-tuple-element.79.refs_0_.refs_1_, f32[4,256,128]{2,1,0:T(8,128)} %get-tuple-element.81.refs_1_, ...), custom_call_target="tpu_custom_call" | custom-call | flops 1409286144 | bytes 16777216 | tf_op jit(solution)/shard_map/pallas_call | solution.py:713
  87.8 6.9 %shard_map.293 = (f32[4,256,384]{2,1,0:T(8,128)}, f32[4,256,384]{2,1,0:T(8,128)}, f32[4,2,256]{2,1,0:T(2,128)}) custom-call(s32[2]{0:T(128)} %pad_add_fusion.meta, s32[4,4]{1,0:T(4,128)} %lens.17, bf16[4,256,640]{2,1,0:T(8,128)(2,1)} %get-tuple-element.79.refs_0_.refs_1_, f32[4,256,128]{2,1,0:T(8,128)} %get-tuple-element.80.refs_2_.refs_1_.refs_3_, ...), custom_call_target="tpu_custom_call" | custom-call | flops 100663296 | bytes 12582912 | tf_op jit(solution)/shard_map/pallas_call | solution.py:713
  94.7 6.0 %all-gather = f32[16,2,256]{2,1,0:T(2,128)} all-gather(f32[4,2,256]{2,1,0:T(2,128)} %get-tuple-element.91), channel_id=2, replica_groups=mesh['seq'=8,'head'=4] {'head'}, dimensions={0}, use_global_device_ids=true | all-gather | bytes 40960 | tf_op jit(solution)/shard_map/all_gather | solution.py:900
  100.7 8.8 %shard_map.294 = (f32[4,256,384]{2,1,0:T(8,128)}, bf16[4,256,384]{2,1,0:T(8,128)(2,1)}, bf16[4,256,384]{2,1,0:T(8,128)(2,1)}, bf16[4,256,384]{2,1,0:T(8,128)(2,1...) custom-call(s32[2]{0:T(128)} %pad_add_fusion.meta, ...), custom_call_target="tpu_custom_call" | custom-call | flops 100663296 | bytes 16777216 | tf_op jit(solution)/shard_map/pallas_call | solution.py:713
  110.1 7.0 %collective-permute-done.19.other.refs_1_ = s16[2,400,128]{2,1,0:T(8,128)(2,1)S(1)} collective-permute-done((s16[2,400,128]{2,1,0:T(8,128)(2,1)}, s16[2,400,128]{2,1,0:T(8,128)(2,1)S(1)}, u32[]{:S(2)}, u32[]{:S(2)}) %collective-permute-start.19) | collective-permute-done | bytes 204832 | tf_op jit(solution)/shard_map/ppermute | solution.py:22
  121.3 5.9 %collective-permute-done.20.refs_1_ = s16[2,400,128]{2,1,0:T(8,128)(2,1)S(1)} collective-permute-done((s16[2,400,128]{2,1,0:T(8,128)(2,1)}, s16[2,400,128]{2,1,0:T(8,128)(2,1)S(1)}, u32[]{:S(2)}, u32[]{:S(2)}) %collective-permute-start.20) | collective-permute-done | bytes 204832 | tf_op jit(solution)/shard_map/ppermute | solution.py:22
  133.2 8.8 %collective-permute-done.21.refs_2_ = s16[2,400,128]{2,1,0:T(8,128)(2,1)S(1)} collective-permute-done((s16[2,400,128]{2,1,0:T(8,128)(2,1)}, s16[2,400,128]{2,1,0:T(8,128)(2,1)S(1)}, u32[]{:S(2)}, u32[]{:S(2)}) %collective-permute-start.21) | collective-permute-done | bytes 204832 | tf_op jit(solution)/shard_map/ppermute | solution.py:22
  146.5 9.9 %shard_map.296 = (f32[4,256,384]{2,1,0:T(8,128)}, f32[4,256,256]{2,1,0:T(8,128)}) custom-call(s32[2]{0:T(128)} %pad_add_fusion.meta, s32[4,4]{1,0:T(4,128)} %lens.17, bf16[4,256,640]{2,1,0:T(8,128)(2,1)} %get-tuple-element.79.refs_0_.refs_1_, f32[4,256,128]{2,1,0:T(8,128)} %get-tuple-element.81.refs_1_, ...), custom_call_target="tpu_custom_call" | custom-call | flops 1610612736 | bytes 12582912 | tf_op jit(solution)/shard_map/pallas_call | solution.py:713
  157.0 6.2 %shard_map.300 = (f32[4,256,128]{2,1,0:T(8,128)}, f32[4,256,128]{2,1,0:T(8,128)}) custom-call(s32[2]{0:T(128)} %pad_add_fusion.meta, s32[4,4]{1,0:T(4,128)} %lens.17, bf16[4,256,640]{2,1,0:T(8,128)(2,1)} %get-tuple-element.79.refs_0_.refs_1_, f32[4,256,128]{2,1,0:T(8,128)} %get-tuple-element.81.refs_1_, ...), custom_call_target="tpu_custom_call" | custom-call | flops 301989888 | bytes 6291456 | tf_op jit(solution)/shard_map/pallas_call | solution.py:713
  170.2 9.8 %shard_map.295 = (f32[4,192,256]{2,1,0:T(8,128)}, f32[4,192,256]{2,1,0:T(8,128)}, bf16[2,4,192,256]{3,2,1,0:T(8,128)(2,1)}, f32[4,768,256]{2,1,0:T(8,128)}, bf16[1536,384]{1,0:T(8,128)(2,1)}) custom-call(s32[2]{0:T(128)} %pad_add_fusion.meta, s32[4,4]{1,0:T(4,128)} %lens.17, bf16[4,256,384]{2,1,0:T(8,128)(2,1)} %get-tuple-element.94.refs_0_, ...), custom_call_target="tpu_custom_call" | custom-call | flops 2415919104 | bytes 20971520 | tf_op jit(solution)/shard_map/pallas_call | solution.py:713
  180.0 16.4 %shard_map.302 = (f32[4,768,256]{2,1,0:T(8,128)}, bf16[128,384]{1,0:T(8,128)(2,1)}, bf16[768,384]{1,0:T(8,128)(2,1)}, f32[8,384]{1,0:T(8,128)}, f32[8,128]{1,0:T(8,128)}, /*index=5*/f32[8,768]{1,0:T(8,128)}) custom-call(s32[2]{0:T(128)} %pad_add_fusion.meta, s32[4,4]{1,0:T(4,128)} %lens.17, bf16[4,256,640]{2,1,0:T(8,128)(2,1)} %get-tuple-element.79.refs_0_.refs_1_, ...), custom_call_target="tpu_custom_call" | custom-call | flops 1283457024 | bytes 25165824 | tf_op jit(solution)/shard_map/pallas_call | solution.py:713
  197.1 8.4 %shard_map.303 = (f32[5,192,256]{2,1,0:T(8,128)}, f32[5,192,256]{2,1,0:T(8,128)}, bf16[2,5,192,256]{3,2,1,0:T(8,128)(2,1)}, f32[5,1,256]{2,1,0:T(1,128)}, bf16[128,384]{1,0:T(8,128)(2,1)}, /*index=5*/f32[8,64]{1,0:T(8,128)}) custom-call(s32[2]{0:T(128)} %pad_add_fusion.meta, s32[4,4]{1,0:T(4,128)} %lens.17, f32[2,256,128]{2,1,0:T(8,128)} %get-tuple-element.113.refs_0_, ...), custom_call_target="tpu_custom_call" | custom-call | flops 213909504 | bytes 20971520 | tf_op jit(solution)/shard_map/pallas_call | solution.py:713
  205.5 12.9 %all_to_all.30.parts = bf16[8,16,384]{2,1,0:T(8,128)(2,1)} all-to-all(bf16[8,16,384]{2,1,0:T(8,128)(2,1)} %bitcast.105), channel_id=1, replica_groups=mesh['seq'=8,'head'=4] {'seq'}, dimensions={0} | all-to-all | bytes 196608 | tf_op jit(solution)/shard_map/all_to_all | solution.py:767
  223.7 13.1 %all-to-all-done.2.parts = bf16[8,96,384]{2,1,0:T(8,128)(2,1)S(1)} async-done(((bf16[8,96,384]{2,1,0:T(8,128)(2,1)}), bf16[8,96,384]{2,1,0:T(8,128)(2,1)S(1)}, u32[]{:S(2)}, u32[]{:S(2)}) %all-to-all-start.2) | async-done | bytes 589856 | tf_op jit(solution)/shard_map/all_to_all | solution.py:767
  236.8 10.7 %all_to_all.31 = bf16[8,16,384]{2,1,0:T(8,128)(2,1)S(1)} all-to-all(bf16[8,16,384]{2,1,0:T(8,128)(2,1)} %shard_map.307), channel_id=1, replica_groups=mesh['seq'=8,'head'=4] {'seq'}, dimensions={0} | all-to-all | bytes 196608 | tf_op jit(solution)/shard_map/all_to_all | solution.py:770
  253.6 24.4 %all-to-all-done.parts = bf16[8,192,384]{2,1,0:T(8,128)(2,1)S(1)} async-done(((bf16[8,192,384]{2,1,0:T(8,128)(2,1)}), bf16[8,192,384]{2,1,0:T(8,128)(2,1)S(1)}, u32[]{:S(2)}, u32[]{:S(2)}) %all-to-all-start) | async-done | bytes 1179680 | tf_op jit(solution)/shard_map/all_to_all | solution.py:767
  293.4 4.1 %all-to-all-done.3 = bf16[8,96,384]{2,1,0:T(8,128)(2,1)S(1)} async-done(((bf16[8,96,384]{2,1,0:T(8,128)(2,1)}), bf16[8,96,384]{2,1,0:T(8,128)(2,1)S(1)}, u32[]{:S(2)}, u32[]{:S(2)}) %all-to-all-start.3) | async-done | bytes 589856 | tf_op jit(solution)/shard_map/all_to_all | solution.py:770
  304.0 5.8 %all-gather.1 = f32[20,1,256]{2,1,0:T(1,128)} all-gather(f32[5,1,256]{2,1,0:T(1,128)} %get-tuple-element.128), channel_id=3, replica_groups=mesh['seq'=8,'head'=4] {'head'}, dimensions={0}, use_global_device_ids=true | all-gather | bytes 25600 | tf_op jit(solution)/shard_map/all_gather | solution.py:1055
  310.6 5.8 %shard_map.304 = (f32[4,192,256]{2,1,0:T(8,128)}, f32[192,128]{1,0:T(8,128)}, f32[192,128]{1,0:T(8,128)}) custom-call(s32[2]{0:T(128)} %pad_add_fusion.meta, f32[5,192,256]{2,1,0:T(8,128)} %get-tuple-element.125.refs_0_, bf16[2,5,192,256]{3,2,1,0:T(8,128)(2,1)} %copy-done.3, bf16[5,192,256]{2,1,0:T(8,128)(2,1)} %copy-done.11, f32[4,5,1,256]{3,2,1,0:T(1,128)} %bitcast.106, ...), custom_call_target="tpu_custom_call" | custom-call | flops 1048576 | bytes 6291456 | tf_op jit(solution)/shard_map/pallas_call | solution.py:713
  325.5 5.1 %collective-permute-done.29 = f32[64,128]{1,0:T(8,128)S(1)} collective-permute-done((f32[64,128]{1,0:T(8,128)S(1)}, f32[64,128]{1,0:T(8,128)S(1)}, u32[]{:S(2)}, u32[]{:S(2)}) %collective-permute-start.29) | collective-permute-done | bytes 32800 | tf_op jit(solution)/shard_map/ppermute | solution.py:22
  (218 shorter events, 127.3 us)
Async XLA Ops:
  0.7 23.1 %collective-permute-start = (bf16[4,192,256]{2,1,0:T(8,128)(2,1)}, bf16[4,192,256]{2,1,0:T(8,128)(2,1)S(1)}, u32[]{:S(2)}, u32[]{:S(2)}) collective-permute-start(bf16[4,192,256]{2,1,0:T(8,128)(2,1)} %bitcast.83), channel_id=1, source_target_pairs={{0,1},{1,0},{2,3},{3,2},{4,5},{5,4},{6,7},{7,6},{8,9},{9,8},{10,11... | collective-permute-start | bytes 1179656 | tf_op jit(solution)/shard_map/ppermute | solution.py:22
  1.2 12.8 %collective-permute-start.1 = (bf16[4,192,256]{2,1,0:T(8,128)(2,1)}, bf16[4,192,256]{2,1,0:T(8,128)(2,1)S(1)}, u32[]{:S(2)}, u32[]{:S(2)}) collective-permute-start(bf16[4,192,256]{2,1,0:T(8,128)(2,1)} %bitcast.84), channel_id=1, source_target_pairs={{0,2},{1,3},{2,0},{3,1},{4,6},{5,7},{6,4},{7,5},{8,10},{9,11},{10,... | collective-permute-start | bytes 1179656 | tf_op jit(solution)/shard_map/ppermute | solution.py:22
  6.3 15.6 %collective-permute-start.7 = (bf16[64,896]{1,0:T(8,128)(2,1)S(1)}, bf16[64,896]{1,0:T(8,128)(2,1)S(1)}, u32[]{:S(2)}, u32[]{:S(2)}) collective-permute-start(bf16[64,896]{1,0:T(8,128)(2,1)S(1)} %fusion.6.refs_8_), channel_id=1, source_target_pairs={{0,1},{1,0},{2,3},{3,2},{4,5},{5,4},{6,7},{7,6},{8,9},{9,8},{10,11... | collective-permute-start | bytes 344072 | tf_op jit(solution)/shard_map/ppermute | solution.py:22
  6.5 11.6 %collective-permute-start.8 = (bf16[64,896]{1,0:T(8,128)(2,1)S(1)}, bf16[64,896]{1,0:T(8,128)(2,1)S(1)}, u32[]{:S(2)}, u32[]{:S(2)}) collective-permute-start(bf16[64,896]{1,0:T(8,128)(2,1)S(1)} %fusion.6.refs_8_), channel_id=1, source_target_pairs={{0,2},{1,3},{2,0},{3,1},{4,6},{5,7},{6,4},{7,5},{8,10},{9,11},{10,... | collective-permute-start | bytes 344072 | tf_op jit(solution)/shard_map/ppermute | solution.py:22
  14.0 9.8 %collective-permute-start.2 = (bf16[4,192,256]{2,1,0:T(8,128)(2,1)S(1)}, bf16[4,192,256]{2,1,0:T(8,128)(2,1)S(1)}, u32[]{:S(2)}, u32[]{:S(2)}) collective-permute-start(bf16[4,192,256]{2,1,0:T(8,128)(2,1)S(1)} %collective-permute-done.1.refs_2_), channel_id=1, source_target_pairs={{0,1},{1,0},{2,3},{3,2},{4,5},{5,4},{6,7},{7,6},{8,9},{9,8},{10,11... | collective-permute-start | bytes 1179656 | tf_op jit(solution)/shard_map/ppermute | solution.py:22
  21.9 31.0 %collective-permute-start.11 = (bf16[4,192,256]{2,1,0:T(8,128)(2,1)S(1)}, bf16[4,192,256]{2,1,0:T(8,128)(2,1)S(1)}, u32[]{:S(2)}, u32[]{:S(2)}) collective-permute-start(bf16[4,192,256]{2,1,0:T(8,128)(2,1)S(1)} %bitcast.92), channel_id=1, source_target_pairs={{0,2},{1,3},{2,0},{3,1},{4,6},{5,7},{6,4},{7,5},{8,10},{9,11},{10,... | collective-permute-start | bytes 1179656 | tf_op jit(solution)/shard_map/ppermute | solution.py:22
  52.8 26.3 %collective-permute-start.10 = (bf16[4,192,256]{2,1,0:T(8,128)(2,1)S(1)}, bf16[4,192,256]{2,1,0:T(8,128)(2,1)S(1)}, u32[]{:S(2)}, u32[]{:S(2)}) collective-permute-start(bf16[4,192,256]{2,1,0:T(8,128)(2,1)S(1)} %bitcast.93), channel_id=1, source_target_pairs={{0,1},{1,0},{2,3},{3,2},{4,5},{5,4},{6,7},{7,6},{8,9},{9,8},{10,11... | collective-permute-start | bytes 1179656 | tf_op jit(solution)/shard_map/ppermute | solution.py:22
  52.8 26.3 %collective-permute-start.12 = (bf16[4,192,256]{2,1,0:T(8,128)(2,1)S(1)}, bf16[4,192,256]{2,1,0:T(8,128)(2,1)S(1)}, u32[]{:S(2)}, u32[]{:S(2)}) collective-permute-start(bf16[4,192,256]{2,1,0:T(8,128)(2,1)S(1)} %collective-permute-done.11.refs_5_), channel_id=1, source_target_pairs={{0,1},{1,0},{2,3},{3,2},{4,5},{5,4},{6,7},{7,6},{8,9},{9,8},{10,11... | collective-permute-start | bytes 1179656 | tf_op jit(solution)/shard_map/ppermute | solution.py:22
  61.5 11.0 %collective-permute-start.15 = (s16[2,400,128]{2,1,0:T(8,128)(2,1)}, s16[2,400,128]{2,1,0:T(8,128)(2,1)S(1)}, u32[]{:S(2)}, u32[]{:S(2)}) collective-permute-start(s16[2,400,128]{2,1,0:T(8,128)(2,1)} %get-tuple-element.85), channel_id=1, source_target_pairs={{0,16},{4,20},{8,24},{12,28},{16,0},{20,4},{24,8},{28,12},{1,17},{... | collective-permute-start | bytes 614408 | tf_op jit(solution)/shard_map/ppermute | solution.py:22
  76.4 10.8 %collective-permute-start.16 = (s16[2,400,128]{2,1,0:T(8,128)(2,1)}, s16[2,400,128]{2,1,0:T(8,128)(2,1)S(1)}, u32[]{:S(2)}, u32[]{:S(2)}) collective-permute-start(s16[2,400,128]{2,1,0:T(8,128)(2,1)} %get-tuple-element.88), channel_id=1, source_target_pairs={{0,4},{4,0},{8,12},{12,8},{16,20},{20,16},{24,28},{28,24},{1,5},{5... | collective-permute-start | bytes 614408 | tf_op jit(solution)/shard_map/ppermute | solution.py:22
  109.5 7.6 %collective-permute-start.19 = (s16[2,400,128]{2,1,0:T(8,128)(2,1)}, s16[2,400,128]{2,1,0:T(8,128)(2,1)S(1)}, u32[]{:S(2)}, u32[]{:S(2)}) collective-permute-start(s16[2,400,128]{2,1,0:T(8,128)(2,1)} %get-tuple-element.106), channel_id=1, source_target_pairs={{0,4},{4,0},{8,12},{12,8},{16,20},{20,16},{24,28},{28,24},{1,5},{5... | collective-permute-start | bytes 614408 | tf_op jit(solution)/shard_map/ppermute | solution.py:22
  130.9 11.1 %collective-permute-start.21 = (s16[2,400,128]{2,1,0:T(8,128)(2,1)}, s16[2,400,128]{2,1,0:T(8,128)(2,1)S(1)}, u32[]{:S(2)}, u32[]{:S(2)}) collective-permute-start(s16[2,400,128]{2,1,0:T(8,128)(2,1)} %get-tuple-element.107), channel_id=1, source_target_pairs={{0,16},{4,20},{8,24},{12,28},{16,0},{20,4},{24,8},{28,12},{1,17},{... | collective-permute-start | bytes 614408 | tf_op jit(solution)/shard_map/ppermute | solution.py:22
  145.9 10.4 %collective-permute-start.22 = (s16[2,400,128]{2,1,0:T(8,128)(2,1)}, s16[2,400,128]{2,1,0:T(8,128)(2,1)S(1)}, u32[]{:S(2)}, u32[]{:S(2)}) collective-permute-start(s16[2,400,128]{2,1,0:T(8,128)(2,1)} %get-tuple-element.110), channel_id=1, source_target_pairs={{0,4},{4,0},{8,12},{12,8},{16,20},{20,16},{24,28},{28,24},{1,5},{5... | collective-permute-start | bytes 614408 | tf_op jit(solution)/shard_map/ppermute | solution.py:22
  169.0 27.4 %collective-permute-start.24 = (f32[2,256,128]{2,1,0:T(8,128)}, f32[2,256,128]{2,1,0:T(8,128)S(1)}, u32[]{:S(2)}, u32[]{:S(2)}) collective-permute-start(f32[2,256,128]{2,1,0:T(8,128)} %get-tuple-element.114), channel_id=1, source_target_pairs={{0,2},{1,3},{2,0},{3,1},{4,6},{5,7},{6,4},{7,5},{8,10},{9,11},{10,... | collective-permute-start | bytes 786440 | tf_op jit(solution)/shard_map/ppermute | solution.py:22
  218.4 18.4 %all-to-all-start.2 = ((bf16[8,96,384]{2,1,0:T(8,128)(2,1)}), bf16[8,96,384]{2,1,0:T(8,128)(2,1)S(1)}, u32[]{:S(2)}, u32[]{:S(2)}) async-start(bf16[8,96,384]{2,1,0:T(8,128)(2,1)} %bitcast.31), calls=%async_computation.2 | async-start | bytes 1179648 | tf_op jit(solution)/shard_map/all_to_all | solution.py:767
  247.5 30.5 %all-to-all-start = ((bf16[8,192,384]{2,1,0:T(8,128)(2,1)}), bf16[8,192,384]{2,1,0:T(8,128)(2,1)S(1)}, u32[]{:S(2)}, u32[]{:S(2)}) async-start(bf16[8,192,384]{2,1,0:T(8,128)(2,1)} %bitcast.29), calls=%async_computation | async-start | bytes 2359296 | tf_op jit(solution)/shard_map/all_to_all | solution.py:767
  251.1 32.0 %collective-permute-start.17 = (bf16[2,4,192,256]{3,2,1,0:T(8,128)(2,1)}, bf16[2,4,192,256]{3,2,1,0:T(8,128)(2,1)}, u32[]{:S(2)}, u32[]{:S(2)}) collective-permute-start(bf16[2,4,192,256]{3,2,1,0:T(8,128)(2,1)} %get-tuple-element.99), channel_id=1, source_target_pairs={{0,1},{1,0},{2,3},{3,2},{4,5},{5,4},{6,7},{7,6},{8,9},{9,8},{10,11... | collective-permute-start | bytes 2359304 | tf_op jit(solution)/shard_map/ppermute | solution.py:22
  251.2 35.3 %collective-permute-start.25 = (bf16[2,5,192,256]{3,2,1,0:T(8,128)(2,1)}, bf16[2,5,192,256]{3,2,1,0:T(8,128)(2,1)S(1)}, u32[]{:S(2)}, u32[]{:S(2)}) collective-permute-start(bf16[2,5,192,256]{3,2,1,0:T(8,128)(2,1)} %get-tuple-element.126), channel_id=1, source_target_pairs={{0,1},{1,0},{2,3},{3,2},{4,5},{5,4},{6,7},{7,6},{8,9},{9,8},{10,11... | collective-permute-start | bytes 2949128 | tf_op jit(solution)/shard_map/ppermute | solution.py:22
  278.0 19.5 %all-to-all-start.3 = ((bf16[8,96,384]{2,1,0:T(8,128)(2,1)}), bf16[8,96,384]{2,1,0:T(8,128)(2,1)S(1)}, u32[]{:S(2)}, u32[]{:S(2)}) async-start(bf16[8,96,384]{2,1,0:T(8,128)(2,1)} %shard_map.306), calls=%async_computation.3 | async-start | bytes 1179648 | tf_op jit(solution)/shard_map/all_to_all | solution.py:770
  285.1 16.0 %collective-permute-start.18 = (bf16[4,192,256]{2,1,0:T(8,128)(2,1)}, bf16[4,192,256]{2,1,0:T(8,128)(2,1)}, u32[]{:S(2)}, u32[]{:S(2)}) collective-permute-start(bf16[4,192,256]{2,1,0:T(8,128)(2,1)} %fusion.1), channel_id=1, source_target_pairs={{0,2},{1,3},{2,0},{3,1},{4,6},{5,7},{6,4},{7,5},{8,10},{9,11},{10,... | collective-permute-start | bytes 1179656 | tf_op jit(solution)/shard_map/ppermute | solution.py:22
  289.0 20.8 %collective-permute-start.26 = (bf16[5,192,256]{2,1,0:T(8,128)(2,1)}, bf16[5,192,256]{2,1,0:T(8,128)(2,1)S(1)}, u32[]{:S(2)}, u32[]{:S(2)}) collective-permute-start(bf16[5,192,256]{2,1,0:T(8,128)(2,1)} %fusion), channel_id=1, source_target_pairs={{0,2},{1,3},{2,0},{3,1},{4,6},{5,7},{6,4},{7,5},{8,10},{9,11},{10,... | collective-permute-start | bytes 1474568 | tf_op jit(solution)/shard_map/ppermute | solution.py:22
  297.5 45.0 %all-to-all-start.1 = ((bf16[8,192,384]{2,1,0:T(8,128)(2,1)}), bf16[8,192,384]{2,1,0:T(8,128)(2,1)S(1)}, u32[]{:S(2)}, u32[]{:S(2)}) async-start(bf16[8,192,384]{2,1,0:T(8,128)(2,1)} %shard_map.305), calls=%async_computation.1 | async-start | bytes 2359296 | tf_op jit(solution)/shard_map/all_to_all | solution.py:770
  322.5 8.1 %collective-permute-start.29 = (f32[64,128]{1,0:T(8,128)S(1)}, f32[64,128]{1,0:T(8,128)S(1)}, u32[]{:S(2)}, u32[]{:S(2)}) collective-permute-start(f32[64,128]{1,0:T(8,128)S(1)} %fusion.29), channel_id=1, source_target_pairs={{0,8},{4,12},{8,0},{12,4},{16,24},{20,28},{24,16},{28,20},{1,9},{5... | collective-permute-start | bytes 98312 | tf_op jit(solution)/shard_map/ppermute | solution.py:22
  324.2 13.3 %collective-permute-start.27 = (f32[192,128]{1,0:T(8,128)}, f32[192,128]{1,0:T(8,128)S(1)}, u32[]{:S(2)}, u32[]{:S(2)}) collective-permute-start(f32[192,128]{1,0:T(8,128)} %get-tuple-element.132), channel_id=1, source_target_pairs={{4,0},{8,4},{12,8},{16,12},{20,16},{24,20},{28,24},{5,1},{9,5},{13... | collective-permute-start | bytes 294920 | tf_op jit(solution)/shard_map/ppermute | solution.py:27
  (56 other events, 486.7 us)

commit v2 on v1

v2 whole, which is shorter than its diff:
```python
import functools

import jax
import jax.numpy as jnp
from jax import lax
from jax.experimental import pallas as pl
from jax.experimental.pallas import tpu as pltpu
from jax.sharding import PartitionSpec as P

EPSILON = 1e-05
bf16 = jnp.bfloat16
f32 = jnp.float32
LANES = 128
EDGE = 16
MIB = 1024 * 1024
STEPS = 32000.0
UNIT = 16384.0
LN2 = 0.6931471805599453
GROUP = 16


def swap(x, axis, bit):
    return lax.ppermute(x, axis, [(i, i ^ bit) for i in range(lax.axis_size(axis))])


def shift(x, axis, distance):
    n = lax.axis_size(axis)
    return lax.ppermute(x, axis, [(i, i + distance) for i in range(n) if 0 <= i + distance < n])


def head_pieces(x):
    far = swap(x, "head", 2)
    near = swap(x, "head", 1)
    return x, near, far, swap(far, "head", 1)


def nn(a, b):
    return lax.dot_general(a, b, (((1,), (0,)), ((), ())), preferred_element_type=f32)


def nt(a, b):
    return lax.dot_general(a, b, (((1,), (1,)), ((), ())), preferred_element_type=f32)


def tn(a, b):
    return lax.dot_general(a, b, (((0,), (0,)), ((), ())), preferred_element_type=f32)


def split2(v):
    hi = v.astype(bf16)
    return hi, (v - hi.astype(f32)).astype(bf16)


def split3(v):
    hi = v.astype(bf16)
    rest = v - hi.astype(f32)
    mid = rest.astype(bf16)
    return hi, mid, (rest - mid.astype(f32)).astype(bf16)


def spread_matrix(heads, size):
    row = lax.broadcasted_iota(jnp.int32, (LANES, heads * size), 0)
    col = lax.broadcasted_iota(jnp.int32, (LANES, heads * size), 1)
    first = (col >= row * size) & (col < (row + 1) * size)
    again = (col >= (row - GROUP) * size) & (col < (row - GROUP + 1) * size)
    return jnp.where(first | again, 1.0, 0.0).astype(bf16)


def spread(v, matrix, heads):
    hi, lo = split2(head_lanes(v, heads))
    return nn((hi.astype(f32) + to_group(lo.astype(f32), 1)).astype(bf16), matrix)


def head_lanes(v, heads):
    return jnp.where(lax.broadcasted_iota(jnp.int32, v.shape, 1) < heads, v, 0.0)


def to_group(v, k):
    return pltpu.roll(v, k * GROUP, 1)


def from_group(v, k, heads):
    return head_lanes(pltpu.roll(v, LANES - k * GROUP, 1) if k else v, heads)


def collapse(v, matrix, heads):
    return head_lanes(nt(jnp.concatenate(split2(v), axis=1), jnp.concatenate([matrix] * 2, axis=1)), heads)


def triangle(count, lower):
    row = lax.broadcasted_iota(jnp.int32, (count, count), 0)
    col = lax.broadcasted_iota(jnp.int32, (count, count), 1)
    keep = (row >= col) if lower else (row <= col)
    return jnp.where(keep, 1.0, 0.0).astype(bf16)


def exact_sums(matrix, v, heads):
    hi, mid, lo = [piece.astype(f32) for piece in split3(v)]
    sums = nn(matrix, (hi + to_group(mid, 1) + to_group(lo, 2)).astype(bf16))
    return from_group(sums, 0, heads) + from_group(sums, 1, heads) + from_group(sums, 2, heads)


def step_sizes(v, heads):
    soft = jnp.maximum(v, 0.0) + jnp.log1p(jnp.exp(-jnp.abs(v)))
    return head_lanes(soft, heads)


def steps_of(block, heads):
    return step_sizes(block, heads), from_group(block, 1, heads)


def segments(positions, lens_ref, pack, count):
    total = jnp.zeros(positions.shape, jnp.int32)
    end = jnp.int32(0)
    for k in range(count):
        end = end + lens_ref[pack, k]
        total = total + jnp.where(positions >= end, 1, 0)
    return total


def column_segments(meta_ref, lens_ref, pack, count, nseq, before):
    rows = lax.broadcasted_iota(jnp.int32, (count + before, 1), 0)
    return segments(rows + (meta_ref[0] * count - before), lens_ref, pack, nseq)


def row_segments(meta_ref, lens_ref, pack, count, nseq):
    cols = lax.broadcasted_iota(jnp.int32, (1, count), 1)
    return segments(cols + meta_ref[0] * count, lens_ref, pack, nseq)


def carry_column(meta_ref, seg_ext, before):
    same = seg_ext[before:] == seg_ext[before - 1 : before]
    return jnp.where(same & (meta_ref[0] > 0), 1.0, 0.0)


def to_int16(v):
    return jnp.floor(v + 0.5).astype(jnp.int32).astype(jnp.int16)


def encode_state(out, p, state, decay, heads, size):
    lane = lax.broadcasted_iota(jnp.int32, (1, LANES), 1)
    powers = jnp.zeros((1, LANES), f32)
    for h in range(heads):
        part = state[h * size : (h + 1) * size]
        top = jnp.max(jnp.max(jnp.abs(part), axis=0, keepdims=True), axis=1, keepdims=True)
        power = jnp.ceil(jnp.log(jnp.maximum(top, 1e-30)) / LN2)
        powers = powers + jnp.where(lane == h, power, 0.0)
        codes = jnp.clip(part * (jnp.exp(-power * LN2) * STEPS), -32767.0, 32767.0)
        out[p, h * size : (h + 1) * size, :] = to_int16(codes)
    row = lax.broadcasted_iota(jnp.int32, (EDGE, LANES), 0)
    coarse = jnp.floor(decay * UNIT)
    fine = (decay * UNIT - coarse) * UNIT
    tail = jnp.where(row == 0, powers, jnp.where(row == 1, coarse, jnp.where(row == 2, fine, 0.0)))
    out[p, heads * size :, :] = to_int16(tail)


def decode_state(block, heads, size):
    values = block.astype(jnp.int32).astype(f32)
    tail = values[heads * size :]
    scale = jnp.exp(tail[0:1] * LN2) / STEPS
    decay = (tail[1:2] + tail[2:3] / UNIT) / UNIT
    return scaled_state(values[: heads * size], scale, heads, size), decay


def sigmoid(v):
    return 1.0 / (1.0 + jnp.exp(-v))


def scaled_state(state, decay, heads, size):
    return jnp.concatenate(
        [state[h * size : (h + 1) * size] * decay[:, h : h + 1] for h in range(heads)], axis=0
    )


def front_kernel(dims, meta, lens, *refs):
    packs, count, features, inner, bc, heads, size, width, nseq = dims
    tokens, edges, shared = refs[0:4], refs[4:8], refs[8:12]
    wx, wdt, conv_x, small = refs[12:16]
    normed_o, inv_o, edge_o, rawx_o, rawbc_o, xbc_o, steps_o, keep_o, send_o, gain_o = refs[16:26]
    stage, edge_stage, weights, raws, edge_raws, conv, gain = refs[26:]
    pack = pl.program_id(0)
    head = meta[1]
    part = features // 4
    wide = edge_stage.shape[2]

    def normalise(values):
        mean = jnp.sum(values * values, axis=0, keepdims=True) / features
        inv = lax.rsqrt(mean + EPSILON)
        return inv, ((values * inv) * gain[...]).astype(bf16)

    def raw_of(normed):
        wbc = weights[...].reshape(bc, weights.shape[2])[:, :features]
        return jnp.concatenate([nn(normed, wx[...]), nt(normed, wbc)], axis=1).astype(bf16)

    @pl.when(pack == 0)
    def _():
        for k in range(4):
            weights[head ^ k] = shared[k][...]
            edge_stage[head ^ k] = edges[k][...]
        extra = weights[...].reshape(bc, weights.shape[2])[:, features:].astype(f32)
        conv[:, :inner] = conv_x[...]
        conv[:, inner:] = jnp.transpose(extra)[0:8]
        bc_part = bc // 4
        pieces = part // bc_part
        for h in range(4):
            for c in range(pieces):
                gain[h * part + c * bc_part : h * part + (c + 1) * bc_part, :] = extra[
                    h * bc_part : (h + 1) * bc_part, width + 1 + c : width + 2 + c
                ]
        _, normed = normalise(edge_stage[...].reshape(features, wide).astype(f32))
        gain_o[...] = gain[...]
        edge_o[...] = normed
        edge_raws[...] = raw_of(jnp.transpose(normed)).astype(f32)

    for k in range(4):
        stage[head ^ k] = tokens[k][0]
    inv, normed_t = normalise(stage[...].reshape(features, count).astype(f32))
    inv_o[0] = inv
    normed_o[0] = normed_t
    normed = jnp.transpose(normed_t)
    raws[EDGE:, :] = raw_of(normed).astype(f32)
    raws[0:EDGE, :] = edge_raws[pl.ds(pl.multiple_of(pack * EDGE, EDGE), EDGE), :]

    def own_bc(values):
        bc_part = bc // 4
        parts = [values[:, inner + h * bc_part : inner + (h + 1) * bc_part] for h in range(4)]
        low = jnp.where((head & 1) == 0, parts[0], parts[1])
        high = jnp.where((head & 1) == 0, parts[2], parts[3])
        return jnp.where((head >> 1) == 0, low, high)

    rawx_o[0] = raws[:, :inner].astype(bf16)
    rawbc_o[0] = own_bc(raws[...]).astype(bf16)
    seg = column_segments(meta, lens, pack, count, nseq, EDGE)
    seg_main = seg[EDGE:]
    pre = convolved(raws, conv, seg, count, width)
    xbc = (pre * sigmoid(pre)).astype(bf16)
    xbc_o[0] = xbc
    v = head_lanes(nt(normed, wdt[...]).astype(bf16).astype(f32) + small[0:1, :], heads)
    dt = step_sizes(v, heads)
    rate = -dt * jnp.exp(small[1:2, :])
    cum = exact_sums(triangle(count, True), rate, heads)
    steps_o[0] = v + to_group(cum, 1)
    cum_end = cum[count - 1 : count]
    weight = jnp.where(seg_main == seg[count + EDGE - 1 :], jnp.exp(cum_end - cum), 0.0) * dt
    matrix = spread_matrix(heads, size)
    scaled = (xbc[:, :inner].astype(f32) * spread(weight, matrix, heads)).astype(bf16)
    state = tn(scaled, xbc[:, inner : inner + bc // 2])
    carry = carry_column(meta, seg, EDGE)
    store_state(
        meta, packs, pack, keep_o, send_o, state, carry[count - 1 :] * jnp.exp(cum_end), heads, size
    )


def convolved(raws, conv, seg, count, width):
    pre = jnp.broadcast_to(conv[width : width + 1, :], (count, raws.shape[1]))
    for k in range(width):
        low = EDGE - (width - 1) + k
        mask = jnp.where(seg[low : low + count] == seg[EDGE:], 1.0, 0.0)
        pre = pre + conv[k : k + 1, :] * raws[low : low + count, :] * mask
    return pre


def gate_slope_kernel(dims, meta, lens, *refs):
    packs, count, features, inner, bc, heads, size, width, nseq = dims
    normed, wz, raw_x, raw_bc, conv_x, conv_bc, gate_o, slope_x_o, slope_bc_o, raws, raws_bc = refs
    pack = pl.program_id(0)
    gate_o[0] = tn(normed[0], wz[...]).astype(bf16)
    seg = column_segments(meta, lens, pack, count, nseq, EDGE)
    for raw, wide, conv, out in ((raw_x, raws, conv_x, slope_x_o), (raw_bc, raws_bc, conv_bc, slope_bc_o)):
        wide[...] = raw[0].astype(f32)
        pre = convolved(wide, conv, seg, count, width)
        sig = sigmoid(pre)
        out[0] = sig * (1.0 + pre * (1.0 - sig))


def store_state(meta, packs, pack, keep_o, send_o, state, decay, heads, size):
    mine = (pack // (packs // 2)) == (meta[0] & 1)

    @pl.when(mine)
    def _():
        encode_state(keep_o, 0, state, decay, heads, size)

    @pl.when(jnp.logical_not(mine))
    def _():
        encode_state(send_o, 0, state, decay, heads, size)


def load_state(meta, packs, pack, keep, recv, heads, size):
    mine = (pack // (packs // 2)) == (meta[0] & 1)
    block = jnp.where(mine, keep[0].astype(jnp.int32), recv[0].astype(jnp.int32))
    return decode_state(block, heads, size)[0]


def decay_parts(cum_col, cum_row, masked):
    return masked * jnp.exp(jnp.minimum(cum_col - cum_row, 0.0))


def block_mask(meta, lens, pack, count, nseq):
    col = column_segments(meta, lens, pack, count, nseq, 0)
    row = row_segments(meta, lens, pack, count, nseq)
    tri = lax.broadcasted_iota(jnp.int32, (count, count), 0) >= lax.broadcasted_iota(
        jnp.int32, (count, count), 1
    )
    return tri & (col == row)


def inner_kernel(dims, meta, lens, *refs):
    packs, count, features, inner, bc, heads, size, width, nseq = dims
    xbc, steps, inner_o = refs
    pack = pl.program_id(0)
    half = bc // 2
    b_vals, c_vals = xbc[0, :, inner : inner + half], xbc[0, :, inner + half :]
    scores = jnp.where(block_mask(meta, lens, pack, count, nseq), nt(c_vals, b_vals), 0.0)
    dt, cum_col = steps_of(steps[0], heads)
    cum_row = jnp.transpose(cum_col)
    dt_row = jnp.transpose(dt)
    lane = lax.broadcasted_iota(jnp.int32, (count, 2 * size), 1)
    for pair in range(heads // 2):
        cols = slice(2 * pair * size, (2 * pair + 2) * size)
        x_pair = xbc[0, :, cols]
        parts = []
        for h in (2 * pair, 2 * pair + 1):
            weights = decay_parts(cum_col[:, h : h + 1], cum_row[h : h + 1], scores)
            parts.append(nn((weights * dt_row[h : h + 1]).astype(bf16), x_pair))
        inner_o[0, :, cols] = jnp.where(lane < size, parts[0], parts[1])


def cot_kernel(dims, meta, lens, *refs):
    packs, count, features, inner, bc, heads, size, width, nseq = dims
    pieces, (wout, cot_o, gg_o, stage) = refs[:4], refs[4:]
    for k in range(4):
        stage[meta[1] ^ k] = pieces[k][0]
    cotangent = stage[...].reshape(features, count)
    cot_o[0] = cotangent
    gg_o[0] = jnp.transpose(nn(wout[...], cotangent))


def compose(lower, upper, heads, size):
    return scaled_state(lower[0], upper[1], heads, size) + upper[0], lower[1] * upper[1]


def choose(flag, a, b):
    return jnp.where(flag, a[0], b[0]), jnp.where(flag, a[1], b[1])


def pair_kernel(dims, rev, meta, own, other, out):
    packs, heads, size = dims
    upper_is_own = ((meta[0] & 1) ^ rev) == 1
    for p in range(packs // 2):
        a, b = decode_state(own[p], heads, size), decode_state(other[p], heads, size)
        both = compose(choose(upper_is_own, b, a), choose(upper_is_own, a, b), heads, size)
        encode_state(out, p, *both, heads, size)


def entering_from(before, b, p, heads, size):
    if before is None:
        return (jnp.zeros_like(b[0]), jnp.ones_like(b[1])), b
    entering = decode_state(before[p], heads, size)
    return entering, compose(b, entering, heads, size)


def cube_kernel(dims, rev, bit, first, meta, *refs):
    packs, heads, size = dims
    total, other = refs[0], refs[1]
    before, next_o, before_o = (None, refs[2], refs[3]) if first else refs[2:5]
    upper_is_own = (((meta[0] >> bit) & 1) ^ rev) == 1
    for p in range(packs // 2):
        a, b = decode_state(total[p], heads, size), decode_state(other[p], heads, size)
        both = compose(choose(upper_is_own, b, a), choose(upper_is_own, a, b), heads, size)
        encode_state(next_o, p, *both, heads, size)
        entering, longer = entering_from(before, b, p, heads, size)
        encode_state(before_o, p, *choose(upper_is_own, longer, entering), heads, size)


def last_kernel(dims, rev, bit, first, meta, *refs):
    packs, heads, size = dims
    own, pair, other = refs[0:3]
    before, keep_o, send_o = (None, refs[3], refs[4]) if first else refs[3:6]
    add = (((meta[0] >> bit) & 1) ^ rev) == 1
    upper_is_own = ((meta[0] & 1) ^ rev) == 1
    for p in range(packs // 2):
        entering, longer = entering_from(
            before, decode_state(other[p], heads, size), p, heads, size
        )
        low = choose(add, longer, entering)
        lower = decode_state(jnp.where(upper_is_own, pair[p].astype(jnp.int32), own[p].astype(jnp.int32)), heads, size)
        high = compose(low, lower, heads, size)
        encode_state(keep_o, p, *choose(upper_is_own, high, low), heads, size)
        encode_state(send_o, p, *choose(upper_is_own, low, high), heads, size)


def gate_kernel(dims, meta, lens, *refs):
    packs, count, features, inner, bc, heads, size, width, nseq = dims
    xbc, steps, inner_in, keep, recv, gate, gg, gain, skip, y_o, stats_o = refs
    pack = pl.program_id(0)
    state = jnp.concatenate(
        split2(load_state(meta, packs, pack, keep, recv, heads, size)), axis=1
    )
    carry = carry_column(meta, column_segments(meta, lens, pack, count, nseq, EDGE), EDGE)
    matrix = spread_matrix(heads, size)
    entering = spread(carry * jnp.exp(from_group(steps[0], 1, heads)), matrix, heads)
    c_vals = xbc[0, :, inner + bc // 2 :]
    y = inner_in[0] + entering * nt(jnp.concatenate([c_vals, c_vals], axis=1), state)
    y_o[0] = y
    gate_f = gate[0].astype(f32)
    ssd = y + xbc[0, :, :inner].astype(f32) * skip[...]
    mixed = ssd * (gate_f * sigmoid(gate_f))
    squares = jnp.sum(mixed * mixed, axis=1, keepdims=True)
    dots = jnp.sum(gain[...] * gg[0] * mixed, axis=1, keepdims=True)
    lane = lax.broadcasted_iota(jnp.int32, (count, LANES), 1)
    both = jnp.where(lane == 0, squares, 0.0) + jnp.where(lane == 1, dots, 0.0)
    stats_o[0] = jnp.transpose(both)[0:2]


def grad_kernel(dims, total_inner, meta, lens, *refs):
    packs, count, features, inner, bc, heads, size, width, nseq = dims
    (
        stats, xbc, steps, y, gate, gg, gain, skip,
        gy_o, gated_o, ggate_o, keep_o, send_o, small_o,
    ) = refs
    pack = pl.program_id(0)
    sums = stats[0, 0] + stats[1, 0] + stats[2, 0] + stats[3, 0]
    row = lax.broadcasted_iota(jnp.int32, (LANES, count), 0)
    wide = jnp.where(row == 0, sums[0:1], 0.0) + jnp.where(row == 1, sums[1:2], 0.0)
    cols = jnp.transpose(wide)
    inv = lax.rsqrt(cols[:, 0:1] / total_inner + EPSILON)
    dot = cols[:, 1:2] / total_inner
    x_f, gg_f, gate_f = xbc[0, :, :inner].astype(f32), gg[0], gate[0].astype(f32)
    ssd = y[0] + x_f * skip[...]
    sig = sigmoid(gate_f)
    act = gate_f * sig
    mixed = ssd * act
    scaled = mixed * inv
    gated_o[0] = (scaled * gain[...]).astype(bf16)
    grad_mixed = inv * gain[...] * gg_f - mixed * (inv * inv * inv * dot)
    gy_f = grad_mixed * act
    gy_o[0] = gy_f
    ggate_o[0] = (grad_mixed * ssd * sig * (1.0 + gate_f * (1.0 - sig))).astype(bf16)
    carry = carry_column(meta, column_segments(meta, lens, pack, count, nseq, EDGE), EDGE)
    cum = from_group(steps[0], 1, heads)
    entering = carry * jnp.exp(cum)
    ey_hi, ey_lo = split2(gy_f * spread(entering, spread_matrix(heads, size), heads))
    c_vals = xbc[0, :, inner + bc // 2 :]
    state_grad = tn(ey_hi, c_vals) + tn(ey_lo, c_vals)
    store_state(
        meta, packs, pack, keep_o, send_o, state_grad, entering[count - 1 :], heads, size
    )

    @pl.when(pack == 0)
    def _():
        small_o[...] = jnp.zeros_like(small_o)

    small_o[0:1, :] += jnp.sum(gg_f * scaled, axis=0, keepdims=True)
    small_o[1:2, :] += jnp.sum(gy_f * x_f, axis=0, keepdims=True)


def diag_kernel(dims, meta, lens, *refs):
    packs, count, features, inner, bc, heads, size, width, nseq = dims
    xbc, steps, gy, y, keep, recv, dx_o, dbc_o, sums_o = refs
    pack = pl.program_id(0)
    half = bc // 2
    b_vals, c_vals = xbc[0, :, inner : inner + half], xbc[0, :, inner + half :]
    mask = block_mask(meta, lens, pack, count, nseq)
    scores = jnp.where(mask, nt(c_vals, b_vals), 0.0)
    dt, cum_col = steps_of(steps[0], heads)
    cum_row = jnp.transpose(cum_col)
    dt_row = jnp.transpose(dt)
    lane = lax.broadcasted_iota(jnp.int32, (count, 2 * size), 1)
    grad_scores = jnp.zeros((count, count), f32)
    zero = jnp.zeros((), bf16)
    for pair in range(heads // 2):
        cols = slice(2 * pair * size, (2 * pair + 2) * size)
        x_pair = xbc[0, :, cols]
        x_twice = jnp.concatenate([x_pair, x_pair], axis=1)
        gy_hi, gy_lo = split2(gy[0, :, cols])
        gy_wide = jnp.concatenate([gy_hi, gy_lo], axis=1)
        parts = []
        for h in (2 * pair, 2 * pair + 1):
            own = (lane < size) if h % 2 == 0 else (lane >= size)
            part = jnp.exp(jnp.minimum(cum_col[:, h : h + 1] - cum_row[h : h + 1], 0.0)) * dt_row[h : h + 1]
            parts.append(tn((scores * part).astype(bf16), gy_wide))
            both = jnp.concatenate([jnp.where(own, gy_hi, zero), jnp.where(own, gy_lo, zero)], axis=1)
            grad_scores = grad_scores + nt(both, x_twice) * part
        two = [part[:, : 2 * size] + part[:, 2 * size :] for part in parts]
        dx_o[0, :, cols] = jnp.where(lane < size, two[0], two[1])
    hi, lo = split2(jnp.where(mask, grad_scores, 0.0))
    state_hi, state_lo = split2(load_state(meta, packs, pack, keep, recv, heads, size))
    carry = carry_column(meta, column_segments(meta, lens, pack, count, nseq, EDGE), EDGE)
    matrix = spread_matrix(heads, size)
    ey_hi, ey_lo = split2(gy[0] * spread(carry * jnp.exp(cum_col), matrix, heads))
    dbc_o[0, :, :half] = tn(hi, c_vals) + tn(lo, c_vals)
    dbc_o[0, :, half:] = (
        nn(jnp.concatenate([hi, lo], axis=1), jnp.concatenate([b_vals, b_vals], axis=0))
        + nn(ey_hi, state_hi) + nn(ey_hi, state_lo) + nn(ey_lo, state_hi)
    )
    row_sum = collapse(gy[0] * y[0], matrix, heads)
    col_sum = collapse(xbc[0, :, :inner].astype(f32) * dx_o[0], matrix, heads)
    sums_o[0] = row_sum + to_group(col_sum, 1)


def scatter_pieces(head, stage, own_o, far_o, send_o):
    own_o[0] = stage[head]
    send_o[0, 0] = stage[head ^ 1].astype(bf16)
    far_o[0] = stage[head ^ 2]
    send_o[1, 0] = stage[head ^ 3].astype(bf16)


def accumulate(meta, pack, packs, sums, term, keep_o, send_o):
    wide = term.reshape(sums.shape)

    @pl.when(pack == 0)
    def _():
        sums[...] = wide

    @pl.when(pack > 0)
    def _():
        sums[...] += wide

    @pl.when(pack == packs - 1)
    def _():
        side = meta[0] & 1
        keep_o[...] = sums[side]
        send_o[...] = sums[1 - side].astype(bf16)


def out_kernel(dims, meta, lens, *refs):
    packs, count, features, inner, bc, heads, size, width, nseq = dims
    gated, cot, wout, own_o, far_o, send_o, keep_o, give_o, stage, sums = refs
    pack = pl.program_id(0)
    stage[...] = tn(wout[...], jnp.transpose(gated[0])).reshape(stage.shape)
    scatter_pieces(meta[1], stage, own_o, far_o, send_o)
    accumulate(meta, pack, packs, sums, nn(cot[0], gated[0]), keep_o, give_o)


def z_kernel(dims, meta, lens, *refs):
    normed, ggate, keep_o, give_o, sums = refs
    accumulate(
        meta, pl.program_id(0), dims[0], sums, nn(normed[0], ggate[0]), keep_o, give_o
    )


def end_weights(seg, seg_main, cum_col, dt_col, count):
    cum_end = cum_col[count - 1 :]
    end = seg[count + EDGE - 1 :]
    return jnp.where(seg_main == end, jnp.exp(cum_end - cum_col), 0.0) * dt_col


def share_kernel(dims, meta, lens, *refs):
    packs, count, features, inner, bc, heads, size, width, nseq = dims
    xbc, steps, dbc, gkeep, grecv, own_o, near_o = refs
    pack = pl.program_id(0)
    half, quarter = bc // 2, bc // 4
    g_hi, g_lo = split2(load_state(meta, packs, pack, gkeep, grecv, heads, size))
    seg = column_segments(meta, lens, pack, count, nseq, EDGE)
    dt, cum = steps_of(steps[0], heads)
    wide = spread(end_weights(seg, seg[EDGE:], cum, dt, count), spread_matrix(heads, size), heads)
    hi, lo = split2(wide * xbc[0, :, :inner].astype(f32))
    grad_b = dbc[0, :, :half] + nn(hi, g_hi) + nn(lo, g_hi) + nn(hi, g_lo)
    grad_c = dbc[0, :, half:]
    even = jnp.concatenate([grad_b[:, :quarter], grad_c[:, :quarter]], axis=1)
    odd = jnp.concatenate([grad_b[:, quarter:], grad_c[:, quarter:]], axis=1)
    first = (meta[1] & 1) == 0
    own_o[0] = jnp.where(first, even, odd)
    near_o[0] = jnp.where(first, odd, even)


def middle_kernel(dims, meta, *refs):
    packs, quarter = dims
    own, near, keep_o, send_o, edge_o = refs
    half = packs // 2
    first = (meta[1] >> 1) == 0
    for p in range(half):
        a, b = own[p] + near[p], own[p + half] + near[p + half]
        low = jnp.concatenate([a[:, :quarter], b[:, :quarter]], axis=1)
        high = jnp.concatenate([a[:, quarter:], b[:, quarter:]], axis=1)
        keep_o[p] = jnp.where(first, low, high)
        send_o[p] = jnp.where(first, high, low)
        edge_o[p] = keep_o[p, :EDGE, :]
        edge_o[half + p] = send_o[p, :EDGE, :]


def conv_taps(grads, raws, gconv_o, seg, count, width):
    seg_main = seg[EDGE : EDGE + count]
    for k in range(width):
        low = EDGE - (width - 1) + k
        mask = jnp.where(seg[low : low + count] == seg_main, 1.0, 0.0)
        gconv_o[k : k + 1, :] += jnp.sum(
            grads * (raws[low : low + count, :] * mask), axis=0, keepdims=True
        )
    gconv_o[width : width + 1, :] += jnp.sum(grads, axis=0, keepdims=True)


def conv_rows(gpad, conv, seg, rows, width):
    total = jnp.zeros((rows, gpad.shape[1]), f32)
    for lag in range(width):
        mask = jnp.where(seg[lag : lag + rows] == seg[:rows], 1.0, 0.0)
        k = width - 1 - lag
        total = total + conv[k : k + 1, :] * (gpad[lag : lag + rows, :] * mask)
    return total


def xback_kernel(dims, meta, lens, *refs):
    packs, count, features, inner, bc, heads, size, width, nseq = dims
    (
        xbc, steps, gy, dx, gkeep, grecv, slope, raw, normed, edge, conv, skip,
        main_o, edge_o, state_sum_o, keep_o, give_o, gconv_o,
        gpad, raws, sums,
    ) = refs
    pack = pl.program_id(0)
    gstate = jnp.concatenate(
        split2(load_state(meta, packs, pack, gkeep, grecv, heads, size)), axis=1
    )
    seg = column_segments(meta, lens, pack, count, nseq, EDGE)
    matrix = spread_matrix(heads, size)
    b_vals = xbc[0, :, inner : inner + bc // 2]
    dt, cum = steps_of(steps[0], heads)
    wide = spread(end_weights(seg, seg[EDGE:], cum, dt, count), matrix, heads)
    u_wide = wide * nt(jnp.concatenate([b_vals, b_vals], axis=1), gstate)
    state_sum_o[0] = collapse(xbc[0, :, :inner].astype(f32) * u_wide, matrix, heads)
    grad_x = (dx[0] + u_wide + gy[0] * skip[...]) * slope[0].astype(f32)

    @pl.when(pack == 0)
    def _():
        for ref in (gconv_o, gpad, edge_o):
            ref[...] = jnp.zeros_like(ref)

    raws[...] = raw[0].astype(f32)
    gpad[EDGE : EDGE + count, :] = grad_x
    conv_taps(grad_x, raws, gconv_o, seg, count, width)
    seg_pad = jnp.concatenate([seg, jnp.full((8, 1), -1, jnp.int32)], axis=0)
    grad_raw = conv_rows(gpad, conv, seg_pad, count + EDGE, width).astype(bf16)
    main_o[0] = grad_raw[EDGE:]
    edge_o[pl.ds(pl.multiple_of(pack * EDGE, EDGE), EDGE), :] = grad_raw[:EDGE]
    term = nn(normed[0], grad_raw[EDGE:]).reshape(sums.shape)

    @pl.when(pack == 0)
    def _():
        sums[...] = term

    @pl.when(pack > 0)
    def _():
        sums[...] += term

    @pl.when(pack == packs - 1)
    def _():
        sums[...] += nn(edge[...], edge_o[...]).reshape(sums.shape)
        side = meta[0] & 1
        keep_o[...] = sums[side]
        give_o[...] = sums[1 - side].astype(bf16)


def conv_bc_kernel(dims, meta, lens, *refs):
    packs, count, features, inner, bc, heads, size, width, nseq = dims
    (
        keep, recv, edge_keep, edge_recv, slope, slope_next, raw, normed, conv,
        rows_o, keep_o, give_o, gconv_o,
        gpad, raws, sums,
    ) = refs
    pack = pl.program_id(0)
    quarter = bc // 4
    early = pack < packs // 2

    @pl.when(pack == 0)
    def _():
        gconv_o[...] = jnp.zeros_like(gconv_o)

    def own_pack(values):
        return jnp.where(early, values[:, :quarter], values[:, quarter:])

    grad = own_pack(keep[0] + recv[0]) * slope[0]
    gpad[:count, :] = grad
    gpad[count:, :] = own_pack(edge_keep[0] + edge_recv[0]) * slope_next[0]
    rows = lax.broadcasted_iota(jnp.int32, (count + 2 * EDGE, 1), 0)
    seg = segments(rows + (meta[0] * count - EDGE), lens, pack, nseq)
    raws[...] = raw[0].astype(f32)
    conv_taps(grad, raws, gconv_o, seg, count, width)
    grad_bc = conv_rows(gpad, conv, seg[EDGE:], count, width).astype(bf16)
    rows_o[0] = grad_bc
    term = nn(normed[0], grad_bc)

    @pl.when(pack == 0)
    def _():
        sums[...] = term

    @pl.when(pack > 0)
    def _():
        sums[...] += term

    @pl.when(pack == packs - 1)
    def _():
        total = jnp.transpose(sums[...])
        first = (meta[0] & 1) == 0
        keep_o[...] = jnp.where(first, total[:, :inner], total[:, inner:])
        give_o[...] = jnp.where(first, total[:, inner:], total[:, :inner]).astype(bf16)


def step_kernel(dims, meta, lens, *refs):
    packs, count, features, inner, bc, heads, size, width, nseq = dims
    (
        steps, sums, state_sums, keep, recv, gkeep, grecv, small, normed, gconv_x, gconv_bc,
        gate_small,
        gdt_o, small_o,
        gdt_sums, gsmall,
    ) = refs
    pack = pl.program_id(0)
    state = load_state(meta, packs, pack, keep, recv, heads, size)
    gstate = load_state(meta, packs, pack, gkeep, grecv, heads, size)
    seg = column_segments(meta, lens, pack, count, nseq, EDGE)
    matrix = spread_matrix(heads, size)
    v = steps[0]
    dt, cum = steps_of(v, heads)
    sig = head_lanes(sigmoid(v), heads)
    row_sum, col_sum = from_group(sums[0], 0, heads), from_group(sums[0], 1, heads)
    state_sum = state_sums[0]
    carry = carry_column(meta, seg, EDGE)
    hi, lo = split2(gstate * state)
    ones = jnp.ones((8, LANES), bf16)
    by_head = collapse(nt(ones, hi) + nt(ones, lo), matrix, heads)[0:1]
    last = by_head * carry[count - 1 :] * jnp.exp(cum[count - 1 :]) + jnp.sum(
        state_sum, axis=0, keepdims=True
    )
    rows = lax.broadcasted_iota(jnp.int32, (count, LANES), 0)
    grad_cum = row_sum - col_sum - state_sum + jnp.where(rows == count - 1, last, 0.0)
    grad_rate = exact_sums(triangle(count, False), grad_cum, heads)
    decay_rate = -jnp.exp(small[1:2, :])
    ratio = jnp.where(dt > 1e-30, sig / jnp.maximum(dt, 1e-30), 1.0)
    grad_dt = head_lanes(ratio * (col_sum + state_sum) + grad_rate * decay_rate * sig, heads)
    low = grad_dt.astype(bf16)
    gdt_o[0] = low

    @pl.when(pack == 0)
    def _():
        for ref in (gsmall, gdt_sums):
            ref[...] = jnp.zeros_like(ref)

    gsmall[0:1, :] += jnp.sum(grad_dt, axis=0, keepdims=True)
    gsmall[1:2, :] += jnp.sum(grad_rate * dt * decay_rate, axis=0, keepdims=True)
    gdt_sums[...] += nn(normed[0], low)

    @pl.when(pack == packs - 1)
    def _():
        taps, quarter = width + 1, bc // 4
        small_o[...] = jnp.zeros_like(small_o)
        small_o[0:heads, :] = jnp.transpose(gdt_sums[...])[0:heads]
        small_o[8 : 8 + taps, :inner] = gconv_x[0:taps, :]
        small_o[8 : 8 + taps, inner : inner + quarter] = gconv_bc[0:taps, :]
        small_o[13:14, :inner] = gate_small[0:1, :]
        skips = collapse(gate_small[...], matrix, heads)
        start = 2 * inner - 3 * LANES
        small_o[13:14, start : start + LANES] = gsmall[0:1, :]
        small_o[13:14, start + LANES : start + 2 * LANES] = gsmall[1:2, :]
        small_o[13:14, start + 2 * LANES :] = skips[1:2, :]


def back_kernel(dims, meta, lens, *refs):
    packs, count, features, inner, bc, heads, size, width, nseq = dims
    (
        main, edge_x, ggate, gdt, gbc, normed, wz, wx, wbc, wdt, gain,
        own_o, far_o, send_o, extra_o,
        stage, gain_sums, gains,
    ) = refs
    pack = pl.program_id(0)
    head = meta[1]
    part = features // 4

    @pl.when(pack == 0)
    def _():
        gain_sums[...] = jnp.zeros_like(gain_sums)
        gains[...] = jnp.zeros_like(gains)

    late = main[0, count - EDGE :, :].astype(f32) + edge_x[...].astype(f32)
    grad_x = jnp.concatenate([main[0, : count - EDGE, :], late.astype(bf16)], axis=0)
    whole = nt(wz[...], ggate[0]) + nt(wx[...], grad_x) + nt(wbc[...], gbc[0]) + nt(wdt[...], gdt[0])
    product = whole * normed[0].astype(f32)
    gain_sums[...] += jnp.sum(product, axis=1, keepdims=True)
    dots = jnp.sum(product, axis=0, keepdims=True)
    stage[...] = whole.reshape(stage.shape)

    @pl.when(pack == packs - 1)
    def _():
        row = jnp.transpose(jnp.broadcast_to(gain_sums[...] / gain[...], (features, LANES)))
        for h in range(4):
            gains[h, 0:1, :part] = row[0:1, h * part : (h + 1) * part]

    own_o[0] = stage[head]
    far_o[0] = stage[head ^ 2]
    extra_o[0, 0:1, :] = dots
    extra_o[0, 1:2, :] = gains[head, 0:1, :]
    extra_o[0, 2:3, :] = gains[head ^ 2, 0:1, :]
    for k in range(2):
        send_o[k, 0, :part, :] = stage[head ^ (1 + 2 * k)].astype(bf16)
        send_o[k, 0, part:, :] = extra_rows(dots, gains[head ^ (1 + 2 * k), 0:1, :])


def extra_rows(*values):
    row = lax.broadcasted_iota(jnp.int32, (EDGE, values[0].shape[1]), 0)
    total = jnp.zeros(row.shape, f32)
    for i, value in enumerate(values):
        for k, piece in enumerate(split3(value)):
            total = total + jnp.where(row == 3 * i + k, piece.astype(f32), 0.0)
    return total.astype(bf16)


def read_extra(block, i):
    rows = block.astype(f32)
    return rows[3 * i : 3 * i + 1] + rows[3 * i + 1 : 3 * i + 2] + rows[3 * i + 2 : 3 * i + 3]


def gather_kernel(own, far, near, extra, own_o, far_o, extra_o):
    part = own.shape[1]
    own_o[0] = own[0] + near[0, 0, :part, :].astype(f32)
    far_o[0, :part, :] = (far[0] + near[1, 0, :part, :].astype(f32)).astype(bf16)
    mine, others = near[0, 0, part:, :], near[1, 0, part:, :]
    dots = extra[0, 0:1, :] + read_extra(mine, 0)
    extra_o[0, 0:1, :] = dots
    extra_o[0, 1:2, :] = extra[0, 1:2, :] + read_extra(mine, 1)
    far_o[0, part:, :] = extra_rows(dots, extra[0, 2:3, :] + read_extra(others, 1))


def final_kernel(dims, own, far, extra, tokens, inv, gain, out_grad, in_grad_o, gain_o):
    packs, count, features = dims
    part = own.shape[1]
    grad = own[0] + far[0, :part, :].astype(f32)
    mean = (extra[0, 0:1, :] + read_extra(far[0, part:, :], 0)) / features
    unit = tokens[0].astype(f32) * inv[0]
    in_grad_o[0] = out_grad[0].astype(f32) + inv[0] * (gain[...] * grad - unit * mean)

    @pl.when(pl.program_id(0) == packs - 1)
    def _():
        gain_o[...] = jnp.broadcast_to(
            extra[0, 1:2, :] + read_extra(far[0, part:, :], 1), gain_o.shape
        )


def add_kernel(bit, halve, segs, count, small, meta, *refs):
    keep, got, refs = refs[:count], refs[count : 2 * count], refs[2 * count :]
    if small:
        refs[-1][...] = refs[0][...] + refs[1][...]
        refs = refs[2:-1]
    read, write = 0, 0
    for i, rows in enumerate(segs):
        if count > 1:
            total = keep[i][...] + got[i][...].astype(f32)
        else:
            total = keep[0][read : read + rows, :].astype(f32) + got[0][read : read + rows, :].astype(f32)
        read += rows
        if halve:
            half = rows // 2
            first = ((meta[0] >> bit) & 1) == 0
            top, bottom = total[:half], total[half:]
            refs[0][write : write + half, :] = jnp.where(first, top, bottom)
            refs[1][write : write + half, :] = jnp.where(first, bottom, top).astype(bf16)
            write += half
        else:
            refs[0][write : write + rows, :] = total.astype(bf16)
            write += rows


def join_kernel(bit, segs, meta, mine, got, out):
    first = ((meta[0] >> bit) & 1) == 0
    read = 0
    for rows in segs:
        a = mine[read : read + rows, :].astype(f32)
        b = got[read : read + rows, :].astype(f32)
        out[2 * read : 2 * read + rows, :] = jnp.where(first, a, b).astype(bf16)
        out[2 * read + rows : 2 * read + 2 * rows, :] = jnp.where(first, b, a).astype(bf16)
        read += rows


def result_kernel(segs, ways, meta, mine, got, *outs):
    first = (meta[0] & 1) == 0
    read = 0
    for rows, way, out in zip(segs, ways, outs):
        a = mine[read : read + rows, :].astype(f32)
        b = got[read : read + rows, :].astype(f32)
        top, bottom = jnp.where(first, a, b), jnp.where(first, b, a)
        if way == "rows":
            out[:rows, :] = top
            out[rows:, :] = bottom
        elif way == "flip":
            out[:, :rows] = jnp.transpose(top)
            out[:, rows:] = jnp.transpose(bottom)
        else:
            out[...] = jnp.concatenate([top, bottom], axis=1)
        read += rows


def whole_spec(shape):
    return pl.BlockSpec(shape, lambda p, *_: (0,) * len(shape))


def pack_spec(shape):
    return pl.BlockSpec((1,) + shape, lambda p, *_: (p,) + (0,) * len(shape))


def half_spec(shape, half):
    return pl.BlockSpec((1,) + shape, lambda p, *_: (p % half,) + (0,) * len(shape))


def side_spec(shape, half, keep):
    def index(p, meta, *_):
        side = meta[0] & 1 if keep else 1 - (meta[0] & 1)
        group = p // half
        spot = jnp.where(group == side, p % half, jnp.where(group < side, 0, half - 1))
        return (spot,) + (0,) * len(shape)

    return pl.BlockSpec((1,) + shape, index)


class Order:
    def __init__(self):
        self.last = ()


order = Order()


def call(kernel, grid, in_specs, out_specs, out_shape, scratch, prefetch, *args, limit=60, wait=(), us=1):
    first = len(prefetch) + len(args)
    held = order.last + tuple(wait)
    late = len(held)

    def body(*refs):
        kernel(*refs[:first], *refs[first + late :])

    outs = pl.pallas_call(
        body,
        grid_spec=pltpu.PrefetchScalarGridSpec(
            num_scalar_prefetch=len(prefetch),
            grid=grid,
            in_specs=list(in_specs) + [pl.BlockSpec(memory_space=pl.ANY)] * late,
            out_specs=out_specs,
            scratch_shapes=scratch,
        ),
        out_shape=out_shape,
        compiler_params=pltpu.CompilerParams(vmem_limit_bytes=limit * MIB),
        cost_estimate=pl.CostEstimate(
            flops=int(us * 10e9), bytes_accessed=int(us * 3e6), transcendentals=0
        ),
    )(*prefetch, *args, *held)
    order.last = (min(jax.tree.leaves(outs), key=lambda x: x.size),)
    return outs


def shape(*dims_and_type):
    return jax.ShapeDtypeStruct(dims_and_type[:-1], dims_and_type[-1])


def scan_states(keep, send, meta, packs, heads, size, rev, beside, waits=lambda: ()):
    dims = (packs, heads, size)
    rows = heads * size
    half = packs // 2
    pay = shape(half, rows + EDGE, LANES, jnp.int16)
    spec = whole_spec(pay.shape)
    bits = (lax.axis_size("seq") - 1).bit_length()
    beside = list(beside)

    def work():
        if beside:
            beside.pop(0)()

    other = swap(send, "seq", 1)
    work()
    total = call(
        functools.partial(pair_kernel, dims, rev), (1,), [spec, spec], spec, pay, [], (meta,),
        keep, other, limit=8,
    )
    before = None
    for bit in range(1, bits):
        got = swap(total, "seq", 1 << bit)
        extra = () if before is None else (before,)
        work()
        if bit < bits - 1:
            total, before = call(
                functools.partial(cube_kernel, dims, rev, bit, before is None), (1,),
                [spec] * (2 + len(extra)), [spec, spec], [pay, pay], [], (meta,),
                total, got, *extra, limit=8,
            )
        else:
            own, back = call(
                functools.partial(last_kernel, dims, rev, bit, before is None), (1,),
                [spec] * (3 + len(extra)), [spec, spec], [pay, pay], [],
                (meta,), keep, other, got, *extra, limit=8, wait=waits(),
            )
    recv = swap(back, "seq", 1)
    while beside:
        work()
    return own, recv


class SeqSum:
    def __init__(self):
        self.keep, self.got, self.segs = [], [], []
        self.small = self.small_got = self.bit = None
        self.bits = list(range(1, (lax.axis_size("seq") - 1).bit_length()))
        self.halved = []

    def put(self, keep, give):
        self.keep.append(keep)
        self.got.append(swap(give, "seq", 1))
        self.segs.append(keep.shape[0])

    def put_small(self, small):
        self.small, self.small_got = small, swap(small, "seq", 1)

    def add(self, meta):
        bit = self.bits.pop(0) if self.bits else None
        halve = bit is not None and all(rows % (2 * EDGE) == 0 for rows in self.segs)
        cols = self.keep[0].shape[1]
        segs = [rows // 2 for rows in self.segs] if halve else self.segs
        rows = sum(segs)
        low = shape(rows, cols, bf16)
        out = [shape(rows, cols, f32), low] if halve else [low]
        small = [] if self.small is None else [self.small, self.small_got]
        if small:
            out.append(shape(*self.small.shape, f32))
        ins = [*self.keep, *self.got, *small]
        outs = call(
            functools.partial(add_kernel, bit, halve, self.segs, len(self.keep), bool(small)), (1,),
            [whole_spec(x.shape) for x in ins], [whole_spec(x.shape) for x in out], out, [],
            (meta,), *ins, limit=12,
        )
        if small:
            self.small = outs[-1]
        self.segs, self.keep = segs, [outs[0]]
        if bit is None:
            return True
        self.got = [swap(outs[1] if halve else outs[0], "seq", 1 << bit)]
        if small:
            self.small_got = swap(self.small, "seq", 1 << bit)
        if halve:
            self.halved.append(bit)
        return False

    def send_back(self):
        self.bit = self.halved.pop() if self.halved else 0
        self.got = [swap(self.keep[0], "seq", 1 << self.bit)]

    def join(self, meta):
        rows, cols = self.keep[0].shape
        both = shape(2 * rows, cols, bf16)
        spec = whole_spec((rows, cols))
        self.keep = [call(
            functools.partial(join_kernel, self.bit, self.segs), (1,), [spec, spec],
            whole_spec(both.shape), both, [], (meta,), self.keep[0], self.got[0], limit=12,
        )]
        self.segs = [2 * rows for rows in self.segs]

    def result(self, meta, ways):
        cols = self.keep[0].shape[1]
        shapes = {"rows": lambda r: (2 * r, cols), "flip": lambda r: (cols, 2 * r), "cols": lambda r: (r, 2 * cols)}
        out = [shape(*shapes[way](rows), f32) for way, rows in zip(ways, self.segs)]
        spec = whole_spec(self.keep[0].shape)
        return call(
            functools.partial(result_kernel, self.segs, ways), (1,), [spec, spec],
            [whole_spec(x.shape) for x in out], out, [], (meta,), self.keep[0], self.got[0],
            limit=16,
            us=2,
        )


def advance(total, meta):
    if total.bit is None:
        if total.add(meta):
            total.send_back()
    elif total.bit:
        total.join(meta)
        total.send_back()


def sum_over(x, axis):
    bit = 1
    while bit < lax.axis_size(axis):
        x = x + swap(x, axis, bit)
        bit *= 2
    return x


def shards(
    tokens_in, out_grad, lengths, norm_gain, proj_z, proj_x, proj_bc, proj_dt, conv_x, conv_bc,
    bias_x, bias_bc, dt_bias, a_log, d_skip, gate_gain, proj_out,
):
    packs, count, part = tokens_in.shape
    features, inner = proj_x.shape
    heads = proj_dt.shape[1]
    size = inner // heads
    width = conv_x.shape[0]
    nseq = lengths.shape[1]
    bc_part = proj_bc.shape[1]
    bc = bc_part * lax.axis_size("head")
    half = packs // 2
    chans = inner + bc
    ext = count + EDGE
    rows = heads * size
    total_inner = inner * lax.axis_size("head")
    dims = (packs, count, features, inner, bc, heads, size, width, nseq)
    seq_place, head_place = lax.axis_index("seq"), lax.axis_index("head")
    meta = jnp.stack([seq_place, head_place]).astype(jnp.int32)
    pre = (meta, lengths)
    grid = (packs,)

    order.last = ()
    tokens = jnp.swapaxes(tokens_in, 1, 2)
    cotangent = jnp.swapaxes(out_grad, 1, 2)
    token_pieces = head_pieces(tokens)
    tail = jnp.concatenate([tokens[p, :, count - EDGE :] for p in range(packs)], axis=1)
    tail = jnp.pad(tail, ((0, 0), (0, LANES - packs * EDGE)))
    edge_pieces = head_pieces(shift(tail, "seq", 1))
    extra = jnp.concatenate(
        [conv_bc.T, bias_bc[:, None], norm_gain.reshape(-1, bc_part).T], axis=1
    )
    extra = jnp.pad(extra, ((0, 0), (0, LANES - extra.shape[1])))
    weight_pieces = head_pieces(jnp.concatenate([proj_bc.T, extra], axis=1))
    conv_own = jnp.pad(
        jnp.concatenate([conv_x, bias_x[None]], axis=0).astype(f32), ((0, 7 - width), (0, 0))
    )
    conv_bc_own = jnp.pad(
        jnp.concatenate([conv_bc, bias_bc[None]], axis=0).astype(f32), ((0, 7 - width), (0, 0))
    )
    w_dt = jnp.pad(proj_dt, ((0, 0), (0, LANES - heads)))
    small = jnp.pad(jnp.stack([dt_bias, a_log]).astype(f32), ((0, 6), (0, LANES - heads)))
    skip = jnp.repeat(d_skip.astype(f32), size)[None]
    gain_gate = gate_gain.astype(f32)[None]

    lane_spec = pack_spec((count, LANES))
    chan_spec = pack_spec((count, inner))
    xbc_spec = pack_spec((count, chans))
    model_spec = pack_spec((features, count))
    piece_spec = pack_spec((part, count))
    edge_spec = whole_spec((part, LANES))
    pay_shape = (rows + EDGE, LANES)
    pay_specs = [side_spec(pay_shape, half, k) for k in (True, False)]
    pay = shape(half, *pay_shape, jnp.int16)
    state_spec = half_spec(pay_shape, half)
    vec = whole_spec((1, inner))
    square = whole_spec((features, inner))

    (
        normed, inv, edge, raw_x, raw_bc, xbc, steps, keep, send, gain_all,
    ) = call(
        functools.partial(front_kernel, dims),
        grid,
        [piece_spec] * 4
        + [edge_spec] * 4
        + [whole_spec((bc_part, features + LANES))] * 4
        + [square, whole_spec((LANES, features)), whole_spec((8, inner)),
           whole_spec((8, LANES))],
        [
            model_spec, pack_spec((1, count)), whole_spec((features, LANES)),
            pack_spec((ext, inner)), pack_spec((ext, bc_part)), xbc_spec, lane_spec, *pay_specs,
            whole_spec((features, 1)),
        ],
        [
            shape(packs, features, count, bf16), shape(packs, 1, count, f32),
            shape(features, LANES, bf16), shape(packs, ext, inner, bf16),
            shape(packs, ext, bc_part, bf16), shape(packs, count, chans, bf16),
            shape(packs, count, LANES, f32), pay, pay, shape(features, 1, f32),
        ],
        [
            pltpu.VMEM((4, part, count), bf16), pltpu.VMEM((4, part, LANES), bf16),
            pltpu.VMEM((4, bc_part, features + LANES), bf16), pltpu.VMEM((ext, chans), f32),
            pltpu.VMEM((LANES, chans), f32), pltpu.VMEM((8, chans), f32),
            pltpu.VMEM((features, 1), f32),
        ],
        pre,
        *token_pieces, *edge_pieces, *weight_pieces, proj_x, w_dt.T, conv_own, small,
        us=15,
    )

    cots = head_pieces(lax.optimization_barrier((cotangent, steps))[0])
    kept = {}

    def inner_work():
        kept["inner"] = call(
            functools.partial(inner_kernel, dims),
            grid,
            [xbc_spec, lane_spec],
            chan_spec,
            shape(packs, count, inner, f32),
            [],
            pre,
            xbc, steps,
            us=6,
        )

    def cot_work():
        kept["cot"], kept["gg"] = call(
            functools.partial(cot_kernel, dims),
            grid,
            [piece_spec] * 4 + [whole_spec((inner, features))],
            [model_spec, chan_spec],
            [shape(packs, features, count, bf16), shape(packs, count, inner, f32)],
            [pltpu.VMEM((4, part, count), bf16)],
            pre,
            *cots, proj_out,
            us=5.5,
        )

    def gate_slope_work():
        kept["slope"] = call(
            functools.partial(gate_slope_kernel, dims),
            grid,
            [model_spec, square, pack_spec((ext, inner)), pack_spec((ext, bc_part)),
             whole_spec((8, inner)), whole_spec((8, bc_part))],
            [chan_spec, chan_spec, pack_spec((count, bc_part))],
            [shape(packs, count, inner, bf16), shape(packs, count, inner, f32),
             shape(packs, count, bc_part, f32)],
            [pltpu.VMEM((ext, inner), f32), pltpu.VMEM((ext, bc_part), f32)],
            pre,
            normed, proj_z, raw_x, raw_bc, conv_own, conv_bc_own,
            us=7,
        )

    state_keep, state_recv = scan_states(
        keep, send, meta, packs, heads, size, 0, (inner_work, cot_work, gate_slope_work)
    )
    inner_out, cot, gg = kept["inner"], kept["cot"], kept["gg"]
    gate, slope_x, slope_bc = kept["slope"]
    slope_next = shift(slope_bc[:, :EDGE], "seq", -1)

    y, stats = call(
        functools.partial(gate_kernel, dims),
        grid,
        [
            xbc_spec, lane_spec, chan_spec, state_spec, state_spec, chan_spec, chan_spec, vec, vec,
        ],
        [chan_spec, pack_spec((2, count))],
        [shape(packs, count, inner, f32), shape(packs, 2, count, f32)],
        [],
        pre,
        xbc, steps, inner_out, state_keep, state_recv, gate, gg, gain_gate, skip,
        us=6.6,
    )
    stats_all = lax.all_gather(stats, "head")

    gy, gated, ggate, gkeep, gsend, gate_small = call(
        functools.partial(grad_kernel, dims, total_inner),
        grid,
        [
            pl.BlockSpec((4, 1, 2, count), lambda p, *_: (0, p, 0, 0)),
            xbc_spec, lane_spec, chan_spec, chan_spec, chan_spec, vec, vec,
        ],
        [chan_spec] * 3 + pay_specs + [whole_spec((8, inner))],
        [shape(packs, count, inner, f32)] + [shape(packs, count, inner, bf16)] * 2
        + [pay, pay, shape(8, inner, f32)],
        [],
        pre,
        stats_all, xbc, steps, y, gate, gg, gain_gate, skip,
        us=8.3,
    )

    piece_shape = shape(packs, part, count, f32)
    send_spec = pl.BlockSpec((2, 1, part, count), lambda p, *_: (0, p, 0, 0))
    rows_half = features // 2
    half_specs = [whole_spec((rows_half, inner))] * 2
    half_shapes = [shape(rows_half, inner, f32), shape(rows_half, inner, bf16)]
    half_sums = pltpu.VMEM((2, rows_half, inner), f32)

    early_sum, late_sum = SeqSum(), SeqSum()

    def out_work():
        *kept["out"], keep, give = call(
            functools.partial(out_kernel, dims),
            grid,
            [chan_spec, model_spec, whole_spec((inner, features))],
            [piece_spec, piece_spec, send_spec] + half_specs,
            [piece_shape, piece_shape, shape(2, packs, part, count, bf16)] + half_shapes,
            [pltpu.VMEM((4, part, count), f32), half_sums],
            pre,
            gated, cot, proj_out,
            us=6.8,
        )
        early_sum.put(keep, give)

    def z_work():
        keep, give = call(
            functools.partial(z_kernel, dims),
            grid,
            [model_spec, chan_spec],
            half_specs,
            half_shapes,
            [half_sums],
            pre,
            normed, ggate,
            us=5.3,
        )
        early_sum.put(keep, give)

    def diag_work():
        kept["diag"] = call(
            functools.partial(diag_kernel, dims),
            grid,
            [xbc_spec, lane_spec, chan_spec, chan_spec, state_spec, state_spec],
            [chan_spec, pack_spec((count, bc)), lane_spec],
            [
                shape(packs, count, inner, f32), shape(packs, count, bc, f32),
                shape(packs, count, LANES, f32),
            ],
            [],
            pre,
            xbc, steps, gy, y, state_keep, state_recv,
            us=12,
        )

    gstate_keep, gstate_recv = scan_states(
        gkeep, gsend, meta, packs, heads, size, 1, (out_work, z_work, diag_work, lambda: early_sum.add(meta)),
        lambda: early_sum.got,
    )
    out_own, out_far, out_send = kept["out"]
    dx, dbc, sums = kept["diag"]

    def to_far(far, near):
        return swap((far + near[1].astype(f32)).astype(bf16), "head", 2)

    near = swap(out_send, "head", 1)
    block_out = tokens.astype(f32) + out_own + near[0].astype(f32) + to_far(out_far, near).astype(f32)
    block_out = jnp.swapaxes(block_out.astype(bf16), 1, 2)

    share_own, share_near = call(
        functools.partial(share_kernel, dims),
        grid,
        [xbc_spec, lane_spec, pack_spec((count, bc)), state_spec, state_spec],
        [lane_spec, lane_spec],
        [shape(packs, count, LANES, f32)] * 2,
        [],
        pre,
        xbc, steps, dbc, gstate_keep, gstate_recv,
        us=6.4,
    )
    share_near = swap(share_near, "head", 1)
    advance(early_sum, meta)
    two = shape(half, count, LANES, f32)
    rows_out = shape(packs, EDGE, LANES, f32)
    bc_keep, bc_send, bc_edge = call(
        functools.partial(middle_kernel, (packs, bc_part)),
        (1,),
        [whole_spec((packs, count, LANES))] * 2,
        [whole_spec(two.shape)] * 2 + [whole_spec(rows_out.shape)],
        [two, two, rows_out],
        [],
        (meta,),
        share_own, share_near,
        limit=8,
    )
    bc_recv = swap(bc_send, "head", 2)
    bc_edge = shift(bc_edge, "seq", -1)
    bc_edge_recv = swap(bc_edge, "head", 2)


    main_x, edge_x, state_sums, keep, give, grad_conv = call(
        functools.partial(xback_kernel, dims),
        grid,
        [
            xbc_spec, lane_spec, chan_spec, chan_spec, state_spec, state_spec, chan_spec,
            pack_spec((ext, inner)), model_spec, whole_spec((features, LANES)),
            whole_spec((8, inner)), vec,
        ],
        [chan_spec, whole_spec((LANES, inner)), lane_spec] + half_specs + [whole_spec((8, inner))],
        [
            shape(packs, count, inner, bf16), shape(LANES, inner, bf16),
            shape(packs, count, LANES, f32), *half_shapes, shape(8, inner, f32),
        ],
        [
            pltpu.VMEM((ext + EDGE, inner), f32), pltpu.VMEM((ext, inner), f32), half_sums,
        ],
        pre,
        xbc, steps, gy, dx, gstate_keep, gstate_recv, slope_x, raw_x, normed, edge, conv_own, skip,
        us=12.5,
    )
    late_sum.put(keep, give)
    edge_x = shift(edge_x, "seq", -1)
    advance(early_sum, meta)

    def half_block(shape_of, first):
        return pl.BlockSpec(
            (1,) + shape_of, lambda p, *_: (p % half + first,) + (0,) * len(shape_of)
        )

    edge_rows = (EDGE, LANES)
    bc_half = (bc_part, inner)
    gbc, keep, give, grad_conv_bc = call(
        functools.partial(conv_bc_kernel, dims),
        grid,
        [
            half_block((count, LANES), 0), half_block((count, LANES), 0),
            half_block(edge_rows, 0), half_block(edge_rows, half),
            pack_spec((count, bc_part)), pack_spec((EDGE, bc_part)), pack_spec((ext, bc_part)),
            model_spec, whole_spec((8, bc_part)),
        ],
        [pack_spec((count, bc_part)), whole_spec(bc_half), whole_spec(bc_half),
         whole_spec((8, bc_part))],
        [
            shape(packs, count, bc_part, bf16), shape(*bc_half, f32), shape(*bc_half, bf16),
            shape(8, bc_part, f32),
        ],
        [
            pltpu.VMEM((count + EDGE, bc_part), f32), pltpu.VMEM((ext, bc_part), f32),
            pltpu.VMEM((features, bc_part), f32),
        ],
        pre,
        bc_keep, bc_recv, bc_edge, bc_edge_recv, slope_bc, slope_next, raw_bc, normed, conv_bc_own,
        us=6.3,
    )
    late_sum.put(keep, give)

    gdt, smalls = call(
        functools.partial(step_kernel, dims),
        grid,
        [
            lane_spec, lane_spec, lane_spec, state_spec, state_spec, state_spec, state_spec,
            whole_spec((8, LANES)), model_spec, whole_spec((8, inner)), whole_spec((8, bc_part)),
            whole_spec((8, inner)),
        ],
        [lane_spec, whole_spec((EDGE, features))],
        [shape(packs, count, LANES, bf16), shape(EDGE, features, f32)],
        [pltpu.VMEM((features, LANES), f32), pltpu.VMEM((8, LANES), f32)],
        pre,
        steps, sums, state_sums, state_keep, state_recv, gstate_keep, gstate_recv, small, normed,
        grad_conv, grad_conv_bc, gate_small,
        us=8,
    )
    late_sum.put_small(smalls)
    advance(early_sum, meta)

    tall = part + EDGE
    send_spec = pl.BlockSpec((2, 1, tall, count), lambda p, *_: (0, p, 0, 0))
    tall_spec = pack_spec((tall, count))
    extra_spec = pack_spec((8, count))
    extra_shape = shape(packs, 8, count, f32)
    gn_own, gn_far, gn_send, extra = call(
        functools.partial(back_kernel, dims),
        grid,
        [
            chan_spec, pl.BlockSpec((EDGE, inner), lambda p, *_: (p, 0)), chan_spec, lane_spec,
            pack_spec((count, bc_part)), model_spec, square, square,
            whole_spec((features, bc_part)), whole_spec((features, LANES)),
            whole_spec((features, 1)),
        ],
        [piece_spec, piece_spec, send_spec, extra_spec],
        [piece_shape, piece_shape, shape(2, packs, tall, count, bf16), extra_shape],
        [
            pltpu.VMEM((4, part, count), f32), pltpu.VMEM((features, 1), f32),
            pltpu.VMEM((4, 8, count), f32),
        ],
        pre,
        main_x, edge_x, ggate, gdt, gbc, normed, proj_z, proj_x, proj_bc, w_dt, gain_all,
        us=8.3,
    )
    near = swap(gn_send, "head", 1)
    advance(late_sum, meta)

    gn_own, gn_far, extra = call(
        gather_kernel,
        grid,
        [piece_spec, piece_spec, send_spec, extra_spec],
        [piece_spec, tall_spec, extra_spec],
        [piece_shape, shape(packs, tall, count, bf16), extra_shape],
        [],
        (),
        gn_own, gn_far, near, extra,
        us=3.8,
    )
    gn_far = swap(gn_far, "head", 2)
    advance(early_sum, meta)
    advance(late_sum, meta)
    while early_sum.bit != 0:
        advance(early_sum, meta)
    advance(late_sum, meta)
    in_grad, grad_gain = call(
        functools.partial(final_kernel, (packs, count, features)),
        grid,
        [
            piece_spec, tall_spec, extra_spec, piece_spec, pack_spec((1, count)),
            whole_spec((part, 1)), piece_spec,
        ],
        [piece_spec, whole_spec((8, count))],
        [piece_shape, shape(8, count, f32)],
        [],
        (),
        gn_own, gn_far, extra, tokens, inv, norm_gain.astype(f32)[:, None], cotangent,
        us=4,
    )
    in_grad = jnp.swapaxes(in_grad, 1, 2)
    advance(late_sum, meta)
    grads_out, grads_z = early_sum.result(meta, ("flip", "rows"))
    while late_sum.bit != 0:
        advance(late_sum, meta)
    grads_x, grad_bc = late_sum.result(meta, ("rows", "cols"))
    smalls = late_sum.small
    grad_gain = sum_over(grad_gain, "seq")[0, :part]
    grad_conv, grad_conv_bc = smalls[8:13, :inner], smalls[8:13, inner : inner + bc_part]
    start = 2 * inner - 3 * LANES
    per_head = [smalls[13, start + k * LANES : start + k * LANES + heads] for k in range(3)]
    return (
        block_out,
        in_grad,
        grad_gain,
        grads_z,
        grads_x,
        grad_bc.T,
        smalls[:heads].T,
        grad_conv[:width],
        grad_conv_bc[:width],
        grad_conv[width],
        grad_conv_bc[width],
        *per_head,
        smalls[13, :inner],
        grads_out,
    )


def solution(mesh):
    token, column, vector = P(None, "seq", "head"), P(None, "head"), P("head")
    row = P("head", None)
    return jax.shard_map(
        shards,
        mesh=mesh,
        in_specs=(
            token, token, P(), vector, column, column, column, column, column, column, vector,
            vector, vector, vector, vector, vector, row,
        ),
        out_specs=(
            token, token, vector, column, column, column, column, column, column, vector, vector,
            vector, vector, vector, vector, row,
        ),
        check_vma=False,
    )
```

time: 348 us -> 282 us (0.81)
  waiting for transfers between devices: 97.8 us -> 17.5 us
  blocking collectives: 35.5 us -> 6.8 us
  Pallas kernels: 121 us -> 143 us
  starting transfers between devices: 46.4 us -> 63.1 us
  local copies, waits for them, and re-layouts: 28 us -> 38.2 us
  other arithmetic: 15.5 us -> 8.66 us
    all_to_all x4 -> x0, waiting for transfers between devices: 41.6 us -> none  [the longest x2 37.4 us: reduce_over_seq(): pieces = lax.all_to_all(parts.reshape(n, rows // n, cols), 'seq', 0, 0)]
    ppermute x29 -> x47, waiting for transfers between devices: 56.3 us -> 17.4 us  [swap(): lax.ppermute(x, axis, [(i, i ^ bit) for i in range(lax.axis_size(axis))])]
    ppermute x29 -> x47, starting transfers between devices: 27 us -> 55.4 us  [swap(): lax.ppermute(x, axis, [(i, i ^ bit) for i in range(lax.axis_size(axis))])]
    all_to_all x2 -> x0, blocking collectives: 23.6 us -> none  [the longest x1 12.9 us: reduce_over_seq(): pieces = lax.all_to_all(parts.reshape(n, rows // n, cols), 'seq', 0, 0)]
    pallas_call x20 -> x35, Pallas kernels: 121 us -> 143 us  [call(): pl.pallas_call(body, grid_spec=pltpu.PrefetchScalarGridSpec(num_scalar_pr...]
    all_to_all x4 -> x0, starting transfers between devices: 14.5 us -> none  [the longest x2 7.32 us: reduce_over_seq(): pieces = lax.all_to_all(parts.reshape(n, rows // n, cols), 'seq', 0, 0)]
    unnamed x92 -> x170, local copies, waits for them, and re-layouts: 11.8 us -> 24.4 us
    all_gather x1 -> x0, blocking collectives: 5.8 us -> none  [shards(): dots_all = lax.all_gather(dots, 'head')]
  transfers between devices with their start and end apart: 35 -> 51, of which waited for: 16 -> 11; matrix products, arithmetic and copies ran while one was open for 9% -> 9% of each run, Pallas kernels for 23% -> 44%
where the time goes in v2:
time: 282 us; the launch traced here: 279 us
  Pallas kernels  143 us (51%)
  starting transfers between devices  63.1 us (22%)
  local copies, waits for them, and re-layouts  38.2 us (14%)
  waiting for transfers between devices  17.5 us (6%)
  other arithmetic  8.66 us (3%)
  blocking collectives  6.8 us (2%)
    pallas_call x35, Pallas kernels, call(): pl.pallas_call(body, grid_spec=pltpu.PrefetchScalarGridSpec(num_scalar_pr...  143 us
    ppermute x47, starting transfers between devices, swap(): lax.ppermute(x, axis, [(i, i ^ bit) for i in range(lax.axis_size(axis))])  55.4 us
    unnamed x170, local copies, waits for them, and re-layouts  24.4 us
    ppermute x47, waiting for transfers between devices, swap(): lax.ppermute(x, axis, [(i, i ^ bit) for i in range(lax.axis_size(axis))])  17.4 us
    ppermute x4, starting transfers between devices, shift(): lax.ppermute(x, axis, [(i, i + distance) for i in range(n) if 0 <= i + di...  7.72 us
    all_gather x1, blocking collectives, shards(): stats_all = lax.all_gather(stats, 'head')  6.8 us
  transfers between devices with their start and end apart: 51, of which 11 were waited for; matrix products, arithmetic and copies ran while one was open for 9% of the time, Pallas kernels for 44%

profile of v2, /device:TPU:0, one launch (start us, length us, event | category | flops | bytes accessed | tf_op | source)
XLA Modules:
  0.0 279.0 jit_solution(13557678999911232746)
XLA Ops:
  7.9 3.6 %collective-permute-start.3 = (bf16[192,128]{1,0:T(8,128)(2,1)S(1)}, bf16[192,128]{1,0:T(8,128)(2,1)S(1)}, u32[]{:S(2)}, u32[]{:S(2)}) collective-permute-start(bf16[192,128]{1,0:T(8,128)(2,1)S(1)} %fusion.12), channel_id=1, source_target_pairs={{0,4},{4,8},{8,12},{12,16},{16,20},{20,24},{24,28},{1,5},{5,9},{9,... | collective-permute-start | bytes 147464 | tf_op jit(solution)/shard_map/ppermute | solution.py:28
  23.2 15.3 %shard_map.288 = (bf16[4,768,256]{2,1,0:T(8,128)(2,1)}, f32[4,1,256]{2,1,0:T(1,128)}, bf16[768,128]{1,0:T(8,128)(2,1)}, bf16[4,272,384]{2,1,0:T(8,128)(2,1)}, bf...) custom-call(s32[2]{0:T(128)} %pad_add_fusion.refs_0_, ...), custom_call_target="tpu_custom_call" | custom-call | flops 149999992832 | bytes 45000000 | tf_op jit(solution)/shard_map/pallas_call | solution.py:926
  42.4 6.0 %shard_map.289.refs_3_.refs_4_ = f32[4,256,384]{2,1,0:T(8,128)} custom-call(s32[2]{0:T(128)} %pad_add_fusion.refs_0_, s32[4,4]{1,0:T(4,128)} %refs_1_.27, bf16[4,256,640]{2,1,0:T(8,128)(2,1)} %get-tuple-element.100.refs_2_.refs_3_, f32[4,256,128]{2,1,0:T(8,128)} %get-tuple-element.101.refs_3_.refs_4_.refs_2_, f32[768,1]{1,0:T(8,128)} %get-tuple-element.102.refs_4_.refs_12_), custom_call_target="tpu_custom_call" | custom-call | flops 60000002048 | bytes 18000000 | tf_op jit(solution)/shard_map/pallas_call | solution.py:926
  56.2 5.5 %shard_map.291 = (bf16[4,768,256]{2,1,0:T(8,128)(2,1)}, f32[4,256,384]{2,1,0:T(8,128)}) custom-call(s32[2]{0:T(128)} %pad_add_fusion.refs_0_, s32[4,4]{1,0:T(4,128)} %refs_1_.27, bf16[4,192,256]{2,1,0:T(8,128)(2,1)} %bitcast.64, bf16[4,192,256]{2,1,0:T(8,128)(2,1)} %copy-done.68, bf16[4,192,256]{2,1,0:T(8,128)(2,1)} %copy-done.69, ...), custom_call_target="tpu_custom_call" | custom-call | flops 54999998464 | bytes 16500000 | tf_op jit(solution)/shard_map/pallas_call | solution.py:926
  67.8 7.1 %shard_map.293 = (bf16[4,256,384]{2,1,0:T(8,128)(2,1)}, f32[4,256,384]{2,1,0:T(8,128)}, f32[4,256,64]{2,1,0:T(8,128)}) custom-call(s32[2]{0:T(128)} %pad_add_fusion.refs_0_, s32[4,4]{1,0:T(4,128)} %refs_1_.27, bf16[4,768,256]{2,1,0:T(8,128)(2,1)} %get-tuple-element.109.refs_2_.refs_10_.refs_9_.refs_7_, bf16[768,384]{1,0:T(8,128)(2,1)} %refs_8_.1, ...), custom_call_target="tpu_custom_call" | custom-call | flops 70000001024 | bytes 21000000 | tf_op jit(solution)/shard_map/pallas_call | solution.py:926
  88.1 6.6 %shard_map.295 = (f32[4,256,384]{2,1,0:T(8,128)}, f32[4,2,256]{2,1,0:T(2,128)}) custom-call(s32[2]{0:T(128)} %pad_add_fusion.refs_0_, s32[4,4]{1,0:T(4,128)} %refs_1_.27, bf16[4,256,640]{2,1,0:T(8,128)(2,1)} %get-tuple-element.100.refs_2_.refs_3_, f32[4,256,128]{2,1,0:T(8,128)} %get-tuple-element.101.refs_3_.refs_4_.refs_2_, ...), custom_call_target="tpu_custom_call" | custom-call | flops 65999998976 | bytes 19800000 | tf_op jit(solution)/shard_map/pallas_call | solution.py:926
  94.7 6.8 %all-gather = f32[16,2,256]{2,1,0:T(2,128)} all-gather(f32[4,2,256]{2,1,0:T(2,128)} %get-tuple-element.116.refs_10_), channel_id=2, replica_groups=mesh['seq'=8,'head'=4] {'head'}, dimensions={0}, use_global_device_ids=true | all-gather | bytes 40960 | tf_op jit(solution)/shard_map/all_gather | solution.py:1234
  101.5 8.3 %shard_map.296 = (f32[4,256,384]{2,1,0:T(8,128)}, bf16[4,256,384]{2,1,0:T(8,128)(2,1)}, bf16[4,256,384]{2,1,0:T(8,128)(2,1)}, s16[2,400,128]{2,1,0:T(8,128)(2,1)...) custom-call(s32[2]{0:T(128)} %pad_add_fusion.refs_0_, s32[4,4]{1,0:T(4,128)} %refs_1_.27, f32[4,4,2,256]{3,2,1,0:T(2,128)} %bitcast.55, ...), custom_call_target="tpu_custom_call" | custom-call | flops 83000000512 | bytes 24900000 | tf_op jit(solution)/shard_map/pallas_call | solution.py:926
  109.8 2.7 collective-permute-start.19
  112.5 6.9 %shard_map.297 = (f32[4,192,256]{2,1,0:T(8,128)}, f32[4,192,256]{2,1,0:T(8,128)}, bf16[2,4,192,256]{3,2,1,0:T(8,128)(2,1)}, f32[384,384]{1,0:T(8,128)}, bf16[384,384]{1,0:T(8,128)(2,1)}) custom-call(s32[2]{0:T(128)} %pad_add_fusion.refs_0_, s32[4,4]{1,0:T(4,128)} %refs_1_.27, bf16[4,256,384]{2,1,0:T(8,128)(2,1)} %get-tuple-element.118.refs_2_, ...), custom_call_target="tpu_custom_call" | custom-call | flops 67999997952 | bytes 20400000 | tf_op jit(solution)/shard_map/pallas_call | solution.py:926
  123.8 5.4 %shard_map.299 = (f32[384,384]{1,0:T(8,128)}, bf16[384,384]{1,0:T(8,128)(2,1)}) custom-call(s32[2]{0:T(128)} %pad_add_fusion.refs_0_, s32[4,4]{1,0:T(4,128)} %refs_1_.27, bf16[4,768,256]{2,1,0:T(8,128)(2,1)} %get-tuple-element.109.refs_2_.refs_10_.refs_9_.refs_7_, bf16[4,256,384]{2,1,0:T(8,128)(2,1)} %get-tuple-element.128.refs_3_.refs_4_, ...), custom_call_target="tpu_custom_call" | custom-call | flops 52999999488 | bytes 15900000 | tf_op jit(solution)/shard_map/pallas_call | solution.py:926
  132.9 3.2 %collective-permute-start.21 = (s16[2,400,128]{2,1,0:T(8,128)(2,1)S(1)}, s16[2,400,128]{2,1,0:T(8,128)(2,1)S(1)}, u32[]{:S(2)}, u32[]{:S(2)}) collective-permute-start(s16[2,400,128]{2,1,0:T(8,128)(2,1)S(1)} %get-tuple-element.130.refs_8_), channel_id=1, source_target_pairs={{0,16},{4,20},{8,24},{12,28},{16,0},{20,4},{24,8},{28,12},{1,17},{... | collective-permute-start | bytes 614408 | tf_op jit(solution)/shard_map/ppermute | solution.py:23
  136.1 12.0 %shard_map.301 = (f32[4,256,384]{2,1,0:T(8,128)}, f32[4,256,256]{2,1,0:T(8,128)}, f32[4,256,128]{2,1,0:T(8,128)}) custom-call(s32[2]{0:T(128)} %pad_add_fusion.refs_0_, s32[4,4]{1,0:T(4,128)} %refs_1_.27, bf16[4,256,640]{2,1,0:T(8,128)(2,1)} %get-tuple-element.100.refs_2_.refs_3_, f32[4,256,128]{2,1,0:T(8,128)} %get-tuple-element.101.refs_3_.refs_4_.refs_2_, ...), custom_call_target="tpu_custom_call" | custom-call | flops 120000004096 | bytes 36000000 | tf_op jit(solution)/shard_map/pallas_call | solution.py:926
  157.5 6.4 %shard_map.304 = (f32[4,256,128]{2,1,0:T(8,128)}, f32[4,256,128]{2,1,0:T(8,128)}) custom-call(s32[2]{0:T(128)} %pad_add_fusion.refs_0_, s32[4,4]{1,0:T(4,128)} %refs_1_.27, bf16[4,256,640]{2,1,0:T(8,128)(2,1)} %get-tuple-element.100.refs_2_.refs_3_, f32[4,256,128]{2,1,0:T(8,128)} %get-tuple-element.101.refs_3_.refs_4_.refs_2_, ...), custom_call_target="tpu_custom_call" | custom-call | flops 64000000000 | bytes 19200000 | tf_op jit(solution)/shard_map/pallas_call | solution.py:926
  168.6 12.5 %shard_map.307 = (bf16[4,256,384]{2,1,0:T(8,128)(2,1)}, bf16[128,384]{1,0:T(8,128)(2,1)}, f32[4,256,128]{2,1,0:T(8,128)}, f32[384,384]{1,0:T(8,128)}, bf16[384,384]{1,0:T(8,128)(2,1)}, /*index=5*/f32[8,384]{1,0:T(8,128)}) custom-call(s32[2]{0:T(128)} %pad_add_fusion.refs_0_, s32[4,4]{1,0:T(4,128)} %refs_1_.27, ...), custom_call_target="tpu_custom_call" | custom-call | flops 124999999488 | bytes 37500000 | tf_op jit(solution)/shard_map/pallas_call | solution.py:926
  186.1 5.1 %collective-permute-start.33 = (bf16[192,384]{1,0:T(8,128)(2,1)S(1)}, bf16[192,384]{1,0:T(8,128)(2,1)S(1)}, u32[]{:S(2)}, u32[]{:S(2)}) collective-permute-start(bf16[192,384]{1,0:T(8,128)(2,1)S(1)} %shard_map.308.refs_11_.refs_1_), channel_id=1, source_target_pairs={{0,16},{4,20},{8,24},{12,28},{16,0},{20,4},{24,8},{28,12},{1,17},{... | collective-permute-start | bytes 442376 | tf_op jit(solution)/shard_map/ppermute | solution.py:23
  191.9 3.0 %collective-permute-start.35 = (bf16[384,384]{1,0:T(8,128)(2,1)}, bf16[384,384]{1,0:T(8,128)(2,1)}, u32[]{:S(2)}, u32[]{:S(2)}) collective-permute-start(bf16[384,384]{1,0:T(8,128)(2,1)} %get-tuple-element.164), channel_id=1, source_target_pairs={{0,4},{4,0},{8,12},{12,8},{16,20},{20,16},{24,28},{28,24},{1,5},{5... | collective-permute-start | bytes 884744 | tf_op jit(solution)/shard_map/ppermute | solution.py:23
  195.5 6.3 %shard_map.309 = (bf16[4,256,64]{2,1,0:T(8,128)(2,1)}, f32[64,384]{1,0:T(8,128)}, bf16[64,384]{1,0:T(8,128)(2,1)}, f32[8,64]{1,0:T(8,128)}) custom-call(s32[2]{0:T(128)} %pad_add_fusion.refs_0_, s32[4,4]{1,0:T(4,128)} %refs_1_.27, f32[2,256,128]{2,1,0:T(8,128)} %copy-done.39, f32[2,256,128]{2,1,0:T(8,128)} %copy-done.71, f32[4,16,128]{2,1,0:T(8,128)} %copy-done.81, ...), custom_call_target="tpu_custom_call" | custom-call | flops 62999998464 | bytes 18900000 | tf_op jit(solution)/shard_map/pallas_call | solution.py:926
  201.9 7.9 %shard_map.310 = (bf16[4,256,128]{2,1,0:T(8,128)(2,1)}, f32[16,768]{1,0:T(8,128)}) custom-call(s32[2]{0:T(128)} %pad_add_fusion.refs_0_, s32[4,4]{1,0:T(4,128)} %refs_1_.27, f32[4,256,128]{2,1,0:T(8,128)} %get-tuple-element.101.refs_3_.refs_4_.refs_2_, f32[4,256,128]{2,1,0:T(8,128)} %get-tuple-element.133.refs_5_.refs_3_, ...), custom_call_target="tpu_custom_call" | custom-call | flops 80000000000 | bytes 24000000 | tf_op jit(solution)/shard_map/pallas_call | solution.py:926
  215.7 8.3 %shard_map.312 = (f32[4,192,256]{2,1,0:T(8,128)}, f32[4,192,256]{2,1,0:T(8,128)}, bf16[2,4,208,256]{3,2,1,0:T(8,128)(2,1)}, f32[4,8,256]{2,1,0:T(8,128)}) custom-call(s32[2]{0:T(128)} %pad_add_fusion.refs_0_, s32[4,4]{1,0:T(4,128)} %refs_1_.27, bf16[4,256,384]{2,1,0:T(8,128)(2,1)} %get-tuple-element.147.refs_2_, ...), custom_call_target="tpu_custom_call" | custom-call | flops 83000000512 | bytes 24900000 | tf_op jit(solution)/shard_map/pallas_call | solution.py:926
  229.6 3.7 %shard_map.314 = (f32[4,192,256]{2,1,0:T(8,128)}, bf16[4,208,256]{2,1,0:T(8,128)(2,1)}, f32[4,8,256]{2,1,0:T(8,128)}) custom-call(f32[4,192,256]{2,1,0:T(8,128)} %get-tuple-element.158.refs_0_, f32[4,192,256]{2,1,0:T(8,128)} %get-tuple-element.159.refs_1_, bf16[2,4,208,256]{3,2,1,0:T(8,128)(2,1)} %copy-done.61, ...), custom_call_target="tpu_custom_call" | custom-call | flops 38000001024 | bytes 11400000 | tf_op jit(solution)/shard_map/pallas_call | solution.py:926
  236.4 2.7 collective-permute-start.42
  247.9 5.9 %collective-permute-done.38.refs_1_ = bf16[4,208,256]{2,1,0:T(8,128)(2,1)S(1)} collective-permute-done((bf16[4,208,256]{2,1,0:T(8,128)(2,1)S(1)}, bf16[4,208,256]{2,1,0:T(8,128)(2,1)S(1)}, u32[]{:S(2)}, u32[]{:S(2)}) %collective-permute-start.38) | collective-permute-done | bytes 426016 | tf_op jit(solution)/shard_map/ppermute | solution.py:23
  254.6 4.0 %shard_map.318 = (f32[4,192,256]{2,1,0:T(8,128)}, f32[8,256]{1,0:T(8,128)}) custom-call(f32[4,192,256]{2,1,0:T(8,128)} %get-tuple-element.167.refs_0_, bf16[4,208,256]{2,1,0:T(8,128)(2,1)} %copy-done.63, f32[4,8,256]{2,1,0:T(8,128)} %get-tuple-element.169.refs_3_.refs_2_, bf16[4,192,256]{2,1,0:T(8,128)(2,1)} %bitcast.53, ...), custom_call_target="tpu_custom_call" | custom-call | flops 40000000000 | bytes 12000000 | tf_op jit(solution)/shard_map/pallas_call | solution.py:926
  (314 shorter events, 122.0 us)
Async XLA Ops:
  0.7 21.0 %collective-permute-start = (bf16[4,192,256]{2,1,0:T(8,128)(2,1)}, bf16[4,192,256]{2,1,0:T(8,128)(2,1)S(1)}, u32[]{:S(2)}, u32[]{:S(2)}) collective-permute-start(bf16[4,192,256]{2,1,0:T(8,128)(2,1)} %bitcast.49), channel_id=1, source_target_pairs={{0,1},{1,0},{2,3},{3,2},{4,5},{5,4},{6,7},{7,6},{8,9},{9,8},{10,11... | collective-permute-start | bytes 1179656 | tf_op jit(solution)/shard_map/ppermute | solution.py:23
  1.2 12.8 %collective-permute-start.1 = (bf16[4,192,256]{2,1,0:T(8,128)(2,1)}, bf16[4,192,256]{2,1,0:T(8,128)(2,1)S(1)}, u32[]{:S(2)}, u32[]{:S(2)}) collective-permute-start(bf16[4,192,256]{2,1,0:T(8,128)(2,1)} %bitcast.50), channel_id=1, source_target_pairs={{0,2},{1,3},{2,0},{3,1},{4,6},{5,7},{6,4},{7,5},{8,10},{9,11},{10,... | collective-permute-start | bytes 1179656 | tf_op jit(solution)/shard_map/ppermute | solution.py:23
  6.3 15.3 %collective-permute-start.7 = (bf16[64,896]{1,0:T(8,128)(2,1)S(1)}, bf16[64,896]{1,0:T(8,128)(2,1)S(1)}, u32[]{:S(2)}, u32[]{:S(2)}) collective-permute-start(bf16[64,896]{1,0:T(8,128)(2,1)S(1)} %fusion.5.refs_10_), channel_id=1, source_target_pairs={{0,1},{1,0},{2,3},{3,2},{4,5},{5,4},{6,7},{7,6},{8,9},{9,8},{10,11... | collective-permute-start | bytes 344072 | tf_op jit(solution)/shard_map/ppermute | solution.py:23
  6.5 11.4 %collective-permute-start.8 = (bf16[64,896]{1,0:T(8,128)(2,1)S(1)}, bf16[64,896]{1,0:T(8,128)(2,1)S(1)}, u32[]{:S(2)}, u32[]{:S(2)}) collective-permute-start(bf16[64,896]{1,0:T(8,128)(2,1)S(1)} %fusion.5.refs_10_), channel_id=1, source_target_pairs={{0,2},{1,3},{2,0},{3,1},{4,6},{5,7},{6,4},{7,5},{8,10},{9,11},{10,... | collective-permute-start | bytes 344072 | tf_op jit(solution)/shard_map/ppermute | solution.py:23
  38.5 16.2 %collective-permute-start.12 = (bf16[4,192,256]{2,1,0:T(8,128)(2,1)S(1)}, bf16[4,192,256]{2,1,0:T(8,128)(2,1)S(1)}, u32[]{:S(2)}, u32[]{:S(2)}) collective-permute-start(bf16[4,192,256]{2,1,0:T(8,128)(2,1)S(1)} %bitcast.66), channel_id=1, source_target_pairs={{0,1},{1,0},{2,3},{3,2},{4,5},{5,4},{6,7},{7,6},{8,9},{9,8},{10,11... | collective-permute-start | bytes 1179656 | tf_op jit(solution)/shard_map/ppermute | solution.py:23
  65.1 12.2 %collective-permute-start.15 = (s16[2,400,128]{2,1,0:T(8,128)(2,1)S(1)}, s16[2,400,128]{2,1,0:T(8,128)(2,1)S(1)}, u32[]{:S(2)}, u32[]{:S(2)}) collective-permute-start(s16[2,400,128]{2,1,0:T(8,128)(2,1)S(1)} %get-tuple-element.107.refs_8_), channel_id=1, source_target_pairs={{0,16},{4,20},{8,24},{12,28},{16,0},{20,4},{24,8},{28,12},{1,17},{... | collective-permute-start | bytes 614408 | tf_op jit(solution)/shard_map/ppermute | solution.py:23
  86.1 100.0 %collective-permute-start.31 = (f32[4,16,64]{2,1,0:T(8,128)}, f32[4,16,64]{2,1,0:T(8,128)}, u32[]{:S(2)}, u32[]{:S(2)}) collective-permute-start(f32[4,16,64]{2,1,0:T(8,128)} %slice.63), channel_id=1, source_target_pairs={{4,0},{8,4},{12,8},{16,12},{20,16},{24,20},{28,24},{5,1},{9,5},{13... | collective-permute-start | bytes 49160 | tf_op jit(solution)/shard_map/ppermute | solution.py:28
  119.4 34.5 %collective-permute-start.17 = (bf16[2,4,192,256]{3,2,1,0:T(8,128)(2,1)}, bf16[2,4,192,256]{3,2,1,0:T(8,128)(2,1)}, u32[]{:S(2)}, u32[]{:S(2)}) collective-permute-start(bf16[2,4,192,256]{3,2,1,0:T(8,128)(2,1)} %get-tuple-element.122), channel_id=1, source_target_pairs={{0,1},{1,0},{2,3},{3,2},{4,5},{5,4},{6,7},{7,6},{8,9},{9,8},{10,11... | collective-permute-start | bytes 2359304 | tf_op jit(solution)/shard_map/ppermute | solution.py:23
  119.5 28.6 %collective-permute-start.22 = (bf16[384,384]{1,0:T(8,128)(2,1)}, bf16[384,384]{1,0:T(8,128)(2,1)}, u32[]{:S(2)}, u32[]{:S(2)}) collective-permute-start(bf16[384,384]{1,0:T(8,128)(2,1)} %get-tuple-element.134), channel_id=1, source_target_pairs={{0,4},{4,0},{8,12},{12,8},{16,20},{20,16},{24,28},{28,24},{1,5},{5... | collective-permute-start | bytes 884744 | tf_op jit(solution)/shard_map/ppermute | solution.py:23
  129.2 19.0 %collective-permute-start.23 = (bf16[384,384]{1,0:T(8,128)(2,1)}, bf16[384,384]{1,0:T(8,128)(2,1)S(1)}, u32[]{:S(2)}, u32[]{:S(2)}) collective-permute-start(bf16[384,384]{1,0:T(8,128)(2,1)} %get-tuple-element.135), channel_id=1, source_target_pairs={{0,4},{4,0},{8,12},{12,8},{16,20},{20,16},{24,28},{28,24},{1,5},{5... | collective-permute-start | bytes 884744 | tf_op jit(solution)/shard_map/ppermute | solution.py:23
  132.9 15.3 %collective-permute-start.21 = (s16[2,400,128]{2,1,0:T(8,128)(2,1)S(1)}, s16[2,400,128]{2,1,0:T(8,128)(2,1)S(1)}, u32[]{:S(2)}, u32[]{:S(2)}) collective-permute-start(s16[2,400,128]{2,1,0:T(8,128)(2,1)S(1)} %get-tuple-element.130.refs_8_), channel_id=1, source_target_pairs={{0,16},{4,20},{8,24},{12,28},{16,0},{20,4},{24,8},{28,12},{1,17},{... | collective-permute-start | bytes 614408 | tf_op jit(solution)/shard_map/ppermute | solution.py:23
  152.4 11.5 %collective-permute-start.26 = (bf16[384,384]{1,0:T(8,128)(2,1)S(1)}, bf16[384,384]{1,0:T(8,128)(2,1)S(1)}, u32[]{:S(2)}, u32[]{:S(2)}) collective-permute-start(bf16[384,384]{1,0:T(8,128)(2,1)S(1)} %get-tuple-element.144), channel_id=1, source_target_pairs={{0,8},{4,12},{8,0},{12,4},{16,24},{20,28},{24,16},{28,20},{1,9},{5... | collective-permute-start | bytes 884744 | tf_op jit(solution)/shard_map/ppermute | solution.py:23
  155.8 83.6 %collective-permute-start.18 = (bf16[4,192,256]{2,1,0:T(8,128)(2,1)}, bf16[4,192,256]{2,1,0:T(8,128)(2,1)}, u32[]{:S(2)}, u32[]{:S(2)}) collective-permute-start(bf16[4,192,256]{2,1,0:T(8,128)(2,1)} %fusion), channel_id=1, source_target_pairs={{0,2},{1,3},{2,0},{3,1},{4,6},{5,7},{6,4},{7,5},{8,10},{9,11},{10,... | collective-permute-start | bytes 1179656 | tf_op jit(solution)/shard_map/ppermute | solution.py:23
  165.6 17.1 %collective-permute-start.32 = (bf16[192,384]{1,0:T(8,128)(2,1)S(1)}, bf16[192,384]{1,0:T(8,128)(2,1)S(1)}, u32[]{:S(2)}, u32[]{:S(2)}) collective-permute-start(bf16[192,384]{1,0:T(8,128)(2,1)S(1)} %get-tuple-element.153), channel_id=1, source_target_pairs={{0,16},{4,20},{8,24},{12,28},{16,0},{20,4},{24,8},{28,12},{1,17},{... | collective-permute-start | bytes 442376 | tf_op jit(solution)/shard_map/ppermute | solution.py:23
  167.3 16.2 %collective-permute-start.29 = (f32[4,16,128]{2,1,0:T(8,128)S(1)}, f32[4,16,128]{2,1,0:T(8,128)S(1)}, u32[]{:S(2)}, u32[]{:S(2)}) collective-permute-start(f32[4,16,128]{2,1,0:T(8,128)S(1)} %get-tuple-element.146.refs_14_), channel_id=1, source_target_pairs={{4,0},{8,4},{12,8},{16,12},{20,16},{24,20},{28,24},{5,1},{9,5},{13... | collective-permute-start | bytes 98312 | tf_op jit(solution)/shard_map/ppermute | solution.py:28
  181.1 33.0 %collective-permute-start.27 = (bf16[128,384]{1,0:T(8,128)(2,1)}, bf16[128,384]{1,0:T(8,128)(2,1)}, u32[]{:S(2)}, u32[]{:S(2)}) collective-permute-start(bf16[128,384]{1,0:T(8,128)(2,1)} %get-tuple-element.148), channel_id=1, source_target_pairs={{4,0},{8,4},{12,8},{16,12},{20,16},{24,20},{28,24},{5,1},{9,5},{13... | collective-permute-start | bytes 294920 | tf_op jit(solution)/shard_map/ppermute | solution.py:28
  182.7 12.2 %collective-permute-start.28 = (f32[2,256,128]{2,1,0:T(8,128)S(1)}, f32[2,256,128]{2,1,0:T(8,128)S(1)}, u32[]{:S(2)}, u32[]{:S(2)}) collective-permute-start(f32[2,256,128]{2,1,0:T(8,128)S(1)} %get-tuple-element.152), channel_id=1, source_target_pairs={{0,2},{1,3},{2,0},{3,1},{4,6},{5,7},{6,4},{7,5},{8,10},{9,11},{10,... | collective-permute-start | bytes 786440 | tf_op jit(solution)/shard_map/ppermute | solution.py:23
  186.1 23.8 %collective-permute-start.33 = (bf16[192,384]{1,0:T(8,128)(2,1)S(1)}, bf16[192,384]{1,0:T(8,128)(2,1)S(1)}, u32[]{:S(2)}, u32[]{:S(2)}) collective-permute-start(bf16[192,384]{1,0:T(8,128)(2,1)S(1)} %shard_map.308.refs_11_.refs_1_), channel_id=1, source_target_pairs={{0,16},{4,20},{8,24},{12,28},{16,0},{20,4},{24,8},{28,12},{1,17},{... | collective-permute-start | bytes 442376 | tf_op jit(solution)/shard_map/ppermute | solution.py:23
  191.9 32.2 %collective-permute-start.35 = (bf16[384,384]{1,0:T(8,128)(2,1)}, bf16[384,384]{1,0:T(8,128)(2,1)}, u32[]{:S(2)}, u32[]{:S(2)}) collective-permute-start(bf16[384,384]{1,0:T(8,128)(2,1)} %get-tuple-element.164), channel_id=1, source_target_pairs={{0,4},{4,0},{8,12},{12,8},{16,20},{20,16},{24,28},{28,24},{1,5},{5... | collective-permute-start | bytes 884744 | tf_op jit(solution)/shard_map/ppermute | solution.py:23
  201.8 22.3 %collective-permute-start.36 = (bf16[64,384]{1,0:T(8,128)(2,1)}, bf16[64,384]{1,0:T(8,128)(2,1)}, u32[]{:S(2)}, u32[]{:S(2)}) collective-permute-start(bf16[64,384]{1,0:T(8,128)(2,1)} %get-tuple-element.165), channel_id=1, source_target_pairs={{0,4},{4,0},{8,12},{12,8},{16,20},{20,16},{24,28},{28,24},{1,5},{5... | collective-permute-start | bytes 147464 | tf_op jit(solution)/shard_map/ppermute | solution.py:23
  209.9 14.3 %collective-permute-start.37 = (f32[16,768]{1,0:T(8,128)}, f32[16,768]{1,0:T(8,128)S(1)}, u32[]{:S(2)}, u32[]{:S(2)}) collective-permute-start(f32[16,768]{1,0:T(8,128)} %get-tuple-element.157.refs_3_.refs_5_), channel_id=1, source_target_pairs={{0,4},{4,0},{8,12},{12,8},{16,20},{20,16},{24,28},{28,24},{1,5},{5... | collective-permute-start | bytes 147464 | tf_op jit(solution)/shard_map/ppermute | solution.py:23
  214.1 19.2 %collective-permute-start.41 = (bf16[384,384]{1,0:T(8,128)(2,1)}, bf16[384,384]{1,0:T(8,128)(2,1)S(1)}, u32[]{:S(2)}, u32[]{:S(2)}) collective-permute-start(bf16[384,384]{1,0:T(8,128)(2,1)} %shard_map.311.refs_13_.refs_1_), channel_id=1, source_target_pairs={{0,8},{4,12},{8,0},{12,4},{16,24},{20,28},{24,16},{28,20},{1,9},{5... | collective-permute-start | bytes 884744 | tf_op jit(solution)/shard_map/ppermute | solution.py:23
  241.5 21.4 %collective-permute-start.47 = (bf16[768,384]{1,0:T(8,128)(2,1)S(1)}, bf16[768,384]{1,0:T(8,128)(2,1)S(1)}, u32[]{:S(2)}, u32[]{:S(2)}) collective-permute-start(bf16[768,384]{1,0:T(8,128)(2,1)S(1)} %shard_map.315.refs_5_.refs_1_), channel_id=1, source_target_pairs={{0,4},{4,0},{8,12},{12,8},{16,20},{20,16},{24,28},{28,24},{1,5},{5... | collective-permute-start | bytes 1769480 | tf_op jit(solution)/shard_map/ppermute | solution.py:23
  246.1 13.1 %collective-permute-start.48 = (bf16[112,384]{1,0:T(8,128)(2,1)S(1)}, bf16[112,384]{1,0:T(8,128)(2,1)S(1)}, u32[]{:S(2)}, u32[]{:S(2)}) collective-permute-start(bf16[112,384]{1,0:T(8,128)(2,1)S(1)} %get-tuple-element.179.refs_1_), channel_id=1, source_target_pairs={{0,16},{4,20},{8,24},{12,28},{16,0},{20,4},{24,8},{28,12},{1,17},{... | collective-permute-start | bytes 258056 | tf_op jit(solution)/shard_map/ppermute | solution.py:23
  (111 other events, 605.2 us)

commit v3 on v2

--- a/solution.py
+++ b/solution.py
@@ -19,13 +19,19 @@
 GROUP = 16
 
 
+def permuted(x, axis, route):
+    y = lax.ppermute(x, axis, route)
+    order.near.append(y)
+    return y
+
+
 def swap(x, axis, bit):
-    return lax.ppermute(x, axis, [(i, i ^ bit) for i in range(lax.axis_size(axis))])
+    return permuted(x, axis, [(i, i ^ bit) for i in range(lax.axis_size(axis))])
 
 
 def shift(x, axis, distance):
     n = lax.axis_size(axis)
-    return lax.ppermute(x, axis, [(i, i + distance) for i in range(n) if 0 <= i + distance < n])
+    return permuted(x, axis, [(i, i + distance) for i in range(n) if 0 <= i + distance < n])
 
 
 def head_pieces(x):
@@ -909,37 +915,58 @@
 
 class Order:
     def __init__(self):
-        self.last = ()
+        self.clear()
+
+    def clear(self):
+        self.last, self.near = (), []
+
+    def placed(self, x):
+        return pltpu.with_memory_space_constraint(x, pltpu.VMEM) if self.holds(x) else x
+
+    def holds(self, x):
+        return any(x is y for y in self.near)
 
 
 order = Order()
 
 
-def call(kernel, grid, in_specs, out_specs, out_shape, scratch, prefetch, *args, limit=60, wait=(), us=1):
+def call(
+    kernel, grid, in_specs, out_specs, out_shape, scratch, prefetch, *args, limit=20, wait=(), us=1,
+    out=False,
+):
     first = len(prefetch) + len(args)
     held = order.last + tuple(wait)
     late = len(held)
+    single = not isinstance(out_shape, (list, tuple))
+    out_specs, out_shape = ([out_specs], [out_shape]) if single else (list(out_specs), list(out_shape))
+    token = jax.ShapeDtypeStruct((8, LANES), f32)
+    count = len(out_shape)
 
     def body(*refs):
-        kernel(*refs[:first], *refs[first + late :])
-
-    outs = pl.pallas_call(
+        ins, rest = refs[:first], refs[first + late :]
+        kernel(*ins, *rest[:count], *rest[count + 1 :])
+
+    *outs, order_out = pl.pallas_call(
         body,
         grid_spec=pltpu.PrefetchScalarGridSpec(
             num_scalar_prefetch=len(prefetch),
             grid=grid,
             in_specs=list(in_specs) + [pl.BlockSpec(memory_space=pl.ANY)] * late,
-            out_specs=out_specs,
+            out_specs=out_specs + [whole_spec(token.shape)],
             scratch_shapes=scratch,
         ),
-        out_shape=out_shape,
+        out_shape=(out_shape if out else [pltpu.VMEM(x.shape, x.dtype) for x in out_shape])
+        + [pltpu.VMEM(token.shape, token.dtype)],
         compiler_params=pltpu.CompilerParams(vmem_limit_bytes=limit * MIB),
         cost_estimate=pl.CostEstimate(
             flops=int(us * 10e9), bytes_accessed=int(us * 3e6), transcendentals=0
         ),
-    )(*prefetch, *args, *held)
-    order.last = (min(jax.tree.leaves(outs), key=lambda x: x.size),)
-    return outs
+    )(*prefetch, *[order.placed(x) for x in args], *[order.placed(x) for x in held])
+    order.last = (order_out,)
+    order.near.append(order_out)
+    if not out:
+        order.near += outs
+    return outs[0] if single else outs
 
 
 def shape(*dims_and_type):
@@ -963,7 +990,7 @@
     work()
     total = call(
         functools.partial(pair_kernel, dims, rev), (1,), [spec, spec], spec, pay, [], (meta,),
-        keep, other, limit=8,
+        keep, other,
     )
     before = None
     for bit in range(1, bits):
@@ -974,13 +1001,13 @@
             total, before = call(
                 functools.partial(cube_kernel, dims, rev, bit, before is None), (1,),
                 [spec] * (2 + len(extra)), [spec, spec], [pay, pay], [], (meta,),
-                total, got, *extra, limit=8,
+                total, got, *extra,
             )
         else:
             own, back = call(
                 functools.partial(last_kernel, dims, rev, bit, before is None), (1,),
                 [spec] * (3 + len(extra)), [spec, spec], [pay, pay], [],
-                (meta,), keep, other, got, *extra, limit=8, wait=waits(),
+                (meta,), keep, other, got, *extra, wait=waits(),
             )
     recv = swap(back, "seq", 1)
     while beside:
@@ -1018,7 +1045,7 @@
         outs = call(
             functools.partial(add_kernel, bit, halve, self.segs, len(self.keep), bool(small)), (1,),
             [whole_spec(x.shape) for x in ins], [whole_spec(x.shape) for x in out], out, [],
-            (meta,), *ins, limit=12,
+            (meta,), *ins,
         )
         if small:
             self.small = outs[-1]
@@ -1042,7 +1069,7 @@
         spec = whole_spec((rows, cols))
         self.keep = [call(
             functools.partial(join_kernel, self.bit, self.segs), (1,), [spec, spec],
-            whole_spec(both.shape), both, [], (meta,), self.keep[0], self.got[0], limit=12,
+            whole_spec(both.shape), both, [], (meta,), self.keep[0], self.got[0],
         )]
         self.segs = [2 * rows for rows in self.segs]
 
@@ -1054,8 +1081,7 @@
         return call(
             functools.partial(result_kernel, self.segs, ways), (1,), [spec, spec],
             [whole_spec(x.shape) for x in out], out, [], (meta,), self.keep[0], self.got[0],
-            limit=16,
-            us=2,
+            out=True, us=2,
         )
 
 
@@ -1099,7 +1125,7 @@
     pre = (meta, lengths)
     grid = (packs,)
 
-    order.last = ()
+    order.clear()
     tokens = jnp.swapaxes(tokens_in, 1, 2)
     cotangent = jnp.swapaxes(out_grad, 1, 2)
     token_pieces = head_pieces(tokens)
@@ -1340,7 +1366,6 @@
         [],
         (meta,),
         share_own, share_near,
-        limit=8,
     )
     bc_recv = swap(bc_send, "head", 2)
     bc_edge = shift(bc_edge, "seq", -1)
@@ -1478,7 +1503,7 @@
         [],
         (),
         gn_own, gn_far, extra, tokens, inv, norm_gain.astype(f32)[:, None], cotangent,
-        us=4,
+        us=4, out=True,
     )
     in_grad = jnp.swapaxes(in_grad, 1, 2)
     advance(late_sum, meta)

time: 282 us -> 236 us (0.84)
  Pallas kernels: 143 us -> 99 us
  local copies, waits for them, and re-layouts: 38.2 us -> 17.9 us
  waiting for transfers between devices: 17.5 us -> 36 us
  starting transfers between devices: 63.1 us -> 68.9 us
    pallas_call x35, Pallas kernels: 143 us -> 99 us  [call(): pl.pallas_call(body, grid_spec=pltpu.PrefetchScalarGridSpec(num_scalar_pr...]
    ppermute x51, waiting for transfers between devices: 17.5 us -> 36 us  [permuted(): y = lax.ppermute(x, axis, route)]
    unnamed x170 -> x108, local copies, waits for them, and re-layouts: 24.4 us -> 10.9 us
    ppermute x51, starting transfers between devices: 63.1 us -> 68.9 us  [permuted(): y = lax.ppermute(x, axis, route)]
  transfers between devices with their start and end apart: 51 -> 51, of which waited for: 11 -> 19; matrix products, arithmetic and copies ran while one was open for 9% -> 6% of each run, Pallas kernels for 44% -> 35%
where the time goes in v3:
time: 236 us; the launch traced here: 235 us
  Pallas kernels  99 us (42%)
  starting transfers between devices  68.9 us (29%)
  waiting for transfers between devices  36 us (15%)
  local copies, waits for them, and re-layouts  17.9 us (8%)
  other arithmetic  6.3 us (3%)
  blocking collectives  5.37 us (2%)
    pallas_call x35, Pallas kernels, call(): pl.pallas_call(body, grid_spec=pltpu.PrefetchScalarGridSpec(num_scalar_pr...  99 us
    ppermute x51, starting transfers between devices, permuted(): y = lax.ppermute(x, axis, route)  68.9 us
    ppermute x51, waiting for transfers between devices, permuted(): y = lax.ppermute(x, axis, route)  36 us
    unnamed x108, local copies, waits for them, and re-layouts  10.9 us
    all_gather x1, blocking collectives, shards(): stats_all = lax.all_gather(stats, 'head')  5.37 us
  transfers between devices with their start and end apart: 51, of which 19 were waited for; matrix products, arithmetic and copies ran while one was open for 6% of the time, Pallas kernels for 35%

profile of v3, /device:TPU:0, one launch (start us, length us, event | category | flops | bytes accessed | tf_op | source)
XLA Modules:
  0.0 234.9 jit_solution(12506153217613075768)
XLA Ops:
  1.3 2.6 %collective-permute-start.1 = (bf16[4,192,256]{2,1,0:T(8,128)(2,1)}, bf16[4,192,256]{2,1,0:T(8,128)(2,1)S(1)}, u32[]{:S(2)}, u32[]{:S(2)}) collective-permute-start(bf16[4,192,256]{2,1,0:T(8,128)(2,1)} %bitcast.50), channel_id=1, source_target_pairs={{0,2},{1,3},{2,0},{3,1},{4,6},{5,7},{6,4},{7,5},{8,10},{9,11},{10,... | collective-permute-start | bytes 1179656 | tf_op jit(solution)/shard_map/ppermute | solution.py:23
  7.9 3.6 %collective-permute-start.3 = (bf16[192,128]{1,0:T(8,128)(2,1)S(1)}, bf16[192,128]{1,0:T(8,128)(2,1)S(1)}, u32[]{:S(2)}, u32[]{:S(2)}) collective-permute-start(bf16[192,128]{1,0:T(8,128)(2,1)S(1)} %fusion.12), channel_id=1, source_target_pairs={{0,4},{4,8},{8,12},{12,16},{16,20},{20,24},{24,28},{1,5},{5,9},{9,... | collective-permute-start | bytes 147464 | tf_op jit(solution)/shard_map/ppermute | solution.py:23
  21.2 11.9 %shard_map.288 = (bf16[4,768,256]{2,1,0:T(8,128)(2,1)S(1)}, f32[4,1,256]{2,1,0:T(1,128)S(1)}, bf16[768,128]{1,0:T(8,128)(2,1)S(1)}, bf16[4,272,384]{2,1,0:T(8,12...) custom-call(s32[2]{0:T(128)S(1)} %pad_add_fusion.refs_0_, ...), custom_call_target="tpu_custom_call" | custom-call | flops 149999992832 | bytes 45000000 | tf_op jit(solution)/shard_map/pallas_call | solution.py:949
  36.8 3.5 %shard_map.289 = (f32[4,256,384]{2,1,0:T(8,128)S(1)}, f32[8,128]{1,0:T(8,128)S(1)}) custom-call(s32[2]{0:T(128)S(1)} %pad_add_fusion.refs_0_, s32[4,4]{1,0:T(4,128)S(1)} %copy-done.11, bf16[4,256,640]{2,1,0:T(8,128)(2,1)S(1)} %get-tuple-element.142.refs_2_.refs_3_, f32[4,256,128]{2,1,0:T(8,128)S(1)} %get-tuple-element.143.refs_3_.refs_4_.refs_2_, ...), custom_call_target="tpu_custom_call" | custom-call | flops 60000002048 | bytes 18000000 | tf_op jit(solution)/shard_map/pallas_call | solution.py:949
  41.6 3.4 %collective-permute-done.13.refs_4_ = bf16[4,192,256]{2,1,0:T(8,128)(2,1)S(1)} collective-permute-done((bf16[4,192,256]{2,1,0:T(8,128)(2,1)S(1)}, bf16[4,192,256]{2,1,0:T(8,128)(2,1)S(1)}, u32[]{:S(2)}, u32[]{:S(2)}) %collective-permute-start.13) | collective-permute-done | bytes 393248 | tf_op jit(solution)/shard_map/ppermute | solution.py:23
  54.6 2.8 %collective-permute-start.15 = (s16[2,400,128]{2,1,0:T(8,128)(2,1)S(1)}, s16[2,400,128]{2,1,0:T(8,128)(2,1)S(1)}, u32[]{:S(2)}, u32[]{:S(2)}) collective-permute-start(s16[2,400,128]{2,1,0:T(8,128)(2,1)S(1)} %get-tuple-element.153), channel_id=1, source_target_pairs={{0,16},{4,20},{8,24},{12,28},{16,0},{20,4},{24,8},{28,12},{1,17},{... | collective-permute-start | bytes 614408 | tf_op jit(solution)/shard_map/ppermute | solution.py:23
  57.5 4.1 %shard_map.293 = (bf16[4,256,384]{2,1,0:T(8,128)(2,1)S(1)}, f32[4,256,384]{2,1,0:T(8,128)S(1)}, f32[4,256,64]{2,1,0:T(8,128)S(1)}, f32[8,128]{1,0:T(8,128)S(1)}) custom-call(s32[2]{0:T(128)S(1)} %pad_add_fusion.refs_0_, s32[4,4]{1,0:T(4,128)S(1)} %copy-done.11, bf16[4,768,256]{2,1,0:T(8,128)(2,1)S(1)} %get-tuple-element.155.refs_2_.refs_10_.refs_9_.refs_7_, ...), custom_call_target="tpu_custom_call" | custom-call | flops 70000001024 | bytes 21000000 | tf_op jit(solution)/shard_map/pallas_call | solution.py:949
  61.6 5.2 %collective-permute-done.15.refs_3_ = s16[2,400,128]{2,1,0:T(8,128)(2,1)S(1)} collective-permute-done((s16[2,400,128]{2,1,0:T(8,128)(2,1)S(1)}, s16[2,400,128]{2,1,0:T(8,128)(2,1)S(1)}, u32[]{:S(2)}, u32[]{:S(2)}) %collective-permute-start.15) | collective-permute-done | bytes 204832 | tf_op jit(solution)/shard_map/ppermute | solution.py:23
  79.2 3.7 %shard_map.295 = (f32[4,256,384]{2,1,0:T(8,128)S(1)}, f32[4,2,256]{2,1,0:T(2,128)S(1)}, f32[8,128]{1,0:T(8,128)S(1)}) custom-call(s32[2]{0:T(128)S(1)} %pad_add_fusion.refs_0_, s32[4,4]{1,0:T(4,128)S(1)} %copy-done.11, bf16[4,256,640]{2,1,0:T(8,128)(2,1)S(1)} %copy-done.27, f32[4,256,128]{2,1,0:T(8,128)S(1)} %copy-done.38, f32[4,256,384]{2,1,0:T(8,128)S(1)} %copy-done.25, ...), custom_call_target="tpu_custom_call" | custom-call | flops 65999998976 | bytes 19800000 | tf_op jit(solution)/shard_map/pallas_call | solution.py:949
  82.9 5.4 %all-gather = f32[16,2,256]{2,1,0:T(2,128)S(1)} all-gather(f32[4,2,256]{2,1,0:T(2,128)S(1)} %get-tuple-element.165), channel_id=2, replica_groups=mesh['seq'=8,'head'=4] {'head'}, dimensions={0}, use_global_device_ids=true | all-gather | bytes 40960 | tf_op jit(solution)/shard_map/all_gather | solution.py:1260
  89.4 5.7 %shard_map.296 = (f32[4,256,384]{2,1,0:T(8,128)S(1)}, bf16[4,256,384]{2,1,0:T(8,128)(2,1)S(1)}, bf16[4,256,384]{2,1,0:T(8,128)(2,1)S(1)}, s16[2,400,128]{2,1,0:T...) custom-call(s32[2]{0:T(128)S(1)} %pad_add_fusion.refs_0_, ...), custom_call_target="tpu_custom_call" | custom-call | flops 83000000512 | bytes 24900000 | tf_op jit(solution)/shard_map/pallas_call | solution.py:949
  96.7 4.5 %shard_map.297 = (f32[4,192,256]{2,1,0:T(8,128)S(1)}, f32[4,192,256]{2,1,0:T(8,128)S(1)}, bf16[2,4,192,256]{3,2,1,0:T(8,128)(2,1)}, f32[384,384]{1,0:T(8,128)S(1...) custom-call(s32[2]{0:T(128)S(1)} %pad_add_fusion.refs_0_, s32[4,4]{1,0:T(4,128)S(1)} %copy-done.11, ...), custom_call_target="tpu_custom_call" | custom-call | flops 67999997952 | bytes 20400000 | tf_op jit(solution)/shard_map/pallas_call | solution.py:949
  111.1 3.5 %collective-permute-start.21 = (s16[2,400,128]{2,1,0:T(8,128)(2,1)S(1)}, s16[2,400,128]{2,1,0:T(8,128)(2,1)S(1)}, u32[]{:S(2)}, u32[]{:S(2)}) collective-permute-start(s16[2,400,128]{2,1,0:T(8,128)(2,1)S(1)} %get-tuple-element.184), channel_id=1, source_target_pairs={{0,16},{4,20},{8,24},{12,28},{16,0},{20,4},{24,8},{28,12},{1,17},{... | collective-permute-start | bytes 614408 | tf_op jit(solution)/shard_map/ppermute | solution.py:23
  114.6 9.8 %shard_map.301 = (f32[4,256,384]{2,1,0:T(8,128)S(1)}, f32[4,256,256]{2,1,0:T(8,128)S(1)}, f32[4,256,128]{2,1,0:T(8,128)S(1)}, f32[8,128]{1,0:T(8,128)S(1)}) custom-call(s32[2]{0:T(128)S(1)} %pad_add_fusion.refs_0_, s32[4,4]{1,0:T(4,128)S(1)} %copy-done.11, bf16[4,256,640]{2,1,0:T(8,128)(2,1)S(1)} %copy-done.28, f32[4,256,128]{2,1,0:T(8,128)S(1)} %copy-done.38, ...), custom_call_target="tpu_custom_call" | custom-call | flops 120000004096 | bytes 36000000 | tf_op jit(solution)/shard_map/pallas_call | solution.py:949
  134.0 3.8 %shard_map.304 = (f32[4,256,128]{2,1,0:T(8,128)S(1)}, f32[4,256,128]{2,1,0:T(8,128)S(1)}, f32[8,128]{1,0:T(8,128)S(1)}) custom-call(s32[2]{0:T(128)S(1)} %pad_add_fusion.refs_0_, s32[4,4]{1,0:T(4,128)S(1)} %copy-done.11, bf16[4,256,640]{2,1,0:T(8,128)(2,1)S(1)} %copy-done.28, f32[4,256,128]{2,1,0:T(8,128)S(1)} %copy-done.39, ...), custom_call_target="tpu_custom_call" | custom-call | flops 64000000000 | bytes 19200000 | tf_op jit(solution)/shard_map/pallas_call | solution.py:949
  141.9 10.0 %shard_map.307 = (bf16[4,256,384]{2,1,0:T(8,128)(2,1)S(1)}, bf16[128,384]{1,0:T(8,128)(2,1)}, f32[4,256,128]{2,1,0:T(8,128)S(1)}, f32[384,384]{1,0:T(8,128)S(1)}...) custom-call(s32[2]{0:T(128)S(1)} %pad_add_fusion.refs_0_, s32[4,4]{1,0:T(4,128)S(1)} %copy-done.11, ...), custom_call_target="tpu_custom_call" | custom-call | flops 124999999488 | bytes 37500000 | tf_op jit(solution)/shard_map/pallas_call | solution.py:949
  156.1 5.5 %collective-permute-start.33 = (bf16[192,384]{1,0:T(8,128)(2,1)S(1)}, bf16[192,384]{1,0:T(8,128)(2,1)S(1)}, u32[]{:S(2)}, u32[]{:S(2)}) collective-permute-start(bf16[192,384]{1,0:T(8,128)(2,1)S(1)} %get-tuple-element.224.refs_1_), channel_id=1, source_target_pairs={{0,16},{4,20},{8,24},{12,28},{16,0},{20,4},{24,8},{28,12},{1,17},{... | collective-permute-start | bytes 442376 | tf_op jit(solution)/shard_map/ppermute | solution.py:23
  162.5 3.0 %collective-permute-start.35 = (bf16[384,384]{1,0:T(8,128)(2,1)}, bf16[384,384]{1,0:T(8,128)(2,1)}, u32[]{:S(2)}, u32[]{:S(2)}) collective-permute-start(bf16[384,384]{1,0:T(8,128)(2,1)} %get-tuple-element.233), channel_id=1, source_target_pairs={{0,4},{4,0},{8,12},{12,8},{16,20},{20,16},{24,28},{28,24},{1,5},{5... | collective-permute-start | bytes 884744 | tf_op jit(solution)/shard_map/ppermute | solution.py:23
  165.5 4.9 %shard_map.309 = (bf16[4,256,64]{2,1,0:T(8,128)(2,1)S(1)}, f32[64,384]{1,0:T(8,128)S(1)}, bf16[64,384]{1,0:T(8,128)(2,1)}, f32[8,64]{1,0:T(8,128)S(1)}, f32[8,128]{1,0:T(8,128)S(1)}) custom-call(s32[2]{0:T(128)S(1)} %pad_add_fusion.refs_0_, s32[4,4]{1,0:T(4,128)S(1)} %copy-done.11, f32[2,256,128]{2,1,0:T(8,128)S(1)} %get-tuple-element.210.refs_2_, ...), custom_call_target="tpu_custom_call" | custom-call | flops 62999998464 | bytes 18900000 | tf_op jit(solution)/shard_map/pallas_call | solution.py:949
  170.4 5.4 %shard_map.310 = (bf16[4,256,128]{2,1,0:T(8,128)(2,1)S(1)}, f32[16,768]{1,0:T(8,128)S(1)}, f32[8,128]{1,0:T(8,128)S(1)}) custom-call(s32[2]{0:T(128)S(1)} %pad_add_fusion.refs_0_, s32[4,4]{1,0:T(4,128)S(1)} %copy-done.11, f32[4,256,128]{2,1,0:T(8,128)S(1)} %copy-done.39, f32[4,256,128]{2,1,0:T(8,128)S(1)} %get-tuple-element.207.refs_3_, ...), custom_call_target="tpu_custom_call" | custom-call | flops 80000000000 | bytes 24000000 | tf_op jit(solution)/shard_map/pallas_call | solution.py:949
  179.4 5.7 %shard_map.312 = (f32[4,192,256]{2,1,0:T(8,128)S(1)}, f32[4,192,256]{2,1,0:T(8,128)S(1)}, bf16[2,4,208,256]{3,2,1,0:T(8,128)(2,1)S(1)}, f32[4,8,256]{2,1,0:T(8,128)S(1)}, f32[8,128]{1,0:T(8,128)S(1)}) custom-call(s32[2]{0:T(128)S(1)} %pad_add_fusion.refs_0_, s32[4,4]{1,0:T(4,128)S(1)} %copy-done.11, bf16[4,256,384]{2,1,0:T(8,128)(2,1)S(1)} %get-tuple-element.205.refs_2_, ...), custom_call_target="tpu_custom_call" | custom-call | flops 83000000512 | bytes 24900000 | tf_op jit(solution)/shard_map/pallas_call | solution.py:949
  191.2 3.9 %collective-permute-done.41.refs_2_ = bf16[384,384]{1,0:T(8,128)(2,1)S(1)} collective-permute-done((bf16[384,384]{1,0:T(8,128)(2,1)S(1)}, bf16[384,384]{1,0:T(8,128)(2,1)S(1)}, u32[]{:S(2)}, u32[]{:S(2)}) %collective-permute-start.41) | collective-permute-done | bytes 294944 | tf_op jit(solution)/shard_map/ppermute | solution.py:23
  195.8 3.6 %collective-permute-done.40.refs_4_ = f32[16,768]{1,0:T(8,128)S(1)} collective-permute-done((f32[16,768]{1,0:T(8,128)S(1)}, f32[16,768]{1,0:T(8,128)S(1)}, u32[]{:S(2)}, u32[]{:S(2)}) %collective-permute-start.40) | collective-permute-done | bytes 49184 | tf_op jit(solution)/shard_map/ppermute | solution.py:23
  211.4 4.5 %collective-permute-done.38.refs_1_ = bf16[4,208,256]{2,1,0:T(8,128)(2,1)S(1)} collective-permute-done((bf16[4,208,256]{2,1,0:T(8,128)(2,1)S(1)}, bf16[4,208,256]{2,1,0:T(8,128)(2,1)S(1)}, u32[]{:S(2)}, u32[]{:S(2)}) %collective-permute-start.38) | collective-permute-done | bytes 426016 | tf_op jit(solution)/shard_map/ppermute | solution.py:23
  (252 shorter events, 113.6 us)
Async XLA Ops:
  0.7 20.4 %collective-permute-start = (bf16[4,192,256]{2,1,0:T(8,128)(2,1)}, bf16[4,192,256]{2,1,0:T(8,128)(2,1)S(1)}, u32[]{:S(2)}, u32[]{:S(2)}) collective-permute-start(bf16[4,192,256]{2,1,0:T(8,128)(2,1)} %bitcast.49), channel_id=1, source_target_pairs={{0,1},{1,0},{2,3},{3,2},{4,5},{5,4},{6,7},{7,6},{8,9},{9,8},{10,11... | collective-permute-start | bytes 1179656 | tf_op jit(solution)/shard_map/ppermute | solution.py:23
  1.3 12.8 %collective-permute-start.1 = (bf16[4,192,256]{2,1,0:T(8,128)(2,1)}, bf16[4,192,256]{2,1,0:T(8,128)(2,1)S(1)}, u32[]{:S(2)}, u32[]{:S(2)}) collective-permute-start(bf16[4,192,256]{2,1,0:T(8,128)(2,1)} %bitcast.50), channel_id=1, source_target_pairs={{0,2},{1,3},{2,0},{3,1},{4,6},{5,7},{6,4},{7,5},{8,10},{9,11},{10,... | collective-permute-start | bytes 1179656 | tf_op jit(solution)/shard_map/ppermute | solution.py:23
  6.3 13.8 %collective-permute-start.7 = (bf16[64,896]{1,0:T(8,128)(2,1)S(1)}, bf16[64,896]{1,0:T(8,128)(2,1)S(1)}, u32[]{:S(2)}, u32[]{:S(2)}) collective-permute-start(bf16[64,896]{1,0:T(8,128)(2,1)S(1)} %fusion.5.refs_10_), channel_id=1, source_target_pairs={{0,1},{1,0},{2,3},{3,2},{4,5},{5,4},{6,7},{7,6},{8,9},{9,8},{10,11... | collective-permute-start | bytes 344072 | tf_op jit(solution)/shard_map/ppermute | solution.py:23
  6.5 11.2 %collective-permute-start.8 = (bf16[64,896]{1,0:T(8,128)(2,1)S(1)}, bf16[64,896]{1,0:T(8,128)(2,1)S(1)}, u32[]{:S(2)}, u32[]{:S(2)}) collective-permute-start(bf16[64,896]{1,0:T(8,128)(2,1)S(1)} %fusion.5.refs_10_), channel_id=1, source_target_pairs={{0,2},{1,3},{2,0},{3,1},{4,6},{5,7},{6,4},{7,5},{8,10},{9,11},{10,... | collective-permute-start | bytes 344072 | tf_op jit(solution)/shard_map/ppermute | solution.py:23
  33.2 14.6 %collective-permute-start.12 = (bf16[4,192,256]{2,1,0:T(8,128)(2,1)S(1)}, bf16[4,192,256]{2,1,0:T(8,128)(2,1)S(1)}, u32[]{:S(2)}, u32[]{:S(2)}) collective-permute-start(bf16[4,192,256]{2,1,0:T(8,128)(2,1)S(1)} %bitcast.55), channel_id=1, source_target_pairs={{0,1},{1,0},{2,3},{3,2},{4,5},{5,4},{6,7},{7,6},{8,9},{9,8},{10,11... | collective-permute-start | bytes 1179656 | tf_op jit(solution)/shard_map/ppermute | solution.py:23
  33.4 11.6 %collective-permute-start.13 = (bf16[4,192,256]{2,1,0:T(8,128)(2,1)S(1)}, bf16[4,192,256]{2,1,0:T(8,128)(2,1)S(1)}, u32[]{:S(2)}, u32[]{:S(2)}) collective-permute-start(bf16[4,192,256]{2,1,0:T(8,128)(2,1)S(1)} %bitcast.56), channel_id=1, source_target_pairs={{0,2},{1,3},{2,0},{3,1},{4,6},{5,7},{6,4},{7,5},{8,10},{9,11},{10,... | collective-permute-start | bytes 1179656 | tf_op jit(solution)/shard_map/ppermute | solution.py:23
  54.6 12.2 %collective-permute-start.15 = (s16[2,400,128]{2,1,0:T(8,128)(2,1)S(1)}, s16[2,400,128]{2,1,0:T(8,128)(2,1)S(1)}, u32[]{:S(2)}, u32[]{:S(2)}) collective-permute-start(s16[2,400,128]{2,1,0:T(8,128)(2,1)S(1)} %get-tuple-element.153), channel_id=1, source_target_pairs={{0,16},{4,20},{8,24},{12,28},{16,0},{20,4},{24,8},{28,12},{1,17},{... | collective-permute-start | bytes 614408 | tf_op jit(solution)/shard_map/ppermute | solution.py:23
  70.7 85.4 %collective-permute-start.31 = (f32[4,16,64]{2,1,0:T(8,128)}, f32[4,16,64]{2,1,0:T(8,128)}, u32[]{:S(2)}, u32[]{:S(2)}) collective-permute-start(f32[4,16,64]{2,1,0:T(8,128)} %slice.63), channel_id=1, source_target_pairs={{4,0},{8,4},{12,8},{16,12},{20,16},{24,20},{28,24},{5,1},{9,5},{13... | collective-permute-start | bytes 49160 | tf_op jit(solution)/shard_map/ppermute | solution.py:23
  101.2 29.4 %collective-permute-start.17 = (bf16[2,4,192,256]{3,2,1,0:T(8,128)(2,1)}, bf16[2,4,192,256]{3,2,1,0:T(8,128)(2,1)}, u32[]{:S(2)}, u32[]{:S(2)}) collective-permute-start(bf16[2,4,192,256]{3,2,1,0:T(8,128)(2,1)} %get-tuple-element.172), channel_id=1, source_target_pairs={{0,1},{1,0},{2,3},{3,2},{4,5},{5,4},{6,7},{7,6},{8,9},{9,8},{10,11... | collective-permute-start | bytes 2359304 | tf_op jit(solution)/shard_map/ppermute | solution.py:23
  101.3 23.1 %collective-permute-start.22 = (bf16[384,384]{1,0:T(8,128)(2,1)}, bf16[384,384]{1,0:T(8,128)(2,1)}, u32[]{:S(2)}, u32[]{:S(2)}) collective-permute-start(bf16[384,384]{1,0:T(8,128)(2,1)} %get-tuple-element.187), channel_id=1, source_target_pairs={{0,4},{4,0},{8,12},{12,8},{16,20},{20,16},{24,28},{28,24},{1,5},{5... | collective-permute-start | bytes 884744 | tf_op jit(solution)/shard_map/ppermute | solution.py:23
  107.9 16.5 %collective-permute-start.23 = (bf16[384,384]{1,0:T(8,128)(2,1)S(1)}, bf16[384,384]{1,0:T(8,128)(2,1)S(1)}, u32[]{:S(2)}, u32[]{:S(2)}) collective-permute-start(bf16[384,384]{1,0:T(8,128)(2,1)S(1)} %get-tuple-element.188), channel_id=1, source_target_pairs={{0,4},{4,0},{8,12},{12,8},{16,20},{20,16},{24,28},{28,24},{1,5},{5... | collective-permute-start | bytes 884744 | tf_op jit(solution)/shard_map/ppermute | solution.py:23
  111.1 13.3 %collective-permute-start.21 = (s16[2,400,128]{2,1,0:T(8,128)(2,1)S(1)}, s16[2,400,128]{2,1,0:T(8,128)(2,1)S(1)}, u32[]{:S(2)}, u32[]{:S(2)}) collective-permute-start(s16[2,400,128]{2,1,0:T(8,128)(2,1)S(1)} %get-tuple-element.184), channel_id=1, source_target_pairs={{0,16},{4,20},{8,24},{12,28},{16,0},{20,4},{24,8},{28,12},{1,17},{... | collective-permute-start | bytes 614408 | tf_op jit(solution)/shard_map/ppermute | solution.py:23
  132.4 70.5 %collective-permute-start.18 = (bf16[4,192,256]{2,1,0:T(8,128)(2,1)}, bf16[4,192,256]{2,1,0:T(8,128)(2,1)}, u32[]{:S(2)}, u32[]{:S(2)}) collective-permute-start(bf16[4,192,256]{2,1,0:T(8,128)(2,1)} %fusion), channel_id=1, source_target_pairs={{0,2},{1,3},{2,0},{3,1},{4,6},{5,7},{6,4},{7,5},{8,10},{9,11},{10,... | collective-permute-start | bytes 1179656 | tf_op jit(solution)/shard_map/ppermute | solution.py:23
  138.5 15.0 %collective-permute-start.32 = (bf16[192,384]{1,0:T(8,128)(2,1)S(1)}, bf16[192,384]{1,0:T(8,128)(2,1)S(1)}, u32[]{:S(2)}, u32[]{:S(2)}) collective-permute-start(bf16[192,384]{1,0:T(8,128)(2,1)S(1)} %get-tuple-element.215), channel_id=1, source_target_pairs={{0,16},{4,20},{8,24},{12,28},{16,0},{20,4},{24,8},{28,12},{1,17},{... | collective-permute-start | bytes 442376 | tf_op jit(solution)/shard_map/ppermute | solution.py:23
  140.5 14.1 %collective-permute-start.29 = (f32[4,16,128]{2,1,0:T(8,128)S(1)}, f32[4,16,128]{2,1,0:T(8,128)S(1)}, u32[]{:S(2)}, u32[]{:S(2)}) collective-permute-start(f32[4,16,128]{2,1,0:T(8,128)S(1)} %get-tuple-element.212), channel_id=1, source_target_pairs={{4,0},{8,4},{12,8},{16,12},{20,16},{24,20},{28,24},{5,1},{9,5},{13... | collective-permute-start | bytes 98312 | tf_op jit(solution)/shard_map/ppermute | solution.py:23
  151.9 26.6 %collective-permute-start.27 = (bf16[128,384]{1,0:T(8,128)(2,1)}, bf16[128,384]{1,0:T(8,128)(2,1)}, u32[]{:S(2)}, u32[]{:S(2)}) collective-permute-start(bf16[128,384]{1,0:T(8,128)(2,1)} %get-tuple-element.206), channel_id=1, source_target_pairs={{4,0},{8,4},{12,8},{16,12},{20,16},{24,20},{28,24},{5,1},{9,5},{13... | collective-permute-start | bytes 294920 | tf_op jit(solution)/shard_map/ppermute | solution.py:23
  153.4 12.1 %collective-permute-start.28 = (f32[2,256,128]{2,1,0:T(8,128)S(1)}, f32[2,256,128]{2,1,0:T(8,128)S(1)}, u32[]{:S(2)}, u32[]{:S(2)}) collective-permute-start(f32[2,256,128]{2,1,0:T(8,128)S(1)} %get-tuple-element.211), channel_id=1, source_target_pairs={{0,2},{1,3},{2,0},{3,1},{4,6},{5,7},{6,4},{7,5},{8,10},{9,11},{10,... | collective-permute-start | bytes 786440 | tf_op jit(solution)/shard_map/ppermute | solution.py:23
  156.1 19.7 %collective-permute-start.33 = (bf16[192,384]{1,0:T(8,128)(2,1)S(1)}, bf16[192,384]{1,0:T(8,128)(2,1)S(1)}, u32[]{:S(2)}, u32[]{:S(2)}) collective-permute-start(bf16[192,384]{1,0:T(8,128)(2,1)S(1)} %get-tuple-element.224.refs_1_), channel_id=1, source_target_pairs={{0,16},{4,20},{8,24},{12,28},{16,0},{20,4},{24,8},{28,12},{1,17},{... | collective-permute-start | bytes 442376 | tf_op jit(solution)/shard_map/ppermute | solution.py:23
  162.5 22.6 %collective-permute-start.35 = (bf16[384,384]{1,0:T(8,128)(2,1)}, bf16[384,384]{1,0:T(8,128)(2,1)}, u32[]{:S(2)}, u32[]{:S(2)}) collective-permute-start(bf16[384,384]{1,0:T(8,128)(2,1)} %get-tuple-element.233), channel_id=1, source_target_pairs={{0,4},{4,0},{8,12},{12,8},{16,20},{20,16},{24,28},{28,24},{1,5},{5... | collective-permute-start | bytes 884744 | tf_op jit(solution)/shard_map/ppermute | solution.py:23
  170.4 16.6 %collective-permute-start.36 = (bf16[64,384]{1,0:T(8,128)(2,1)}, bf16[64,384]{1,0:T(8,128)(2,1)}, u32[]{:S(2)}, u32[]{:S(2)}) collective-permute-start(bf16[64,384]{1,0:T(8,128)(2,1)} %get-tuple-element.234), channel_id=1, source_target_pairs={{0,4},{4,0},{8,12},{12,8},{16,20},{20,16},{24,28},{28,24},{1,5},{5... | collective-permute-start | bytes 147464 | tf_op jit(solution)/shard_map/ppermute | solution.py:23
  175.8 11.2 %collective-permute-start.37 = (f32[16,768]{1,0:T(8,128)S(1)}, f32[16,768]{1,0:T(8,128)S(1)}, u32[]{:S(2)}, u32[]{:S(2)}) collective-permute-start(f32[16,768]{1,0:T(8,128)S(1)} %get-tuple-element.235.refs_5_), channel_id=1, source_target_pairs={{0,4},{4,0},{8,12},{12,8},{16,20},{20,16},{24,28},{28,24},{1,5},{5... | collective-permute-start | bytes 147464 | tf_op jit(solution)/shard_map/ppermute | solution.py:23
  188.6 10.7 %collective-permute-start.39 = (bf16[224,384]{1,0:T(8,128)(2,1)S(1)}, bf16[224,384]{1,0:T(8,128)(2,1)S(1)}, u32[]{:S(2)}, u32[]{:S(2)}) collective-permute-start(bf16[224,384]{1,0:T(8,128)(2,1)S(1)} %get-tuple-element.243), channel_id=1, source_target_pairs={{0,8},{4,12},{8,0},{12,4},{16,24},{20,28},{24,16},{28,20},{1,9},{5... | collective-permute-start | bytes 516104 | tf_op jit(solution)/shard_map/ppermute | solution.py:23
  205.0 10.8 %collective-permute-start.38 = (bf16[4,208,256]{2,1,0:T(8,128)(2,1)S(1)}, bf16[4,208,256]{2,1,0:T(8,128)(2,1)S(1)}, u32[]{:S(2)}, u32[]{:S(2)}) collective-permute-start(bf16[4,208,256]{2,1,0:T(8,128)(2,1)S(1)} %get-tuple-element.239), channel_id=1, source_target_pairs={{0,2},{1,3},{2,0},{3,1},{4,6},{5,7},{6,4},{7,5},{8,10},{9,11},{10,... | collective-permute-start | bytes 1277960 | tf_op jit(solution)/shard_map/ppermute | solution.py:23
  206.1 16.8 %collective-permute-start.47 = (bf16[768,384]{1,0:T(8,128)(2,1)S(1)}, bf16[768,384]{1,0:T(8,128)(2,1)S(1)}, u32[]{:S(2)}, u32[]{:S(2)}) collective-permute-start(bf16[768,384]{1,0:T(8,128)(2,1)S(1)} %get-tuple-element.255.refs_1_), channel_id=1, source_target_pairs={{0,4},{4,0},{8,12},{12,8},{16,20},{20,16},{24,28},{28,24},{1,5},{5... | collective-permute-start | bytes 1769480 | tf_op jit(solution)/shard_map/ppermute | solution.py:23
  (80 other events, 617.3 us)

commit v4 on v3

--- a/solution.py
+++ b/solution.py
@@ -17,6 +17,7 @@
 UNIT = 16384.0
 LN2 = 0.6931471805599453
 GROUP = 16
+SMALL = 32
 
 
 def permuted(x, axis, route):
@@ -176,6 +177,61 @@
     return jnp.concatenate(
         [state[h * size : (h + 1) * size] * decay[:, h : h + 1] for h in range(heads)], axis=0
     )
+
+
+def tail_kernel(tokens, out):
+    lane = lax.broadcasted_iota(jnp.int32, out.shape, 1)
+    total = jnp.zeros(out.shape, f32)
+    for p in range(tokens.shape[0]):
+        moved = pltpu.roll(tokens[p].astype(f32), (p + 1) * EDGE, 1)
+        total = jnp.where((lane >= p * EDGE) & (lane < (p + 1) * EDGE), moved, total)
+    out[...] = total.astype(bf16)
+
+
+def wide_row(ref, lanes=LANES):
+    row = ref[...].astype(f32)[None, :]
+    blank = lanes - row.shape[1]
+    return jnp.concatenate([row, jnp.zeros((1, blank), f32)], axis=1) if blank else row
+
+
+def prepare_kernel(dims, *refs):
+    packs, count, features, inner, bc, heads, size, width, nseq = dims
+    (
+        wbc, conv_bc, bias_bc, norm_gain, wdt, conv_x, bias_x, dt_bias, a_log, d_skip, gate_gain,
+        shared_o, wbc_o, wdt_o, wdt_rows_o, conv_x_o, conv_bc_o, small_o, skip_o, gate_gain_o, gain_o,
+    ) = refs
+    bc_part, part = bc // 4, features // 4
+    taps = conv_bc[...].astype(f32)
+    bias = wide_row(bias_bc, bc_part)
+    gain = wide_row(norm_gain, part)
+    pieces = [gain[:, c * bc_part : (c + 1) * bc_part] for c in range(part // bc_part)]
+    rows = jnp.concatenate([taps, bias] + pieces, axis=0)
+    rows = jnp.concatenate([rows, jnp.zeros((LANES - rows.shape[0], bc_part), f32)], axis=0)
+    rows = jnp.concatenate([rows, jnp.zeros((LANES, LANES - bc_part), f32)], axis=1)
+    extra = jnp.transpose(rows)[:bc_part].astype(bf16)
+    shared_o[:, :features] = wbc[...]
+    shared_o[:, features:] = extra
+    wbc_o[...] = jnp.transpose(wbc[...].astype(f32)).astype(bf16)
+    dt_rows = jnp.concatenate(
+        [wdt[...].astype(f32), jnp.zeros((LANES - heads, features), f32)], axis=0
+    )
+    wdt_rows_o[...] = dt_rows.astype(bf16)
+    wdt_o[...] = jnp.transpose(dt_rows).astype(bf16)
+    blank = jnp.zeros((7 - width, inner), f32)
+    conv_x_o[...] = jnp.concatenate(
+        [conv_x[...].astype(f32), wide_row(bias_x, inner), blank], axis=0
+    )
+    conv_bc_o[...] = jnp.concatenate([taps, bias, blank[:, :bc_part]], axis=0)
+    small_o[...] = jnp.concatenate(
+        [wide_row(dt_bias), wide_row(a_log), jnp.zeros((6, LANES), f32)], axis=0
+    )
+    skips = jnp.concatenate([wide_row(d_skip), jnp.zeros((7, LANES), f32)], axis=0)
+    matrix = spread_matrix(heads, size)
+    skip_o[...] = sum(nn(piece, matrix) for piece in split3(skips))[0:1]
+    gate_gain_o[...] = wide_row(gate_gain, inner)
+    column = jnp.concatenate([gain, jnp.zeros((LANES - 1, part), f32)], axis=0)
+    column = jnp.concatenate([column, jnp.zeros((LANES, 2 * LANES - part), f32)], axis=1)
+    gain_o[...] = jnp.transpose(column)[:part, 0:1]
 
 
 def front_kernel(dims, meta, lens, *refs):
@@ -421,11 +477,11 @@
 def grad_kernel(dims, total_inner, meta, lens, *refs):
     packs, count, features, inner, bc, heads, size, width, nseq = dims
     (
-        stats, xbc, steps, y, gate, gg, gain, skip,
+        stats, near, far, diagonal, xbc, steps, y, gate, gg, gain, skip,
         gy_o, gated_o, ggate_o, keep_o, send_o, small_o,
     ) = refs
     pack = pl.program_id(0)
-    sums = stats[0, 0] + stats[1, 0] + stats[2, 0] + stats[3, 0]
+    sums = (stats[0] + near[0]) + (far[0] + diagonal[0])
     row = lax.broadcasted_iota(jnp.int32, (LANES, count), 0)
     wide = jnp.where(row == 0, sums[0:1], 0.0) + jnp.where(row == 1, sums[1:2], 0.0)
     cols = jnp.transpose(wide)
@@ -538,11 +594,19 @@
     accumulate(meta, pack, packs, sums, nn(cot[0], gated[0]), keep_o, give_o)
 
 
+def gain_row(weights, grads):
+    part = jnp.sum(weights.astype(f32) * grads, axis=1, keepdims=True)
+    return jnp.transpose(jnp.broadcast_to(part, (part.shape[0], LANES)))[0:8]
+
+
 def z_kernel(dims, meta, lens, *refs):
-    normed, ggate, keep_o, give_o, sums = refs
-    accumulate(
-        meta, pl.program_id(0), dims[0], sums, nn(normed[0], ggate[0]), keep_o, give_o
-    )
+    normed, ggate, wz, keep_o, give_o, gain_o, sums = refs
+    pack = pl.program_id(0)
+    accumulate(meta, pack, dims[0], sums, nn(normed[0], ggate[0]), keep_o, give_o)
+
+    @pl.when(pack == dims[0] - 1)
+    def _():
+        gain_o[...] = gain_row(wz[...], sums[...].reshape(wz.shape))
 
 
 def end_weights(seg, seg_main, cum_col, dt_col, count):
@@ -553,14 +617,20 @@
 
 def share_kernel(dims, meta, lens, *refs):
     packs, count, features, inner, bc, heads, size, width, nseq = dims
-    xbc, steps, dbc, gkeep, grecv, own_o, near_o = refs
+    (
+        xbc, steps, dbc, gkeep, grecv, gy, dx, slope, conv, skip,
+        own_o, near_o, grad_o, state_sum_o, edge_o,
+        gpad,
+    ) = refs
     pack = pl.program_id(0)
     half, quarter = bc // 2, bc // 4
     g_hi, g_lo = split2(load_state(meta, packs, pack, gkeep, grecv, heads, size))
     seg = column_segments(meta, lens, pack, count, nseq, EDGE)
     dt, cum = steps_of(steps[0], heads)
-    wide = spread(end_weights(seg, seg[EDGE:], cum, dt, count), spread_matrix(heads, size), heads)
-    hi, lo = split2(wide * xbc[0, :, :inner].astype(f32))
+    matrix = spread_matrix(heads, size)
+    wide = spread(end_weights(seg, seg[EDGE:], cum, dt, count), matrix, heads)
+    x_f = xbc[0, :, :inner].astype(f32)
+    hi, lo = split2(wide * x_f)
     grad_b = dbc[0, :, :half] + nn(hi, g_hi) + nn(lo, g_hi) + nn(hi, g_lo)
     grad_c = dbc[0, :, half:]
     even = jnp.concatenate([grad_b[:, :quarter], grad_c[:, :quarter]], axis=1)
@@ -568,11 +638,21 @@
     first = (meta[1] & 1) == 0
     own_o[0] = jnp.where(first, even, odd)
     near_o[0] = jnp.where(first, odd, even)
+    b_vals = xbc[0, :, inner : inner + half]
+    u_wide = wide * nt(
+        jnp.concatenate([b_vals, b_vals], axis=1), jnp.concatenate([g_hi, g_lo], axis=1)
+    )
+    state_sum_o[0] = collapse(x_f * u_wide, matrix, heads)
+    grad_x = (dx[0] + u_wide + gy[0] * skip[...]) * slope[0]
+    grad_o[0] = grad_x
+    gpad[:EDGE, :] = jnp.zeros((EDGE, inner), f32)
+    gpad[EDGE:, :] = grad_x[:EDGE]
+    edge_o[0] = conv_rows(gpad, conv, seg, EDGE, width).astype(bf16)
 
 
 def middle_kernel(dims, meta, *refs):
     packs, quarter = dims
-    own, near, keep_o, send_o, edge_o = refs
+    own, near, keep_o, send_o = refs
     half = packs // 2
     first = (meta[1] >> 1) == 0
     for p in range(half):
@@ -581,8 +661,6 @@
         high = jnp.concatenate([a[:, quarter:], b[:, quarter:]], axis=1)
         keep_o[p] = jnp.where(first, low, high)
         send_o[p] = jnp.where(first, high, low)
-        edge_o[p] = keep_o[p, :EDGE, :]
-        edge_o[half + p] = send_o[p, :EDGE, :]
 
 
 def conv_taps(grads, raws, gconv_o, seg, count, width):
@@ -605,108 +683,12 @@
     return total
 
 
-def xback_kernel(dims, meta, lens, *refs):
-    packs, count, features, inner, bc, heads, size, width, nseq = dims
-    (
-        xbc, steps, gy, dx, gkeep, grecv, slope, raw, normed, edge, conv, skip,
-        main_o, edge_o, state_sum_o, keep_o, give_o, gconv_o,
-        gpad, raws, sums,
-    ) = refs
-    pack = pl.program_id(0)
-    gstate = jnp.concatenate(
-        split2(load_state(meta, packs, pack, gkeep, grecv, heads, size)), axis=1
-    )
-    seg = column_segments(meta, lens, pack, count, nseq, EDGE)
-    matrix = spread_matrix(heads, size)
-    b_vals = xbc[0, :, inner : inner + bc // 2]
-    dt, cum = steps_of(steps[0], heads)
-    wide = spread(end_weights(seg, seg[EDGE:], cum, dt, count), matrix, heads)
-    u_wide = wide * nt(jnp.concatenate([b_vals, b_vals], axis=1), gstate)
-    state_sum_o[0] = collapse(xbc[0, :, :inner].astype(f32) * u_wide, matrix, heads)
-    grad_x = (dx[0] + u_wide + gy[0] * skip[...]) * slope[0].astype(f32)
-
-    @pl.when(pack == 0)
-    def _():
-        for ref in (gconv_o, gpad, edge_o):
-            ref[...] = jnp.zeros_like(ref)
-
-    raws[...] = raw[0].astype(f32)
-    gpad[EDGE : EDGE + count, :] = grad_x
-    conv_taps(grad_x, raws, gconv_o, seg, count, width)
-    seg_pad = jnp.concatenate([seg, jnp.full((8, 1), -1, jnp.int32)], axis=0)
-    grad_raw = conv_rows(gpad, conv, seg_pad, count + EDGE, width).astype(bf16)
-    main_o[0] = grad_raw[EDGE:]
-    edge_o[pl.ds(pl.multiple_of(pack * EDGE, EDGE), EDGE), :] = grad_raw[:EDGE]
-    term = nn(normed[0], grad_raw[EDGE:]).reshape(sums.shape)
-
-    @pl.when(pack == 0)
-    def _():
-        sums[...] = term
-
-    @pl.when(pack > 0)
-    def _():
-        sums[...] += term
-
-    @pl.when(pack == packs - 1)
-    def _():
-        sums[...] += nn(edge[...], edge_o[...]).reshape(sums.shape)
-        side = meta[0] & 1
-        keep_o[...] = sums[side]
-        give_o[...] = sums[1 - side].astype(bf16)
-
-
-def conv_bc_kernel(dims, meta, lens, *refs):
-    packs, count, features, inner, bc, heads, size, width, nseq = dims
-    (
-        keep, recv, edge_keep, edge_recv, slope, slope_next, raw, normed, conv,
-        rows_o, keep_o, give_o, gconv_o,
-        gpad, raws, sums,
-    ) = refs
-    pack = pl.program_id(0)
-    quarter = bc // 4
-    early = pack < packs // 2
-
-    @pl.when(pack == 0)
-    def _():
-        gconv_o[...] = jnp.zeros_like(gconv_o)
-
-    def own_pack(values):
-        return jnp.where(early, values[:, :quarter], values[:, quarter:])
-
-    grad = own_pack(keep[0] + recv[0]) * slope[0]
-    gpad[:count, :] = grad
-    gpad[count:, :] = own_pack(edge_keep[0] + edge_recv[0]) * slope_next[0]
-    rows = lax.broadcasted_iota(jnp.int32, (count + 2 * EDGE, 1), 0)
-    seg = segments(rows + (meta[0] * count - EDGE), lens, pack, nseq)
-    raws[...] = raw[0].astype(f32)
-    conv_taps(grad, raws, gconv_o, seg, count, width)
-    grad_bc = conv_rows(gpad, conv, seg[EDGE:], count, width).astype(bf16)
-    rows_o[0] = grad_bc
-    term = nn(normed[0], grad_bc)
-
-    @pl.when(pack == 0)
-    def _():
-        sums[...] = term
-
-    @pl.when(pack > 0)
-    def _():
-        sums[...] += term
-
-    @pl.when(pack == packs - 1)
-    def _():
-        total = jnp.transpose(sums[...])
-        first = (meta[0] & 1) == 0
-        keep_o[...] = jnp.where(first, total[:, :inner], total[:, inner:])
-        give_o[...] = jnp.where(first, total[:, inner:], total[:, :inner]).astype(bf16)
-
-
 def step_kernel(dims, meta, lens, *refs):
     packs, count, features, inner, bc, heads, size, width, nseq = dims
     (
-        steps, sums, state_sums, keep, recv, gkeep, grecv, small, normed, gconv_x, gconv_bc,
-        gate_small,
-        gdt_o, small_o,
-        gdt_sums, gsmall,
+        steps, sums, state_sums, keep, recv, gkeep, grecv, small, normed, wdt,
+        gdt_o, gdt_rows_o, gsmall_o, gain_o,
+        gdt_sums,
     ) = refs
     pack = pl.program_id(0)
     state = load_state(meta, packs, pack, keep, recv, heads, size)
@@ -736,66 +718,151 @@
 
     @pl.when(pack == 0)
     def _():
-        for ref in (gsmall, gdt_sums):
+        for ref in (gsmall_o, gdt_sums):
             ref[...] = jnp.zeros_like(ref)
 
-    gsmall[0:1, :] += jnp.sum(grad_dt, axis=0, keepdims=True)
-    gsmall[1:2, :] += jnp.sum(grad_rate * dt * decay_rate, axis=0, keepdims=True)
+    gsmall_o[0:1, :] += jnp.sum(grad_dt, axis=0, keepdims=True)
+    gsmall_o[1:2, :] += jnp.sum(grad_rate * dt * decay_rate, axis=0, keepdims=True)
     gdt_sums[...] += nn(normed[0], low)
 
     @pl.when(pack == packs - 1)
     def _():
-        taps, quarter = width + 1, bc // 4
+        gdt_rows_o[...] = jnp.transpose(gdt_sums[...])[0:8]
+        gain_o[...] = gain_row(wdt[...], gdt_sums[...])
+
+
+def xback_kernel(dims, meta, lens, *refs):
+    packs, count, features, inner, bc, heads, size, width, nseq = dims
+    (
+        grads, raw, normed, edge, edge_x, conv, wx,
+        main_o, keep_o, give_o, gconv_o, gain_o,
+        gpad, raws, sums, rows_x,
+    ) = refs
+    pack = pl.program_id(0)
+    seg = column_segments(meta, lens, pack, count, nseq, EDGE)
+
+    @pl.when(pack == 0)
+    def _():
+        for ref in (gconv_o, gpad, rows_x):
+            ref[...] = jnp.zeros_like(ref)
+
+    raws[...] = raw[0].astype(f32)
+    gpad[:count, :] = grads[0]
+    conv_taps(grads[0], raws, gconv_o, seg, count, width)
+    seg_pad = jnp.concatenate([seg[EDGE:], jnp.full((8, 1), -1, jnp.int32)], axis=0)
+    main = conv_rows(gpad, conv, seg_pad, count, width).astype(bf16)
+    main_o[0] = main
+    rows_x[pl.ds(pl.multiple_of(pack * EDGE, EDGE), EDGE), :] = edge_x[0]
+    term = nn(normed[0], main).reshape(sums.shape)
+
+    @pl.when(pack == 0)
+    def _():
+        sums[...] = term
+
+    @pl.when(pack > 0)
+    def _():
+        sums[...] += term
+
+    @pl.when(pack == packs - 1)
+    def _():
+        sums[...] += nn(edge[...], rows_x[...]).reshape(sums.shape)
+        side = meta[0] & 1
+        keep_o[...] = sums[side]
+        give_o[...] = sums[1 - side].astype(bf16)
+        gain_o[...] = gain_row(wx[...], sums[...].reshape(wx.shape))
+
+
+def conv_bc_kernel(dims, meta, lens, *refs):
+    packs, count, features, inner, bc, heads, size, width, nseq = dims
+    (
+        keep, recv, slope, raw, normed, edge, wbc, conv, edge_x,
+        gconv_x, gdt_rows, gsmall, gate_small, gain_z, gain_x, gain_dt, gain,
+        rows_o, edges_o, keep_o, give_o, small_o,
+        gpad, raws, sums, edge_bc, gconv,
+    ) = refs
+    pack = pl.program_id(0)
+    quarter = bc // 4
+
+    @pl.when(pack == 0)
+    def _():
+        for ref in (gconv, gpad, edge_bc, sums):
+            ref[...] = jnp.zeros_like(ref)
+
+    both = keep[0] + recv[0]
+    grad = jnp.where(pack < packs // 2, both[:, :quarter], both[:, quarter:]) * slope[0]
+    seg = column_segments(meta, lens, pack, count, nseq, EDGE)
+    raws[...] = raw[0].astype(f32)
+    gpad[EDGE : EDGE + count, :] = grad
+    conv_taps(grad, raws, gconv, seg, count, width)
+    seg_pad = jnp.concatenate([seg, jnp.full((8, 1), -1, jnp.int32)], axis=0)
+    grad_raw = conv_rows(gpad, conv, seg_pad, count + EDGE, width).astype(bf16)
+    rows_o[0] = grad_raw[EDGE:]
+    edge_bc[pl.ds(pl.multiple_of(pack * EDGE, EDGE), EDGE), :] = grad_raw[:EDGE]
+    edges_o[0, :, :inner] = edge_x[0]
+    blank = jnp.zeros((EDGE, LANES - quarter), bf16)
+    edges_o[0, :, inner:] = jnp.concatenate([grad_raw[:EDGE], blank], axis=1)
+    sums[...] += nn(normed[0], grad_raw[EDGE:])
+
+    @pl.when(pack == packs - 1)
+    def _():
+        total = sums[...] + nn(edge[...], edge_bc[...])
+        rows = jnp.transpose(total)
+        left, right = rows[:, :inner], rows[:, inner:]
+        first = (meta[0] & 1) == 0
+        taps = width + 1
+        keep_o[...] = jnp.where(first, left, right)
+        give_o[:quarter, :] = jnp.where(first, right, left).astype(bf16)
         small_o[...] = jnp.zeros_like(small_o)
-        small_o[0:heads, :] = jnp.transpose(gdt_sums[...])[0:heads]
-        small_o[8 : 8 + taps, :inner] = gconv_x[0:taps, :]
-        small_o[8 : 8 + taps, inner : inner + quarter] = gconv_bc[0:taps, :]
-        small_o[13:14, :inner] = gate_small[0:1, :]
-        skips = collapse(gate_small[...], matrix, heads)
-        start = 2 * inner - 3 * LANES
-        small_o[13:14, start : start + LANES] = gsmall[0:1, :]
-        small_o[13:14, start + LANES : start + 2 * LANES] = gsmall[1:2, :]
-        small_o[13:14, start + 2 * LANES :] = skips[1:2, :]
+        for h in range(heads):
+            small_o[2 * h : 2 * h + 1, :] = gdt_rows[h : h + 1, :inner]
+            small_o[2 * h + 1 : 2 * h + 2, :] = gdt_rows[h : h + 1, inner:]
+        row = 2 * heads
+        small_o[row : row + taps, :] = gconv_x[:taps, :]
+        row += taps
+        small_o[row : row + 1, :] = gate_small[0:1, :]
+        skips = collapse(gate_small[...], spread_matrix(heads, size), heads)
+        small_o[row + 1 : row + 2, :] = jnp.concatenate(
+            [gsmall[0:1, :], gsmall[1:2, :], skips[1:2, :]], axis=1
+        )
+        blank_row = jnp.zeros((1, inner - taps * quarter), f32)
+        small_o[row + 2 : row + 3, :] = jnp.concatenate(
+            [gconv[k : k + 1, :] for k in range(taps)] + [blank_row], axis=1
+        )
+        gains = gain_row(wbc[...], total)[0:1] + gain_z[0:1, :] + gain_x[0:1, :] + gain_dt[0:1, :]
+        gains = gains / jnp.transpose(jnp.broadcast_to(gain[...], (features, LANES)))[0:1]
+        small_o[row + 3 : row + 4, :] = gains[:, :inner]
+        small_o[row + 4 : row + 5, :] = gains[:, inner:]
+        hi, lo = split2(small_o[...])
+        give_o[quarter : quarter + SMALL, :] = hi
+        give_o[quarter + SMALL :, :] = lo
 
 
 def back_kernel(dims, meta, lens, *refs):
     packs, count, features, inner, bc, heads, size, width, nseq = dims
     (
-        main, edge_x, ggate, gdt, gbc, normed, wz, wx, wbc, wdt, gain,
-        own_o, far_o, send_o, extra_o,
-        stage, gain_sums, gains,
+        main, edges, ggate, gdt, gbc, normed, wz, wx, wbc, wdt,
+        own_o, far_o, send_o, dots_o,
+        stage,
     ) = refs
-    pack = pl.program_id(0)
     head = meta[1]
-    part = features // 4
-
-    @pl.when(pack == 0)
-    def _():
-        gain_sums[...] = jnp.zeros_like(gain_sums)
-        gains[...] = jnp.zeros_like(gains)
-
-    late = main[0, count - EDGE :, :].astype(f32) + edge_x[...].astype(f32)
-    grad_x = jnp.concatenate([main[0, : count - EDGE, :], late.astype(bf16)], axis=0)
-    whole = nt(wz[...], ggate[0]) + nt(wx[...], grad_x) + nt(wbc[...], gbc[0]) + nt(wdt[...], gdt[0])
-    product = whole * normed[0].astype(f32)
-    gain_sums[...] += jnp.sum(product, axis=1, keepdims=True)
-    dots = jnp.sum(product, axis=0, keepdims=True)
+    part, quarter = features // 4, bc // 4
+    late = count - EDGE
+
+    def with_edge(rows, edge):
+        low = (rows[late:].astype(f32) + edge.astype(f32)).astype(bf16)
+        return jnp.concatenate([rows[:late], low], axis=0)
+
+    grad_x = with_edge(main[0], edges[0, :, :inner])
+    grad_bc = with_edge(gbc[0], edges[0, :, inner : inner + quarter])
+    whole = nt(wz[...], ggate[0]) + nt(wx[...], grad_x) + nt(wbc[...], grad_bc) + nt(wdt[...], gdt[0])
+    dots = jnp.sum(whole * normed[0].astype(f32), axis=0, keepdims=True)
     stage[...] = whole.reshape(stage.shape)
-
-    @pl.when(pack == packs - 1)
-    def _():
-        row = jnp.transpose(jnp.broadcast_to(gain_sums[...] / gain[...], (features, LANES)))
-        for h in range(4):
-            gains[h, 0:1, :part] = row[0:1, h * part : (h + 1) * part]
-
+    dots_o[0] = dots
     own_o[0] = stage[head]
     far_o[0] = stage[head ^ 2]
-    extra_o[0, 0:1, :] = dots
-    extra_o[0, 1:2, :] = gains[head, 0:1, :]
-    extra_o[0, 2:3, :] = gains[head ^ 2, 0:1, :]
     for k in range(2):
         send_o[k, 0, :part, :] = stage[head ^ (1 + 2 * k)].astype(bf16)
-        send_o[k, 0, part:, :] = extra_rows(dots, gains[head ^ (1 + 2 * k), 0:1, :])
+        send_o[k, 0, part:, :] = extra_rows(dots)
 
 
 def extra_rows(*values):
@@ -812,41 +879,54 @@
     return rows[3 * i : 3 * i + 1] + rows[3 * i + 1 : 3 * i + 2] + rows[3 * i + 2 : 3 * i + 3]
 
 
-def gather_kernel(own, far, near, extra, own_o, far_o, extra_o):
+def gather_kernel(own, far, near, dots, own_o, far_o, dots_o):
     part = own.shape[1]
     own_o[0] = own[0] + near[0, 0, :part, :].astype(f32)
     far_o[0, :part, :] = (far[0] + near[1, 0, :part, :].astype(f32)).astype(bf16)
-    mine, others = near[0, 0, part:, :], near[1, 0, part:, :]
-    dots = extra[0, 0:1, :] + read_extra(mine, 0)
-    extra_o[0, 0:1, :] = dots
-    extra_o[0, 1:2, :] = extra[0, 1:2, :] + read_extra(mine, 1)
-    far_o[0, part:, :] = extra_rows(dots, extra[0, 2:3, :] + read_extra(others, 1))
-
-
-def final_kernel(dims, own, far, extra, tokens, inv, gain, out_grad, in_grad_o, gain_o):
+    both = dots[0] + read_extra(near[0, 0, part:, :], 0)
+    dots_o[0] = both
+    far_o[0, part:, :] = extra_rows(both)
+
+
+def final_kernel(dims, own, far, dots, tokens, inv, gain, out_grad, in_grad_o):
     packs, count, features = dims
     part = own.shape[1]
     grad = own[0] + far[0, :part, :].astype(f32)
-    mean = (extra[0, 0:1, :] + read_extra(far[0, part:, :], 0)) / features
+    mean = (dots[0] + read_extra(far[0, part:, :], 0)) / features
     unit = tokens[0].astype(f32) * inv[0]
     in_grad_o[0] = out_grad[0].astype(f32) + inv[0] * (gain[...] * grad - unit * mean)
 
-    @pl.when(pl.program_id(0) == packs - 1)
-    def _():
-        gain_o[...] = jnp.broadcast_to(
-            extra[0, 1:2, :] + read_extra(far[0, part:, :], 1), gain_o.shape
-        )
+
+def out_gather_kernel(own, far, near, own_o, far_o):
+    own_o[0] = own[0] + near[0, 0].astype(f32)
+    far_o[0] = (far[0] + near[1, 0].astype(f32)).astype(bf16)
+
+
+def out_final_kernel(own, far, tokens, out):
+    out[0] = (tokens[0].astype(f32) + (own[0] + far[0].astype(f32))).astype(bf16)
 
 
 def add_kernel(bit, halve, segs, count, small, meta, *refs):
     keep, got, refs = refs[:count], refs[count : 2 * count], refs[2 * count :]
+    end = segs[-1] if count > 1 else sum(segs)
+    write = 0
     if small:
-        refs[-1][...] = refs[0][...] + refs[1][...]
-        refs = refs[2:-1]
-    read, write = 0, 0
+        small_in, *refs, small_o = refs
+        hi, lo = split2(small_in[...])
+        mine = hi.astype(f32) + lo.astype(f32)
+        theirs = got[-1][end : end + SMALL, :].astype(f32) + got[-1][end + SMALL :, :].astype(f32)
+        total = mine + theirs
+        small_o[...] = total
+        if bit is not None:
+            send_o = refs[-1]
+            behind = send_o.shape[0] - 2 * SMALL
+            hi, lo = split2(total)
+            send_o[behind : behind + SMALL, :] = hi
+            send_o[behind + SMALL :, :] = lo
+    read = 0
     for i, rows in enumerate(segs):
         if count > 1:
-            total = keep[i][...] + got[i][...].astype(f32)
+            total = keep[i][...] + got[i][:rows, :].astype(f32)
         else:
             total = keep[0][read : read + rows, :].astype(f32) + got[0][read : read + rows, :].astype(f32)
         read += rows
@@ -891,6 +971,36 @@
         read += rows
 
 
+def plus_kernel(a, b, out):
+    out[...] = a[...] + b[...]
+
+
+def unpack_kernel(dims, meta, *refs):
+    heads, features, bc_part, width = dims
+    smalls, gains, dt_o, taps_x_o, taps_bc_o, bias_x_o, bias_bc_o, dt_bias_o, a_log_o, skip_o, gate_o, gain_o = refs
+    for h in range(heads):
+        dt_o[h : h + 1, :] = jnp.concatenate(
+            [smalls[2 * h : 2 * h + 1, :], smalls[2 * h + 1 : 2 * h + 2, :]], axis=1
+        )
+    row = 2 * heads
+    taps_x_o[...] = smalls[row : row + width, :]
+    bias_x_o[...] = smalls[row + width, :]
+    row += width + 1
+    gate_o[...] = smalls[row, :]
+    for k, out in enumerate((dt_bias_o, a_log_o, skip_o)):
+        out[...] = smalls[row + 1, k * LANES : k * LANES + heads]
+    taps = smalls[row + 2 : row + 3, :]
+    for k in range(width):
+        taps_bc_o[k : k + 1, :] = taps[:, k * bc_part : (k + 1) * bc_part]
+    bias_bc_o[...] = taps[0, width * bc_part : (width + 1) * bc_part]
+    both = jnp.concatenate([gains[row + 3 : row + 4, :], gains[row + 4 : row + 5, :]], axis=1)
+    part = features // 4
+    parts = [both[:, h * part : (h + 1) * part] for h in range(4)]
+    low = jnp.where((meta[1] & 1) == 0, parts[0], parts[1])
+    high = jnp.where((meta[1] & 1) == 0, parts[2], parts[3])
+    gain_o[...] = jnp.where((meta[1] >> 1) == 0, low, high)[0]
+
+
 def whole_spec(shape):
     return pl.BlockSpec(shape, lambda p, *_: (0,) * len(shape))
 
@@ -918,7 +1028,13 @@
         self.clear()
 
     def clear(self):
-        self.last, self.near = (), []
+        self.last, self.near, self.held = (), [], []
+
+    def hold(self, *arrays):
+        self.held += arrays
+
+    def drop(self, *arrays):
+        self.held = [x for x in self.held if not any(x is y for y in arrays)]
 
     def placed(self, x):
         return pltpu.with_memory_space_constraint(x, pltpu.VMEM) if self.holds(x) else x
@@ -936,6 +1052,7 @@
 ):
     first = len(prefetch) + len(args)
     held = order.last + tuple(wait)
+    held += tuple(x for x in order.held if not any(x is y for y in args + held))
     late = len(held)
     single = not isinstance(out_shape, (list, tuple))
     out_specs, out_shape = ([out_specs], [out_shape]) if single else (list(out_specs), list(out_shape))
@@ -961,7 +1078,7 @@
         cost_estimate=pl.CostEstimate(
             flops=int(us * 10e9), bytes_accessed=int(us * 3e6), transcendentals=0
         ),
-    )(*prefetch, *[order.placed(x) for x in args], *[order.placed(x) for x in held])
+    )(*[pltpu.with_memory_space_constraint(x, pltpu.VMEM) for x in prefetch], *[order.placed(x) for x in args], *[order.placed(x) for x in held])
     order.last = (order_out,)
     order.near.append(order_out)
     if not out:
@@ -982,12 +1099,12 @@
     bits = (lax.axis_size("seq") - 1).bit_length()
     beside = list(beside)
 
-    def work():
+    def work(newest):
         if beside:
-            beside.pop(0)()
+            beside.pop(0)(newest)
 
     other = swap(send, "seq", 1)
-    work()
+    work(send)
     total = call(
         functools.partial(pair_kernel, dims, rev), (1,), [spec, spec], spec, pay, [], (meta,),
         keep, other,
@@ -996,7 +1113,7 @@
     for bit in range(1, bits):
         got = swap(total, "seq", 1 << bit)
         extra = () if before is None else (before,)
-        work()
+        work(total)
         if bit < bits - 1:
             total, before = call(
                 functools.partial(cube_kernel, dims, rev, bit, before is None), (1,),
@@ -1011,41 +1128,41 @@
             )
     recv = swap(back, "seq", 1)
     while beside:
-        work()
+        work(back)
     return own, recv
 
 
 class SeqSum:
     def __init__(self):
         self.keep, self.got, self.segs = [], [], []
-        self.small = self.small_got = self.bit = None
+        self.small = self.bit = None
         self.bits = list(range(1, (lax.axis_size("seq") - 1).bit_length()))
         self.halved = []
 
-    def put(self, keep, give):
+    def put(self, keep, give, segs=None, small=None):
         self.keep.append(keep)
         self.got.append(swap(give, "seq", 1))
-        self.segs.append(keep.shape[0])
-
-    def put_small(self, small):
-        self.small, self.small_got = small, swap(small, "seq", 1)
-
-    def add(self, meta):
+        self.segs += segs or [keep.shape[0]]
+        self.small = small
+
+    def add(self, meta, us=1, wait=()):
         bit = self.bits.pop(0) if self.bits else None
         halve = bit is not None and all(rows % (2 * EDGE) == 0 for rows in self.segs)
         cols = self.keep[0].shape[1]
         segs = [rows // 2 for rows in self.segs] if halve else self.segs
         rows = sum(segs)
-        low = shape(rows, cols, bf16)
+        small = self.small is not None
+        behind = 2 * SMALL if small and bit is not None else 0
+        low = shape(rows + behind, cols, bf16)
         out = [shape(rows, cols, f32), low] if halve else [low]
-        small = [] if self.small is None else [self.small, self.small_got]
+        ins = [*self.keep, *self.got]
         if small:
+            ins.append(self.small)
             out.append(shape(*self.small.shape, f32))
-        ins = [*self.keep, *self.got, *small]
         outs = call(
-            functools.partial(add_kernel, bit, halve, self.segs, len(self.keep), bool(small)), (1,),
+            functools.partial(add_kernel, bit, halve, self.segs, len(self.keep), small), (1,),
             [whole_spec(x.shape) for x in ins], [whole_spec(x.shape) for x in out], out, [],
-            (meta,), *ins,
+            (meta,), *ins, us=us, wait=wait,
         )
         if small:
             self.small = outs[-1]
@@ -1053,8 +1170,6 @@
         if bit is None:
             return True
         self.got = [swap(outs[1] if halve else outs[0], "seq", 1 << bit)]
-        if small:
-            self.small_got = swap(self.small, "seq", 1 << bit)
         if halve:
             self.halved.append(bit)
         return False
@@ -1063,13 +1178,13 @@
         self.bit = self.halved.pop() if self.halved else 0
         self.got = [swap(self.keep[0], "seq", 1 << self.bit)]
 
-    def join(self, meta):
+    def join(self, meta, us=1):
         rows, cols = self.keep[0].shape
         both = shape(2 * rows, cols, bf16)
         spec = whole_spec((rows, cols))
         self.keep = [call(
             functools.partial(join_kernel, self.bit, self.segs), (1,), [spec, spec],
-            whole_spec(both.shape), both, [], (meta,), self.keep[0], self.got[0],
+            whole_spec(both.shape), both, [], (meta,), self.keep[0], self.got[0], us=us,
         )]
         self.segs = [2 * rows for rows in self.segs]
 
@@ -1081,25 +1196,17 @@
         return call(
             functools.partial(result_kernel, self.segs, ways), (1,), [spec, spec],
             [whole_spec(x.shape) for x in out], out, [], (meta,), self.keep[0], self.got[0],
-            out=True, us=2,
+            out=True, us=0.1,
         )
 
 
-def advance(total, meta):
+def advance(total, meta, us=1, wait=()):
     if total.bit is None:
-        if total.add(meta):
+        if total.add(meta, us, wait):
             total.send_back()
     elif total.bit:
-        total.join(meta)
+        total.join(meta, us)
         total.send_back()
-
-
-def sum_over(x, axis):
-    bit = 1
-    while bit < lax.axis_size(axis):
-        x = x + swap(x, axis, bit)
-        bit *= 2
-    return x
 
 
 def shards(
@@ -1128,25 +1235,36 @@
     order.clear()
     tokens = jnp.swapaxes(tokens_in, 1, 2)
     cotangent = jnp.swapaxes(out_grad, 1, 2)
-    token_pieces = head_pieces(tokens)
-    tail = jnp.concatenate([tokens[p, :, count - EDGE :] for p in range(packs)], axis=1)
-    tail = jnp.pad(tail, ((0, 0), (0, LANES - packs * EDGE)))
-    edge_pieces = head_pieces(shift(tail, "seq", 1))
-    extra = jnp.concatenate(
-        [conv_bc.T, bias_bc[:, None], norm_gain.reshape(-1, bc_part).T], axis=1
-    )
-    extra = jnp.pad(extra, ((0, 0), (0, LANES - extra.shape[1])))
-    weight_pieces = head_pieces(jnp.concatenate([proj_bc.T, extra], axis=1))
-    conv_own = jnp.pad(
-        jnp.concatenate([conv_x, bias_x[None]], axis=0).astype(f32), ((0, 7 - width), (0, 0))
-    )
-    conv_bc_own = jnp.pad(
-        jnp.concatenate([conv_bc, bias_bc[None]], axis=0).astype(f32), ((0, 7 - width), (0, 0))
-    )
-    w_dt = jnp.pad(proj_dt, ((0, 0), (0, LANES - heads)))
-    small = jnp.pad(jnp.stack([dt_bias, a_log]).astype(f32), ((0, 6), (0, LANES - heads)))
-    skip = jnp.repeat(d_skip.astype(f32), size)[None]
-    gain_gate = gate_gain.astype(f32)[None]
+    far = swap(tokens, "head", 2)
+    near = swap(tokens, "head", 1)
+    tail = call(
+        tail_kernel, (1,),
+        [pl.BlockSpec((packs, part, LANES), lambda p: (0, 0, count // LANES - 1))],
+        whole_spec((part, LANES)), shape(part, LANES, bf16), [], (), tokens, us=0.05,
+    )
+    tail = shift(tail, "seq", 1)
+    ins = [
+        proj_bc.T, conv_bc, bias_bc, norm_gain, proj_dt.T, conv_x, bias_x, dt_bias, a_log, d_skip,
+        gate_gain,
+    ]
+    outs = [
+        shape(bc_part, features + LANES, bf16), shape(features, bc_part, bf16),
+        shape(features, LANES, bf16), shape(LANES, features, bf16), shape(8, inner, f32),
+        shape(8, bc_part, f32), shape(8, LANES, f32), shape(1, inner, f32), shape(1, inner, f32),
+        shape(part, 1, f32),
+    ]
+    (
+        shared, w_bc, w_dt, w_dt_rows, conv_own, conv_bc_own, small, skip, gain_gate, norm_gain_own,
+    ) = call(
+        functools.partial(prepare_kernel, dims), (1,), [whole_spec(x.shape) for x in ins],
+        [whole_spec(x.shape) for x in outs], outs, [], (), *ins, wait=(tail,),
+        us=0.05,
+    )
+    edge_pieces = head_pieces(tail)
+    weight_pieces = head_pieces(shared)
+    behind = (far, edge_pieces[2], weight_pieces[2])
+    diagonal = swap(lax.optimization_barrier(behind)[0], "head", 1)
+    token_pieces = tokens, near, far, diagonal
 
     lane_spec = pack_spec((count, LANES))
     chan_spec = pack_spec((count, inner))
@@ -1189,14 +1307,14 @@
             pltpu.VMEM((features, 1), f32),
         ],
         pre,
-        *token_pieces, *edge_pieces, *weight_pieces, proj_x, w_dt.T, conv_own, small,
+        *token_pieces, *edge_pieces, *weight_pieces, proj_x, w_dt_rows, conv_own, small,
         us=15,
     )
 
-    cots = head_pieces(lax.optimization_barrier((cotangent, steps))[0])
     kept = {}
-
-    def inner_work():
+    order.hold(xbc, steps, normed)
+
+    def inner_work(_):
         kept["inner"] = call(
             functools.partial(inner_kernel, dims),
             grid,
@@ -1208,8 +1326,14 @@
             xbc, steps,
             us=6,
         )
-
-    def cot_work():
+        own = lax.optimization_barrier((cotangent, kept["inner"]))[0]
+        kept["cots"] = own, swap(own, "head", 2)
+        order.hold(kept["inner"])
+
+    def cot_work(newest):
+        own, far = kept["cots"]
+        near = swap(own, "head", 1)
+        cots = own, near, far, swap(lax.optimization_barrier((far, newest))[0], "head", 1)
         kept["cot"], kept["gg"] = call(
             functools.partial(cot_kernel, dims),
             grid,
@@ -1222,7 +1346,7 @@
             us=5.5,
         )
 
-    def gate_slope_work():
+    def gate_slope_work(_):
         kept["slope"] = call(
             functools.partial(gate_slope_kernel, dims),
             grid,
@@ -1238,11 +1362,11 @@
         )
 
     state_keep, state_recv = scan_states(
-        keep, send, meta, packs, heads, size, 0, (inner_work, cot_work, gate_slope_work)
+        keep, send, meta, packs, heads, size, 0, (inner_work, gate_slope_work, cot_work)
     )
     inner_out, cot, gg = kept["inner"], kept["cot"], kept["gg"]
     gate, slope_x, slope_bc = kept["slope"]
-    slope_next = shift(slope_bc[:, :EDGE], "seq", -1)
+    order.drop(inner_out)
 
     y, stats = call(
         functools.partial(gate_kernel, dims),
@@ -1257,21 +1381,21 @@
         xbc, steps, inner_out, state_keep, state_recv, gate, gg, gain_gate, skip,
         us=6.6,
     )
-    stats_all = lax.all_gather(stats, "head")
+    stats = head_pieces(stats)
 
     gy, gated, ggate, gkeep, gsend, gate_small = call(
         functools.partial(grad_kernel, dims, total_inner),
         grid,
         [
-            pl.BlockSpec((4, 1, 2, count), lambda p, *_: (0, p, 0, 0)),
-            xbc_spec, lane_spec, chan_spec, chan_spec, chan_spec, vec, vec,
+            *[pack_spec((2, count))] * 4, xbc_spec, lane_spec, chan_spec, chan_spec, chan_spec, vec,
+            vec,
         ],
         [chan_spec] * 3 + pay_specs + [whole_spec((8, inner))],
         [shape(packs, count, inner, f32)] + [shape(packs, count, inner, bf16)] * 2
         + [pay, pay, shape(8, inner, f32)],
         [],
         pre,
-        stats_all, xbc, steps, y, gate, gg, gain_gate, skip,
+        *stats, xbc, steps, y, gate, gg, gain_gate, skip,
         us=8.3,
     )
 
@@ -1281,10 +1405,11 @@
     half_specs = [whole_spec((rows_half, inner))] * 2
     half_shapes = [shape(rows_half, inner, f32), shape(rows_half, inner, bf16)]
     half_sums = pltpu.VMEM((2, rows_half, inner), f32)
+    row8, row8_shape = whole_spec((8, features)), shape(8, features, f32)
 
     early_sum, late_sum = SeqSum(), SeqSum()
 
-    def out_work():
+    def out_work(_):
         *kept["out"], keep, give = call(
             functools.partial(out_kernel, dims),
             grid,
@@ -1298,21 +1423,21 @@
         )
         early_sum.put(keep, give)
 
-    def z_work():
-        keep, give = call(
+    def z_work(_):
+        keep, give, kept["gain"] = call(
             functools.partial(z_kernel, dims),
             grid,
-            [model_spec, chan_spec],
-            half_specs,
-            half_shapes,
+            [model_spec, chan_spec, square],
+            half_specs + [row8],
+            half_shapes + [row8_shape],
             [half_sums],
             pre,
-            normed, ggate,
+            normed, ggate, proj_z,
             us=5.3,
         )
         early_sum.put(keep, give)
 
-    def diag_work():
+    def diag_work(_):
         kept["diag"] = call(
             functools.partial(diag_kernel, dims),
             grid,
@@ -1328,194 +1453,208 @@
             us=12,
         )
 
+    def early_work(_):
+        early_sum.add(meta)
+        own, far, send = kept["out"]
+        own, far = call(
+            out_gather_kernel, grid, [piece_spec, piece_spec, send_spec], [piece_spec, piece_spec],
+            [piece_shape, shape(packs, part, count, bf16)], [], (), own, far, swap(send, "head", 1),
+        )
+        kept["out"] = own, swap(far, "head", 2)
+
     gstate_keep, gstate_recv = scan_states(
-        gkeep, gsend, meta, packs, heads, size, 1, (out_work, z_work, diag_work, lambda: early_sum.add(meta)),
+        gkeep, gsend, meta, packs, heads, size, 1, (out_work, z_work, diag_work, early_work),
         lambda: early_sum.got,
     )
-    out_own, out_far, out_send = kept["out"]
+    out_own, out_far = kept["out"]
     dx, dbc, sums = kept["diag"]
 
-    def to_far(far, near):
-        return swap((far + near[1].astype(f32)).astype(bf16), "head", 2)
-
-    near = swap(out_send, "head", 1)
-    block_out = tokens.astype(f32) + out_own + near[0].astype(f32) + to_far(out_far, near).astype(f32)
-    block_out = jnp.swapaxes(block_out.astype(bf16), 1, 2)
-
-    share_own, share_near = call(
+    edge_tile = (EDGE, inner)
+    share_own, share_near, grad_x, state_sums, edge_x = call(
         functools.partial(share_kernel, dims),
         grid,
-        [xbc_spec, lane_spec, pack_spec((count, bc)), state_spec, state_spec],
-        [lane_spec, lane_spec],
-        [shape(packs, count, LANES, f32)] * 2,
-        [],
+        [xbc_spec, lane_spec, pack_spec((count, bc)), state_spec, state_spec, chan_spec, chan_spec,
+         chan_spec, whole_spec((8, inner)), vec],
+        [lane_spec, lane_spec, chan_spec, lane_spec, pack_spec(edge_tile)],
+        [shape(packs, count, LANES, f32)] * 2
+        + [shape(packs, count, inner, f32), shape(packs, count, LANES, f32),
+           shape(packs, *edge_tile, bf16)],
+        [pltpu.VMEM((2 * EDGE, inner), f32)],
         pre,
-        xbc, steps, dbc, gstate_keep, gstate_recv,
+        xbc, steps, dbc, gstate_keep, gstate_recv, gy, dx, slope_x, conv_own, skip,
         us=6.4,
     )
     share_near = swap(share_near, "head", 1)
     advance(early_sum, meta)
     two = shape(half, count, LANES, f32)
-    rows_out = shape(packs, EDGE, LANES, f32)
-    bc_keep, bc_send, bc_edge = call(
+    bc_keep, bc_send = call(
         functools.partial(middle_kernel, (packs, bc_part)),
         (1,),
         [whole_spec((packs, count, LANES))] * 2,
-        [whole_spec(two.shape)] * 2 + [whole_spec(rows_out.shape)],
-        [two, two, rows_out],
+        [whole_spec(two.shape)] * 2,
+        [two, two],
         [],
         (meta,),
         share_own, share_near,
     )
     bc_recv = swap(bc_send, "head", 2)
-    bc_edge = shift(bc_edge, "seq", -1)
-    bc_edge_recv = swap(bc_edge, "head", 2)
-
-
-    main_x, edge_x, state_sums, keep, give, grad_conv = call(
+
+    main_x, keep, give, grad_conv, gain_x = call(
         functools.partial(xback_kernel, dims),
         grid,
         [
-            xbc_spec, lane_spec, chan_spec, chan_spec, state_spec, state_spec, chan_spec,
-            pack_spec((ext, inner)), model_spec, whole_spec((features, LANES)),
-            whole_spec((8, inner)), vec,
+            chan_spec, pack_spec((ext, inner)), model_spec, whole_spec((features, LANES)),
+            pack_spec(edge_tile), whole_spec((8, inner)), square,
         ],
-        [chan_spec, whole_spec((LANES, inner)), lane_spec] + half_specs + [whole_spec((8, inner))],
+        [chan_spec, *half_specs, whole_spec((8, inner)), row8],
+        [shape(packs, count, inner, bf16), *half_shapes, shape(8, inner, f32), row8_shape],
         [
-            shape(packs, count, inner, bf16), shape(LANES, inner, bf16),
-            shape(packs, count, LANES, f32), *half_shapes, shape(8, inner, f32),
-        ],
-        [
-            pltpu.VMEM((ext + EDGE, inner), f32), pltpu.VMEM((ext, inner), f32), half_sums,
+            pltpu.VMEM((count + EDGE, inner), f32), pltpu.VMEM((ext, inner), f32), half_sums,
+            pltpu.VMEM((LANES, inner), bf16),
         ],
         pre,
-        xbc, steps, gy, dx, gstate_keep, gstate_recv, slope_x, raw_x, normed, edge, conv_own, skip,
-        us=12.5,
+        grad_x, raw_x, normed, edge, edge_x, conv_own, proj_x,
+        us=7, wait=(out_far,),
     )
     late_sum.put(keep, give)
-    edge_x = shift(edge_x, "seq", -1)
     advance(early_sum, meta)
 
-    def half_block(shape_of, first):
-        return pl.BlockSpec(
-            (1,) + shape_of, lambda p, *_: (p % half + first,) + (0,) * len(shape_of)
-        )
-
-    edge_rows = (EDGE, LANES)
-    bc_half = (bc_part, inner)
-    gbc, keep, give, grad_conv_bc = call(
-        functools.partial(conv_bc_kernel, dims),
-        grid,
-        [
-            half_block((count, LANES), 0), half_block((count, LANES), 0),
-            half_block(edge_rows, 0), half_block(edge_rows, half),
-            pack_spec((count, bc_part)), pack_spec((EDGE, bc_part)), pack_spec((ext, bc_part)),
-            model_spec, whole_spec((8, bc_part)),
-        ],
-        [pack_spec((count, bc_part)), whole_spec(bc_half), whole_spec(bc_half),
-         whole_spec((8, bc_part))],
-        [
-            shape(packs, count, bc_part, bf16), shape(*bc_half, f32), shape(*bc_half, bf16),
-            shape(8, bc_part, f32),
-        ],
-        [
-            pltpu.VMEM((count + EDGE, bc_part), f32), pltpu.VMEM((ext, bc_part), f32),
-            pltpu.VMEM((features, bc_part), f32),
-        ],
-        pre,
-        bc_keep, bc_recv, bc_edge, bc_edge_recv, slope_bc, slope_next, raw_bc, normed, conv_bc_own,
-        us=6.3,
-    )
-    late_sum.put(keep, give)
-
-    gdt, smalls = call(
+    gdt, gdt_rows, grad_small, gain_dt = call(
         functools.partial(step_kernel, dims),
         grid,
         [
             lane_spec, lane_spec, lane_spec, state_spec, state_spec, state_spec, state_spec,
-            whole_spec((8, LANES)), model_spec, whole_spec((8, inner)), whole_spec((8, bc_part)),
-            whole_spec((8, inner)),
+            whole_spec((8, LANES)), model_spec, whole_spec((features, LANES)),
         ],
-        [lane_spec, whole_spec((EDGE, features))],
-        [shape(packs, count, LANES, bf16), shape(EDGE, features, f32)],
-        [pltpu.VMEM((features, LANES), f32), pltpu.VMEM((8, LANES), f32)],
+        [lane_spec, row8, whole_spec((8, LANES)), row8],
+        [shape(packs, count, LANES, bf16), row8_shape, shape(8, LANES, f32), row8_shape],
+        [pltpu.VMEM((features, LANES), f32)],
         pre,
         steps, sums, state_sums, state_keep, state_recv, gstate_keep, gstate_recv, small, normed,
-        grad_conv, grad_conv_bc, gate_small,
-        us=8,
-    )
-    late_sum.put_small(smalls)
+        w_dt,
+        us=6,
+    )
     advance(early_sum, meta)
+    give_rows = bc_part + 2 * SMALL
+    gbc, edges, keep, give, smalls = call(
+        functools.partial(conv_bc_kernel, dims),
+        grid,
+        [
+            half_spec((count, LANES), half), half_spec((count, LANES), half),
+            pack_spec((count, bc_part)), pack_spec((ext, bc_part)), model_spec,
+            whole_spec((features, LANES)), whole_spec((features, bc_part)),
+            whole_spec((8, bc_part)), pack_spec(edge_tile), whole_spec((8, inner)), row8,
+            whole_spec((8, LANES)), whole_spec((8, inner)), row8, row8, row8,
+            whole_spec((features, 1)),
+        ],
+        [
+            pack_spec((count, bc_part)), pack_spec((EDGE, inner + LANES)),
+            whole_spec((bc_part, inner)), whole_spec((give_rows, inner)),
+            whole_spec((SMALL, inner)),
+        ],
+        [
+            shape(packs, count, bc_part, bf16), shape(packs, EDGE, inner + LANES, bf16),
+            shape(bc_part, inner, f32), shape(give_rows, inner, bf16), shape(SMALL, inner, f32),
+        ],
+        [
+            pltpu.VMEM((ext + EDGE, bc_part), f32), pltpu.VMEM((ext, bc_part), f32),
+            pltpu.VMEM((features, bc_part), f32), pltpu.VMEM((LANES, bc_part), bf16),
+            pltpu.VMEM((8, bc_part), f32),
+        ],
+        pre,
+        bc_keep, bc_recv, slope_bc, raw_bc, normed, edge, w_bc, conv_bc_own, edge_x, grad_conv,
+        gdt_rows, grad_small, gate_small, kept["gain"], gain_x, gain_dt, gain_all,
+        us=5,
+    )
+    edges = shift(edges, "seq", -1)
+    late_sum.put(keep, give, small=smalls)
+    advance(late_sum, meta, wait=early_sum.got)
+    advance(early_sum, meta)
 
     tall = part + EDGE
-    send_spec = pl.BlockSpec((2, 1, tall, count), lambda p, *_: (0, p, 0, 0))
+    tall_send = pl.BlockSpec((2, 1, tall, count), lambda p, *_: (0, p, 0, 0))
     tall_spec = pack_spec((tall, count))
-    extra_spec = pack_spec((8, count))
-    extra_shape = shape(packs, 8, count, f32)
-    gn_own, gn_far, gn_send, extra = call(
+    row_spec, row_shape = pack_spec((1, count)), shape(packs, 1, count, f32)
+    gn_own, gn_far, gn_send, dots = call(
         functools.partial(back_kernel, dims),
         grid,
         [
-            chan_spec, pl.BlockSpec((EDGE, inner), lambda p, *_: (p, 0)), chan_spec, lane_spec,
+            chan_spec, pack_spec((EDGE, inner + LANES)), chan_spec, lane_spec,
             pack_spec((count, bc_part)), model_spec, square, square,
             whole_spec((features, bc_part)), whole_spec((features, LANES)),
-            whole_spec((features, 1)),
         ],
-        [piece_spec, piece_spec, send_spec, extra_spec],
-        [piece_shape, piece_shape, shape(2, packs, tall, count, bf16), extra_shape],
-        [
-            pltpu.VMEM((4, part, count), f32), pltpu.VMEM((features, 1), f32),
-            pltpu.VMEM((4, 8, count), f32),
-        ],
+        [piece_spec, piece_spec, tall_send, row_spec],
+        [piece_shape, piece_shape, shape(2, packs, tall, count, bf16), row_shape],
+        [pltpu.VMEM((4, part, count), f32)],
         pre,
-        main_x, edge_x, ggate, gdt, gbc, normed, proj_z, proj_x, proj_bc, w_dt, gain_all,
-        us=8.3,
+        main_x, edges, ggate, gdt, gbc, normed, proj_z, proj_x, w_bc, w_dt,
+        us=6,
     )
     near = swap(gn_send, "head", 1)
-    advance(late_sum, meta)
-
-    gn_own, gn_far, extra = call(
+    order.drop(xbc, steps, normed)
+    advance(late_sum, meta, 0.1)
+
+    block_out = call(
+        out_final_kernel, grid, [piece_spec] * 3, piece_spec, shape(packs, part, count, bf16), [],
+        (), out_own, out_far, tokens, out=True, us=2,
+    )
+    block_out = jnp.swapaxes(block_out, 1, 2)
+    while early_sum.bit != 0:
+        advance(early_sum, meta)
+    advance(late_sum, meta, 0.1)
+
+    gn_own, gn_far, dots = call(
         gather_kernel,
         grid,
-        [piece_spec, piece_spec, send_spec, extra_spec],
-        [piece_spec, tall_spec, extra_spec],
-        [piece_shape, shape(packs, tall, count, bf16), extra_shape],
+        [piece_spec, piece_spec, tall_send, row_spec],
+        [piece_spec, tall_spec, row_spec],
+        [piece_shape, shape(packs, tall, count, bf16), row_shape],
         [],
         (),
-        gn_own, gn_far, near, extra,
-        us=3.8,
+        gn_own, gn_far, near, dots,
+        us=0.1,
     )
     gn_far = swap(gn_far, "head", 2)
-    advance(early_sum, meta)
+    order.hold(gn_own)
+    grads_out, grads_z = early_sum.result(meta, ("flip", "rows"))
+    advance(late_sum, meta, 0.1)
+    smalls = gains = late_sum.small
+    small_spec = whole_spec(smalls.shape)
+
+    def head_step(x, bit):
+        return call(
+            plus_kernel, (1,), [small_spec, small_spec], small_spec, shape(*x.shape, f32), [], (),
+            x, swap(x, "head", bit), us=1,
+        )
+
+    gains = head_step(gains, 1)
     advance(late_sum, meta)
-    while early_sum.bit != 0:
-        advance(early_sum, meta)
-    advance(late_sum, meta)
-    in_grad, grad_gain = call(
+    gains = head_step(gains, 2)
+    while late_sum.bit != 0:
+        advance(late_sum, meta)
+    in_grad = call(
         functools.partial(final_kernel, (packs, count, features)),
         grid,
-        [
-            piece_spec, tall_spec, extra_spec, piece_spec, pack_spec((1, count)),
-            whole_spec((part, 1)), piece_spec,
-        ],
-        [piece_spec, whole_spec((8, count))],
-        [piece_shape, shape(8, count, f32)],
+        [piece_spec, tall_spec, row_spec, piece_spec, row_spec, whole_spec((part, 1)), piece_spec],
+        piece_spec,
+        piece_shape,
         [],
         (),
-        gn_own, gn_far, extra, tokens, inv, norm_gain.astype(f32)[:, None], cotangent,
-        us=4, out=True,
+        gn_own, gn_far, dots, tokens, inv, norm_gain_own, cotangent,
+        us=2, out=True,
     )
     in_grad = jnp.swapaxes(in_grad, 1, 2)
-    advance(late_sum, meta)
-    grads_out, grads_z = early_sum.result(meta, ("flip", "rows"))
-    while late_sum.bit != 0:
-        advance(late_sum, meta)
+    order.drop(gn_own)
+    vectors = [(inner,), (bc_part,), (heads,), (heads,), (heads,), (inner,), (part,)]
+    tables = [(heads, features), (width, inner), (width, bc_part)]
+    outs = call(
+        functools.partial(unpack_kernel, (heads, features, bc_part, width)), (1,),
+        [small_spec, small_spec], [whole_spec(x) for x in tables + vectors],
+        [shape(*x, f32) for x in tables + vectors], [], (meta,), smalls, gains, out=True,
+    )
+    grad_dt, grad_conv, grad_conv_bc = outs[:3]
+    bias_x_grad, bias_bc_grad, dt_bias_grad, a_log_grad, skip_grad, gate_grad, grad_gain = outs[3:]
     grads_x, grad_bc = late_sum.result(meta, ("rows", "cols"))
-    smalls = late_sum.small
-    grad_gain = sum_over(grad_gain, "seq")[0, :part]
-    grad_conv, grad_conv_bc = smalls[8:13, :inner], smalls[8:13, inner : inner + bc_part]
-    start = 2 * inner - 3 * LANES
-    per_head = [smalls[13, start + k * LANES : start + k * LANES + heads] for k in range(3)]
     return (
         block_out,
         in_grad,
@@ -1523,13 +1662,15 @@
         grads_z,
         grads_x,
         grad_bc.T,
-        smalls[:heads].T,
-        grad_conv[:width],
-        grad_conv_bc[:width],
-        grad_conv[width],
-        grad_conv_bc[width],
-        *per_head,
-        smalls[13, :inner],
+        grad_dt.T,
+        grad_conv,
+        grad_conv_bc,
+        bias_x_grad,
+        bias_bc_grad,
+        dt_bias_grad,
+        a_log_grad,
+        skip_grad,
+        gate_grad,
         grads_out,
     )
 

time: 236 us -> 203 us (0.86)
  starting transfers between devices: 68.9 us -> 46.1 us
  waiting for transfers between devices: 36 us -> 53.7 us
  local copies, waits for them, and re-layouts: 17.9 us -> 2.37 us
  other arithmetic: 6.3 us -> 0.07 us
  blocking collectives: 5.37 us -> 0 us
    ppermute x51 -> x47, starting transfers between devices: 68.9 us -> 46.1 us  [permuted(): y = lax.ppermute(x, axis, route)]
    ppermute x51 -> x47, waiting for transfers between devices: 36 us -> 53.7 us  [permuted(): y = lax.ppermute(x, axis, route)]
    unnamed x108 -> x76, local copies, waits for them, and re-layouts: 10.9 us -> 2.37 us
    all_gather x1 -> x0, blocking collectives: 5.37 us -> none  [shards(): stats_all = lax.all_gather(stats, 'head')]
    slice x4 -> x0, local copies, waits for them, and re-layouts: 2.39 us -> none  [the longest x1 0.62 us: shards(): slope_next = shift(slope_bc[:, :EDGE], 'seq', -1)]
    pallas_call x35 -> x42, Pallas kernels: 99 us -> 98.8 us  [call(): pl.pallas_call(body, grid_spec=pltpu.PrefetchScalarGridSpec(num_scalar_pr...]
  transfers between devices with their start and end apart: 51 -> 47, of which waited for: 19 -> 20; matrix products, arithmetic and copies ran while one was open for 6% -> 0% of each run, Pallas kernels for 35% -> 37%
where the time goes in v4:
time: 203 us; the launch traced here: 202 us
  Pallas kernels  98.8 us (49%)
  waiting for transfers between devices  53.7 us (26%)
  starting transfers between devices  46.1 us (23%)
  local copies, waits for them, and re-layouts  2.37 us (1%)
    pallas_call x42, Pallas kernels, call(): pl.pallas_call(body, grid_spec=pltpu.PrefetchScalarGridSpec(num_scalar_pr...  98.8 us
    ppermute x47, waiting for transfers between devices, permuted(): y = lax.ppermute(x, axis, route)  53.7 us
    ppermute x47, starting transfers between devices, permuted(): y = lax.ppermute(x, axis, route)  46.1 us
  transfers between devices with their start and end apart: 47, of which 20 were waited for; matrix products, arithmetic and copies ran while one was open for 0% of the time, Pallas kernels for 37%

profile of v4, /device:TPU:0, one launch (start us, length us, event | category | flops | bytes accessed | tf_op | source)
XLA Modules:
  0.0 202.3 jit_solution(972948535768534539)
XLA Ops:
  0.7 3.0 %collective-permute-start.1 = (bf16[4,192,256]{2,1,0:T(8,128)(2,1)}, bf16[4,192,256]{2,1,0:T(8,128)(2,1)S(1)}, u32[]{:S(2)}, u32[]{:S(2)}) collective-permute-start(bf16[4,192,256]{2,1,0:T(8,128)(2,1)} %bitcast.10), channel_id=1, source_target_pairs={{0,2},{1,3},{2,0},{3,1},{4,6},{5,7},{6,4},{7,5},{8,10},{9,11},{10,... | collective-permute-start | bytes 1179656 | tf_op jit(solution)/shard_map/ppermute | solution.py:24
  5.0 3.5 %collective-permute-start.2 = (bf16[192,128]{1,0:T(8,128)(2,1)S(1)}, bf16[192,128]{1,0:T(8,128)(2,1)S(1)}, u32[]{:S(2)}, u32[]{:S(2)}) collective-permute-start(bf16[192,128]{1,0:T(8,128)(2,1)S(1)} %get-tuple-element.181), channel_id=1, source_target_pairs={{0,4},{4,8},{8,12},{12,16},{16,20},{20,24},{24,28},{1,5},{5,9},{9,... | collective-permute-start | bytes 147464 | tf_op jit(solution)/shard_map/ppermute | solution.py:24
  12.7 3.9 %collective-permute-done.3.refs_8_ = bf16[192,128]{1,0:T(8,128)(2,1)S(1)} collective-permute-done((bf16[192,128]{1,0:T(8,128)(2,1)S(1)}, bf16[192,128]{1,0:T(8,128)(2,1)S(1)}, u32[]{:S(2)}, u32[]{:S(2)}) %collective-permute-start.3) | collective-permute-done | bytes 49184 | tf_op jit(solution)/shard_map/ppermute | solution.py:24
  19.6 11.8 %shard_map.290 = (bf16[4,768,256]{2,1,0:T(8,128)(2,1)S(1)}, f32[4,1,256]{2,1,0:T(1,128)S(1)}, bf16[768,128]{1,0:T(8,128)(2,1)S(1)}, bf16[4,272,384]{2,1,0:T(8,12...) custom-call(s32[2]{0:T(128)S(1)} %pad_add_fusion.refs_0_, ...), custom_call_target="tpu_custom_call" | custom-call | flops 149999992832 | bytes 45000000 | tf_op jit(solution)/shard_map/pallas_call | solution.py:1066
  33.3 3.5 %shard_map.291 = (f32[4,256,384]{2,1,0:T(8,128)S(1)}, f32[8,128]{1,0:T(8,128)S(1)}) custom-call(s32[2]{0:T(128)S(1)} %pad_add_fusion.refs_0_, s32[4,4]{1,0:T(4,128)S(1)} %copy-done.18, bf16[4,256,640]{2,1,0:T(8,128)(2,1)S(1)} %get-tuple-element.189.refs_2_.refs_4_.refs_9_.refs_8_.refs_6_.refs_11_.refs_13_.refs_20_, ...), custom_call_target="tpu_custom_call" | custom-call | flops 60000002048 | bytes 18000000 | tf_op jit(solution)/shard_map/pallas_call | solution.py:1066
  39.7 2.8 %collective-permute-start.11 = (s16[2,400,128]{2,1,0:T(8,128)(2,1)S(1)}, s16[2,400,128]{2,1,0:T(8,128)(2,1)S(1)}, u32[]{:S(2)}, u32[]{:S(2)}) collective-permute-start(s16[2,400,128]{2,1,0:T(8,128)(2,1)S(1)} %get-tuple-element.197.refs_1_), channel_id=1, source_target_pairs={{0,8},{4,12},{8,0},{12,4},{16,24},{20,28},{24,16},{28,20},{1,9},{5... | collective-permute-start | bytes 614408 | tf_op jit(solution)/shard_map/ppermute | solution.py:24
  42.5 4.1 %shard_map.293 = (bf16[4,256,384]{2,1,0:T(8,128)(2,1)S(1)}, f32[4,256,384]{2,1,0:T(8,128)S(1)}, f32[4,256,64]{2,1,0:T(8,128)S(1)}, f32[8,128]{1,0:T(8,128)S(1)}) custom-call(s32[2]{0:T(128)S(1)} %pad_add_fusion.refs_0_, s32[4,4]{1,0:T(4,128)S(1)} %copy-done.18, ...), custom_call_target="tpu_custom_call" | custom-call | flops 70000001024 | bytes 21000000 | tf_op jit(solution)/shard_map/pallas_call | solution.py:1066
  48.2 2.8 %collective-permute-start.12 = (s16[2,400,128]{2,1,0:T(8,128)(2,1)S(1)}, s16[2,400,128]{2,1,0:T(8,128)(2,1)S(1)}, u32[]{:S(2)}, u32[]{:S(2)}) collective-permute-start(s16[2,400,128]{2,1,0:T(8,128)(2,1)S(1)} %get-tuple-element.203), channel_id=1, source_target_pairs={{0,16},{4,20},{8,24},{12,28},{16,0},{20,4},{24,8},{28,12},{1,17},{... | collective-permute-start | bytes 614408 | tf_op jit(solution)/shard_map/ppermute | solution.py:24
  53.4 7.7 %collective-permute-done.12.refs_3_ = s16[2,400,128]{2,1,0:T(8,128)(2,1)S(1)} collective-permute-done((s16[2,400,128]{2,1,0:T(8,128)(2,1)S(1)}, s16[2,400,128]{2,1,0:T(8,128)(2,1)S(1)}, u32[]{:S(2)}, u32[]{:S(2)}) %collective-permute-start.12) | collective-permute-done | bytes 204832 | tf_op jit(solution)/shard_map/ppermute | solution.py:24
  63.3 5.8 %collective-permute-done.16.refs_6_.refs_7_ = s16[2,400,128]{2,1,0:T(8,128)(2,1)S(1)} collective-permute-done((s16[2,400,128]{2,1,0:T(8,128)(2,1)S(1)}, s16[2,400,128]{2,1,0:T(8,128)(2,1)S(1)}, u32[]{:S(2)}, u32[]{:S(2)}) %collective-permute-start.16) | collective-permute-done | bytes 204832 | tf_op jit(solution)/shard_map/ppermute | solution.py:24
  69.1 3.7 %shard_map.297 = (f32[4,256,384]{2,1,0:T(8,128)S(1)}, f32[4,2,256]{2,1,0:T(2,128)S(1)}, f32[8,128]{1,0:T(8,128)S(1)}) custom-call(s32[2]{0:T(128)S(1)} %pad_add_fusion.refs_0_, s32[4,4]{1,0:T(4,128)S(1)} %copy-done.18, bf16[4,256,640]{2,1,0:T(8,128)(2,1)S(1)} %get-tuple-element.189.refs_2_.refs_4_.refs_9_.refs_8_.refs_6_.refs_11_.refs_13_.refs_20_, ...), custom_call_target="tpu_custom_call" | custom-call | flops 65999998976 | bytes 19800000 | tf_op jit(solution)/shard_map/pallas_call | solution.py:1066
  77.6 5.7 %shard_map.298 = (f32[4,256,384]{2,1,0:T(8,128)S(1)}, bf16[4,256,384]{2,1,0:T(8,128)(2,1)S(1)}, bf16[4,256,384]{2,1,0:T(8,128)(2,1)S(1)}, s16[2,400,128]{2,1,0:T...) custom-call(s32[2]{0:T(128)S(1)} %pad_add_fusion.refs_0_, ...), custom_call_target="tpu_custom_call" | custom-call | flops 83000000512 | bytes 24900000 | tf_op jit(solution)/shard_map/pallas_call | solution.py:1066
  84.4 4.5 %shard_map.299 = (f32[4,192,256]{2,1,0:T(8,128)S(1)}, f32[4,192,256]{2,1,0:T(8,128)S(1)}, bf16[2,4,192,256]{3,2,1,0:T(8,128)(2,1)}, f32[384,384]{1,0:T(8,128)S(1...) custom-call(s32[2]{0:T(128)S(1)} %pad_add_fusion.refs_0_, s32[4,4]{1,0:T(4,128)S(1)} %copy-done.18, ...), custom_call_target="tpu_custom_call" | custom-call | flops 67999997952 | bytes 20400000 | tf_op jit(solution)/shard_map/pallas_call | solution.py:1066
  102.3 10.0 %shard_map.303 = (f32[4,256,384]{2,1,0:T(8,128)S(1)}, f32[4,256,256]{2,1,0:T(8,128)S(1)}, f32[4,256,128]{2,1,0:T(8,128)S(1)}, f32[8,128]{1,0:T(8,128)S(1)}) custom-call(s32[2]{0:T(128)S(1)} %pad_add_fusion.refs_0_, s32[4,4]{1,0:T(4,128)S(1)} %copy-done.18, ...), custom_call_target="tpu_custom_call" | custom-call | flops 120000004096 | bytes 36000000 | tf_op jit(solution)/shard_map/pallas_call | solution.py:1066
  121.3 5.1 %shard_map.307 = (f32[4,256,128]{2,1,0:T(8,128)S(1)}, f32[4,256,128]{2,1,0:T(8,128)S(1)}, f32[4,256,384]{2,1,0:T(8,128)S(1)}, f32[4,256,128]{2,1,0:T(8,128)S(1)}...) custom-call(s32[2]{0:T(128)S(1)} %pad_add_fusion.refs_0_, s32[4,4]{1,0:T(4,128)S(1)} %copy-done.18, ...), custom_call_target="tpu_custom_call" | custom-call | flops 64000000000 | bytes 19200000 | tf_op jit(solution)/shard_map/pallas_call | solution.py:1066
  129.7 5.7 %shard_map.310 = (bf16[4,256,384]{2,1,0:T(8,128)(2,1)S(1)}, f32[384,384]{1,0:T(8,128)S(1)}, bf16[384,384]{1,0:T(8,128)(2,1)S(1)}, f32[8,384]{1,0:T(8,128)S(1)}, ...) custom-call(s32[2]{0:T(128)S(1)} %pad_add_fusion.refs_0_, s32[4,4]{1,0:T(4,128)S(1)} %copy-done.18, ...), custom_call_target="tpu_custom_call" | custom-call | flops 70000001024 | bytes 21000000 | tf_op jit(solution)/shard_map/pallas_call | solution.py:1066
  140.4 5.5 %shard_map.312 = (bf16[4,256,128]{2,1,0:T(8,128)(2,1)S(1)}, f32[8,768]{1,0:T(8,128)S(1)}, f32[8,128]{1,0:T(8,128)S(1)}, f32[8,768]{1,0:T(8,128)S(1)}, f32[8,128]{1,0:T(8,128)S(1)}) custom-call(s32[2]{0:T(128)S(1)} %pad_add_fusion.refs_0_, s32[4,4]{1,0:T(4,128)S(1)} %copy-done.18, ...), custom_call_target="tpu_custom_call" | custom-call | flops 60000002048 | bytes 18000000 | tf_op jit(solution)/shard_map/pallas_call | solution.py:1066
  148.9 4.0 %shard_map.314 = (bf16[4,256,64]{2,1,0:T(8,128)(2,1)S(1)}, bf16[4,16,512]{2,1,0:T(8,128)(2,1)S(1)}, f32[64,384]{1,0:T(8,128)S(1)}, bf16[128,384]{1,0:T(8,128)(2,...) custom-call(s32[2]{0:T(128)S(1)} %pad_add_fusion.refs_0_, s32[4,4]{1,0:T(4,128)S(1)} %copy-done.18, ...), custom_call_target="tpu_custom_call" | custom-call | flops 49999998976 | bytes 15000000 | tf_op jit(solution)/shard_map/pallas_call | solution.py:1066
  155.2 3.0 %collective-permute-done.34.refs_4_ = bf16[128,384]{1,0:T(8,128)(2,1)S(1)} collective-permute-done((bf16[128,384]{1,0:T(8,128)(2,1)S(1)}, bf16[128,384]{1,0:T(8,128)(2,1)S(1)}, u32[]{:S(2)}, u32[]{:S(2)}) %collective-permute-start.34) | collective-permute-done | bytes 98336 | tf_op jit(solution)/shard_map/ppermute | solution.py:24
  160.7 4.6 %shard_map.317 = (f32[4,192,256]{2,1,0:T(8,128)S(1)}, f32[4,192,256]{2,1,0:T(8,128)S(1)}, bf16[2,4,208,256]{3,2,1,0:T(8,128)(2,1)S(1)}, f32[4,1,256]{2,1,0:T(1,128)S(1)}, f32[8,128]{1,0:T(8,128)S(1)}) custom-call(s32[2]{0:T(128)S(1)} %pad_add_fusion.refs_0_, s32[4,4]{1,0:T(4,128)S(1)} %copy-done.18, bf16[4,256,384]{2,1,0:T(8,128)(2,1)S(1)} %get-tuple-element.293.refs_2_, ...), custom_call_target="tpu_custom_call" | custom-call | flops 60000002048 | bytes 18000000 | tf_op jit(solution)/shard_map/pallas_call | solution.py:1066
  169.0 6.9 %collective-permute-done.39.refs_2_ = bf16[176,384]{1,0:T(8,128)(2,1)S(1)} collective-permute-done((bf16[176,384]{1,0:T(8,128)(2,1)S(1)}, bf16[176,384]{1,0:T(8,128)(2,1)S(1)}, u32[]{:S(2)}, u32[]{:S(2)}) %collective-permute-start.39) | collective-permute-done | bytes 135200 | tf_op jit(solution)/shard_map/ppermute | solution.py:24
  180.5 3.1 %collective-permute-done.42.refs_2_ = bf16[112,384]{1,0:T(8,128)(2,1)S(1)} collective-permute-done((bf16[112,384]{1,0:T(8,128)(2,1)S(1)}, bf16[112,384]{1,0:T(8,128)(2,1)S(1)}, u32[]{:S(2)}, u32[]{:S(2)}) %collective-permute-start.42) | collective-permute-done | bytes 86048 | tf_op jit(solution)/shard_map/ppermute | solution.py:24
  185.5 5.2 %collective-permute-done.45.refs_2_ = bf16[224,384]{1,0:T(8,128)(2,1)S(1)} collective-permute-done((bf16[224,384]{1,0:T(8,128)(2,1)S(1)}, bf16[224,384]{1,0:T(8,128)(2,1)S(1)}, u32[]{:S(2)}, u32[]{:S(2)}) %collective-permute-start.45) | collective-permute-done | bytes 172064 | tf_op jit(solution)/shard_map/ppermute | solution.py:24
  196.2 4.3 %collective-permute-done.46.refs_2_ = bf16[448,384]{1,0:T(8,128)(2,1)S(1)} collective-permute-done((bf16[448,384]{1,0:T(8,128)(2,1)S(1)}, bf16[448,384]{1,0:T(8,128)(2,1)S(1)}, u32[]{:S(2)}, u32[]{:S(2)}) %collective-permute-start.46) | collective-permute-done | bytes 344096 | tf_op jit(solution)/shard_map/ppermute | solution.py:24
  (189 shorter events, 80.5 us)
Async XLA Ops:
  0.7 15.9 %collective-permute-start.1 = (bf16[4,192,256]{2,1,0:T(8,128)(2,1)}, bf16[4,192,256]{2,1,0:T(8,128)(2,1)S(1)}, u32[]{:S(2)}, u32[]{:S(2)}) collective-permute-start(bf16[4,192,256]{2,1,0:T(8,128)(2,1)} %bitcast.10), channel_id=1, source_target_pairs={{0,2},{1,3},{2,0},{3,1},{4,6},{5,7},{6,4},{7,5},{8,10},{9,11},{10,... | collective-permute-start | bytes 1179656 | tf_op jit(solution)/shard_map/ppermute | solution.py:24
  36.9 11.2 %collective-permute-start.14 = (bf16[4,192,256]{2,1,0:T(8,128)(2,1)S(1)}, bf16[4,192,256]{2,1,0:T(8,128)(2,1)S(1)}, u32[]{:S(2)}, u32[]{:S(2)}) collective-permute-start(bf16[4,192,256]{2,1,0:T(8,128)(2,1)S(1)} %bitcast.16), channel_id=1, source_target_pairs={{0,2},{1,3},{2,0},{3,1},{4,6},{5,7},{6,4},{7,5},{8,10},{9,11},{10,... | collective-permute-start | bytes 1179656 | tf_op jit(solution)/shard_map/ppermute | solution.py:24
  38.4 12.6 %collective-permute-start.13 = (bf16[4,192,256]{2,1,0:T(8,128)(2,1)S(1)}, bf16[4,192,256]{2,1,0:T(8,128)(2,1)S(1)}, u32[]{:S(2)}, u32[]{:S(2)}) collective-permute-start(bf16[4,192,256]{2,1,0:T(8,128)(2,1)S(1)} %bitcast.17), channel_id=1, source_target_pairs={{0,1},{1,0},{2,3},{3,2},{4,5},{5,4},{6,7},{7,6},{8,9},{9,8},{10,11... | collective-permute-start | bytes 1179656 | tf_op jit(solution)/shard_map/ppermute | solution.py:24
  39.7 7.4 %collective-permute-start.11 = (s16[2,400,128]{2,1,0:T(8,128)(2,1)S(1)}, s16[2,400,128]{2,1,0:T(8,128)(2,1)S(1)}, u32[]{:S(2)}, u32[]{:S(2)}) collective-permute-start(s16[2,400,128]{2,1,0:T(8,128)(2,1)S(1)} %get-tuple-element.197.refs_1_), channel_id=1, source_target_pairs={{0,8},{4,12},{8,0},{12,4},{16,24},{20,28},{24,16},{28,20},{1,9},{5... | collective-permute-start | bytes 614408 | tf_op jit(solution)/shard_map/ppermute | solution.py:24
  48.2 12.9 %collective-permute-start.12 = (s16[2,400,128]{2,1,0:T(8,128)(2,1)S(1)}, s16[2,400,128]{2,1,0:T(8,128)(2,1)S(1)}, u32[]{:S(2)}, u32[]{:S(2)}) collective-permute-start(s16[2,400,128]{2,1,0:T(8,128)(2,1)S(1)} %get-tuple-element.203), channel_id=1, source_target_pairs={{0,16},{4,20},{8,24},{12,28},{16,0},{20,4},{24,8},{28,12},{1,17},{... | collective-permute-start | bytes 614408 | tf_op jit(solution)/shard_map/ppermute | solution.py:24
  89.0 23.3 %collective-permute-start.22 = (bf16[384,384]{1,0:T(8,128)(2,1)}, bf16[384,384]{1,0:T(8,128)(2,1)}, u32[]{:S(2)}, u32[]{:S(2)}) collective-permute-start(bf16[384,384]{1,0:T(8,128)(2,1)} %get-tuple-element.232), channel_id=1, source_target_pairs={{0,4},{4,0},{8,12},{12,8},{16,20},{20,16},{24,28},{28,24},{1,5},{5... | collective-permute-start | bytes 884744 | tf_op jit(solution)/shard_map/ppermute | solution.py:24
  90.0 28.0 %collective-permute-start.20 = (bf16[2,4,192,256]{3,2,1,0:T(8,128)(2,1)}, bf16[2,4,192,256]{3,2,1,0:T(8,128)(2,1)}, u32[]{:S(2)}, u32[]{:S(2)}) collective-permute-start(bf16[2,4,192,256]{3,2,1,0:T(8,128)(2,1)} %get-tuple-element.224), channel_id=1, source_target_pairs={{0,1},{1,0},{2,3},{3,2},{4,5},{5,4},{6,7},{7,6},{8,9},{9,8},{10,11... | collective-permute-start | bytes 2359304 | tf_op jit(solution)/shard_map/ppermute | solution.py:24
  95.4 16.9 %collective-permute-start.23 = (bf16[384,384]{1,0:T(8,128)(2,1)S(1)}, bf16[384,384]{1,0:T(8,128)(2,1)S(1)}, u32[]{:S(2)}, u32[]{:S(2)}) collective-permute-start(bf16[384,384]{1,0:T(8,128)(2,1)S(1)} %get-tuple-element.233), channel_id=1, source_target_pairs={{0,4},{4,0},{8,12},{12,8},{16,20},{20,16},{24,28},{28,24},{1,5},{5... | collective-permute-start | bytes 884744 | tf_op jit(solution)/shard_map/ppermute | solution.py:24
  99.6 12.7 %collective-permute-start.25 = (s16[2,400,128]{2,1,0:T(8,128)(2,1)S(1)}, s16[2,400,128]{2,1,0:T(8,128)(2,1)S(1)}, u32[]{:S(2)}, u32[]{:S(2)}) collective-permute-start(s16[2,400,128]{2,1,0:T(8,128)(2,1)S(1)} %get-tuple-element.236), channel_id=1, source_target_pairs={{0,16},{4,20},{8,24},{12,28},{16,0},{20,4},{24,8},{28,12},{1,17},{... | collective-permute-start | bytes 614408 | tf_op jit(solution)/shard_map/ppermute | solution.py:24
  113.5 7.8 %collective-permute-start.27 = (s16[2,400,128]{2,1,0:T(8,128)(2,1)S(1)}, s16[2,400,128]{2,1,0:T(8,128)(2,1)S(1)}, u32[]{:S(2)}, u32[]{:S(2)}) collective-permute-start(s16[2,400,128]{2,1,0:T(8,128)(2,1)S(1)} %get-tuple-element.247), channel_id=1, source_target_pairs={{0,4},{4,0},{8,12},{12,8},{16,20},{20,16},{24,28},{28,24},{1,5},{5... | collective-permute-start | bytes 614408 | tf_op jit(solution)/shard_map/ppermute | solution.py:24
  116.2 10.3 %collective-permute-start.29 = (bf16[384,384]{1,0:T(8,128)(2,1)S(1)}, bf16[384,384]{1,0:T(8,128)(2,1)S(1)}, u32[]{:S(2)}, u32[]{:S(2)}) collective-permute-start(bf16[384,384]{1,0:T(8,128)(2,1)S(1)} %get-tuple-element.257), channel_id=1, source_target_pairs={{0,8},{4,12},{8,0},{12,4},{16,24},{20,28},{24,16},{28,20},{1,9},{5... | collective-permute-start | bytes 884744 | tf_op jit(solution)/shard_map/ppermute | solution.py:24
  120.1 9.4 %collective-permute-start.26 = (bf16[4,192,256]{2,1,0:T(8,128)(2,1)S(1)}, bf16[4,192,256]{2,1,0:T(8,128)(2,1)S(1)}, u32[]{:S(2)}, u32[]{:S(2)}) collective-permute-start(bf16[4,192,256]{2,1,0:T(8,128)(2,1)S(1)} %get-tuple-element.244), channel_id=1, source_target_pairs={{0,2},{1,3},{2,0},{3,1},{4,6},{5,7},{6,4},{7,5},{8,10},{9,11},{10,... | collective-permute-start | bytes 1179656 | tf_op jit(solution)/shard_map/ppermute | solution.py:24
  127.1 10.1 %collective-permute-start.31 = (bf16[192,384]{1,0:T(8,128)(2,1)S(1)}, bf16[192,384]{1,0:T(8,128)(2,1)S(1)}, u32[]{:S(2)}, u32[]{:S(2)}) collective-permute-start(bf16[192,384]{1,0:T(8,128)(2,1)S(1)} %get-tuple-element.271), channel_id=1, source_target_pairs={{0,16},{4,20},{8,24},{12,28},{16,0},{20,4},{24,8},{28,12},{1,17},{... | collective-permute-start | bytes 442376 | tf_op jit(solution)/shard_map/ppermute | solution.py:24
  137.8 9.1 %collective-permute-start.32 = (bf16[192,384]{1,0:T(8,128)(2,1)S(1)}, bf16[192,384]{1,0:T(8,128)(2,1)S(1)}, u32[]{:S(2)}, u32[]{:S(2)}) collective-permute-start(bf16[192,384]{1,0:T(8,128)(2,1)S(1)} %get-tuple-element.281.refs_1_), channel_id=1, source_target_pairs={{0,16},{4,20},{8,24},{12,28},{16,0},{20,4},{24,8},{28,12},{1,17},{... | collective-permute-start | bytes 442376 | tf_op jit(solution)/shard_map/ppermute | solution.py:24
  138.4 10.5 %collective-permute-start.30 = (f32[2,256,128]{2,1,0:T(8,128)S(1)}, f32[2,256,128]{2,1,0:T(8,128)S(1)}, u32[]{:S(2)}, u32[]{:S(2)}) collective-permute-start(f32[2,256,128]{2,1,0:T(8,128)S(1)} %get-tuple-element.263), channel_id=1, source_target_pairs={{0,2},{1,3},{2,0},{3,1},{4,6},{5,7},{6,4},{7,5},{8,10},{9,11},{10,... | collective-permute-start | bytes 786440 | tf_op jit(solution)/shard_map/ppermute | solution.py:24
  139.5 15.6 %collective-permute-start.33 = (bf16[384,384]{1,0:T(8,128)(2,1)S(1)}, bf16[384,384]{1,0:T(8,128)(2,1)S(1)}, u32[]{:S(2)}, u32[]{:S(2)}) collective-permute-start(bf16[384,384]{1,0:T(8,128)(2,1)S(1)} %get-tuple-element.285), channel_id=1, source_target_pairs={{0,4},{4,0},{8,12},{12,8},{16,20},{20,16},{24,28},{28,24},{1,5},{5... | collective-permute-start | bytes 884744 | tf_op jit(solution)/shard_map/ppermute | solution.py:24
  147.5 10.7 %collective-permute-start.35 = (bf16[384,384]{1,0:T(8,128)(2,1)S(1)}, bf16[384,384]{1,0:T(8,128)(2,1)S(1)}, u32[]{:S(2)}, u32[]{:S(2)}) collective-permute-start(bf16[384,384]{1,0:T(8,128)(2,1)S(1)} %get-tuple-element.289.refs_1_), channel_id=1, source_target_pairs={{0,8},{4,12},{8,0},{12,4},{16,24},{20,28},{24,16},{28,20},{1,9},{5... | collective-permute-start | bytes 884744 | tf_op jit(solution)/shard_map/ppermute | solution.py:24
  159.8 18.5 %collective-permute-start.43 = (bf16[768,384]{1,0:T(8,128)(2,1)S(1)}, bf16[768,384]{1,0:T(8,128)(2,1)S(1)}, u32[]{:S(2)}, u32[]{:S(2)}) collective-permute-start(bf16[768,384]{1,0:T(8,128)(2,1)S(1)} %get-tuple-element.318.refs_1_), channel_id=1, source_target_pairs={{0,4},{4,0},{8,12},{12,8},{16,20},{20,16},{24,28},{28,24},{1,5},{5... | collective-permute-start | bytes 1769480 | tf_op jit(solution)/shard_map/ppermute | solution.py:24
  165.3 11.3 %collective-permute-start.38 = (bf16[2,4,208,256]{3,2,1,0:T(8,128)(2,1)S(1)}, bf16[2,4,208,256]{3,2,1,0:T(8,128)(2,1)S(1)}, u32[]{:S(2)}, u32[]{:S(2)}) collective-permute-start(bf16[2,4,208,256]{3,2,1,0:T(8,128)(2,1)S(1)} %get-tuple-element.304), channel_id=1, source_target_pairs={{0,1},{1,0},{2,3},{3,2},{4,5},{5,4},{6,7},{7,6},{8,9},{9,8},{10,11... | collective-permute-start | bytes 2555912 | tf_op jit(solution)/shard_map/ppermute | solution.py:24
  166.1 9.8 %collective-permute-start.39 = (bf16[176,384]{1,0:T(8,128)(2,1)S(1)}, bf16[176,384]{1,0:T(8,128)(2,1)S(1)}, u32[]{:S(2)}, u32[]{:S(2)}) collective-permute-start(bf16[176,384]{1,0:T(8,128)(2,1)S(1)} %get-tuple-element.307), channel_id=1, source_target_pairs={{0,16},{4,20},{8,24},{12,28},{16,0},{20,4},{24,8},{28,12},{1,17},{... | collective-permute-start | bytes 405512 | tf_op jit(solution)/shard_map/ppermute | solution.py:24
  176.5 7.8 %collective-permute-start.41 = (f32[32,384]{1,0:T(8,128)S(1)}, f32[32,384]{1,0:T(8,128)S(1)}, u32[]{:S(2)}, u32[]{:S(2)}) collective-permute-start(f32[32,384]{1,0:T(8,128)S(1)} %get-tuple-element.316.refs_0_.refs_1_), channel_id=1, source_target_pairs={{0,1},{1,0},{2,3},{3,2},{4,5},{5,4},{6,7},{7,6},{8,9},{9,8},{10,11... | collective-permute-start | bytes 147464 | tf_op jit(solution)/shard_map/ppermute | solution.py:24
  177.0 15.3 %collective-permute-start.40 = (bf16[4,208,256]{2,1,0:T(8,128)(2,1)S(1)}, bf16[4,208,256]{2,1,0:T(8,128)(2,1)S(1)}, u32[]{:S(2)}, u32[]{:S(2)}) collective-permute-start(bf16[4,208,256]{2,1,0:T(8,128)(2,1)S(1)} %get-tuple-element.312), channel_id=1, source_target_pairs={{0,2},{1,3},{2,0},{3,1},{4,6},{5,7},{6,4},{7,5},{8,10},{9,11},{10,... | collective-permute-start | bytes 1277960 | tf_op jit(solution)/shard_map/ppermute | solution.py:24
  184.3 8.0 %collective-permute-start.44 = (f32[32,384]{1,0:T(8,128)S(1)}, f32[32,384]{1,0:T(8,128)S(1)}, u32[]{:S(2)}, u32[]{:S(2)}) collective-permute-start(f32[32,384]{1,0:T(8,128)S(1)} %get-tuple-element.322.refs_0_), channel_id=1, source_target_pairs={{0,2},{1,3},{2,0},{3,1},{4,6},{5,7},{6,4},{7,5},{8,10},{9,11},{10,... | collective-permute-start | bytes 147464 | tf_op jit(solution)/shard_map/ppermute | solution.py:24
  191.3 9.3 %collective-permute-start.46 = (bf16[448,384]{1,0:T(8,128)(2,1)S(1)}, bf16[448,384]{1,0:T(8,128)(2,1)S(1)}, u32[]{:S(2)}, u32[]{:S(2)}) collective-permute-start(bf16[448,384]{1,0:T(8,128)(2,1)S(1)} %get-tuple-element.332.refs_1_), channel_id=1, source_target_pairs={{0,4},{4,0},{8,12},{12,8},{16,20},{20,16},{24,28},{28,24},{1,5},{5... | collective-permute-start | bytes 1032200 | tf_op jit(solution)/shard_map/ppermute | solution.py:24
  (61 other events, 334.3 us)
